TPU v7x, 32 devices: a whole 2x2x4 slice. The times are simulated.
32 devices in a mesh: parts: 2 (over x), dp: 16 (over z, y, core).
Axes of the slice: x: 2, y: 2, z: 4, core: 2. Of those that a mesh axis runs over, the one named last changes fastest.
Arguments:
- cache_keys: bfloat16 [128, 256, 512], P(('parts', 'dp')), parts along dimension 0, may hold values from -6 to 6
- cache_values: bfloat16 [128, 256, 512], P(('parts', 'dp')), parts along dimension 0, may hold values from -6 to 6
- lengths: int32 [128], P(('parts', 'dp')), parts along dimension 0, may hold values from 1 to 255
- unfinished: int32 [128], P(('parts', 'dp')), parts along dimension 0, may hold values from 0 to 1
- send_slot: int32 [32], P('parts'), parts along dimension 0, may hold values from 0 to 3, as said below
- send_to: int32 [32], P('parts'), parts along dimension 0, may hold values from 0 to 15, as said below
- receive_from: int32 [32], P('parts'), parts along dimension 0, may hold values from 0 to 15, as said below
- land_slot: int32 [32], P('parts'), parts along dimension 0, may hold values from 0 to 3, as said below
- land_length: int32 [32], P('parts'), parts along dimension 0, may hold values from 1 to 255, as said below
- queries: bfloat16 [128, 4096], P(('parts', 'dp')), parts along dimension 0
- new_keys: bfloat16 [128, 512], P(('parts', 'dp')), parts along dimension 0
- new_values: bfloat16 [128, 512], P(('parts', 'dp')), parts along dimension 0, may hold values from -6 to 6
- norm_gain: float32 [4096], replicated, may hold values from 0.1 to 1.9
- gate_weight: bfloat16 [4096, 4096], P(None, 'dp'), may hold values from -0.09375 to 0.09375
- up_weight: bfloat16 [4096, 4096], P(None, 'dp'), may hold values from -0.09375 to 0.09375
- down_weight: bfloat16 [4096, 4096], P('dp'), may hold values from -0.125 to 0.125
Outputs:
- decoded: bfloat16 [128, 4096], P(('parts', 'dp')), parts along dimension 0
- keys_after: bfloat16 [128, 256, 512], P(('parts', 'dp')), parts along dimension 0
- values_after: bfloat16 [128, 256, 512], P(('parts', 'dp')), parts along dimension 0
There are 2 independent parts, one for each index of `parts`. A program takes and returns all parts, laid end to end along the dimension named above; an argument that names none is the same for every part. Nothing has to cross between parts.
Inputs may be any that keep to these rules, and one draw needn't show every extreme that they name: No replica both gives and receives; on a giving replica r, send_to[r] is a receiving replica. `receive_from`: on a receiving replica r, the giving replica s with send_to[s] = r. `send_slot`: on a giving replica, the slot of an unfinished sequence. `land_slot`: on a receiving replica, a slot whose sequence is finished. `land_length`: equals lengths at row receive_from[r] * 4 + send_slot[receive_from[r]].
All inputs are finite; a program needn't handle non-finite values.
Results may differ from a plain program's by a relative error of at most 0.0078.
Values may be sent and summed in bfloat16 or wider, within the bound.
No kernel may reach another device: no remote copies, remote signals or barrier semaphores. Data moves between devices by JAX's collectives and lax.ppermute only.
A program may use at most 192 MiB of HBM per device.

v0:
```python
import math

import jax
import jax.numpy as jnp
from jax import lax
from jax.sharding import PartitionSpec as P

HQ = 32
KVH = 4
HD = 128


def per_device(
    cache_keys,
    cache_values,
    lengths,
    unfinished,
    send_slot,
    send_to,
    receive_from,
    land_slot,
    land_length,
    queries,
    new_keys,
    new_values,
    norm_gain,
    gate_weight,
    up_weight,
    down_weight,
):
    my_index = lax.axis_index("dp")
    slot_count, capacity, kv_width = cache_keys.shape
    leaving_slot = send_slot[my_index]
    leaving_keys = lax.dynamic_index_in_dim(cache_keys, leaving_slot, 0, keepdims=False)
    leaving_values = lax.dynamic_index_in_dim(cache_values, leaving_slot, 0, keepdims=False)
    source_index = receive_from[my_index]
    empty_cache = jnp.zeros((capacity, kv_width), jnp.bfloat16)
    shard_rows = (
        lax.all_gather(leaving_keys[None], "dp", axis=0, tiled=True),
        lax.all_gather(leaving_values[None], "dp", axis=0, tiled=True),
    )
    held = shard_rows[0].shape[0]
    inside = (source_index >= 0) & (source_index < held)
    chosen = jnp.clip(source_index, 0, held - 1)
    picked_keys = lax.dynamic_index_in_dim(shard_rows[0], chosen, 0, keepdims=False)
    picked_values = lax.dynamic_index_in_dim(shard_rows[1], chosen, 0, keepdims=False)
    arrived_keys = jnp.where(inside, picked_keys, empty_cache)
    arrived_values = jnp.where(inside, picked_values, empty_cache)
    slot_ids = jnp.arange(slot_count)
    arriving = source_index != my_index
    giving = send_to[my_index] != my_index
    landing = (slot_ids == land_slot[my_index]) & arriving
    vacated = (slot_ids == leaving_slot) & giving
    moved_keys = jnp.where(landing[:, None, None], arrived_keys[None], cache_keys)
    moved_values = jnp.where(landing[:, None, None], arrived_values[None], cache_values)
    length_now = jnp.where(landing, land_length[my_index], lengths)
    alive = jnp.where(landing, 1, unfinished)
    alive = jnp.where(vacated, 0, alive)
    positions = jnp.arange(capacity)
    append = (positions[None, :] == length_now[:, None]) & (alive[:, None] > 0)
    keys_after = jnp.where(append[:, :, None], new_keys[:, None, :], moved_keys)
    values_after = jnp.where(append[:, :, None], new_values[:, None, :], moved_values)
    query_heads = queries.reshape(slot_count, KVH, HQ // KVH, HD)
    key_heads = keys_after.reshape(slot_count, capacity, KVH, HD)
    value_heads = values_after.reshape(slot_count, capacity, KVH, HD)
    scores = jnp.einsum(
        "skgd,sckd->skgc", query_heads, key_heads, preferred_element_type=jnp.float32
    ) * (1.0 / math.sqrt(HD))
    visible = (positions[None, :] <= length_now[:, None])[:, None, None, :]
    scores = jnp.where(visible, scores, jnp.float32(-1e30))
    top = jnp.max(scores, axis=-1, keepdims=True)
    expo = jnp.exp(scores - top)
    probs = (expo / jnp.sum(expo, axis=-1, keepdims=True)).astype(jnp.bfloat16)
    attended = jnp.einsum(
        "skgc,sckd->skgd", probs, value_heads, preferred_element_type=jnp.float32
    ).reshape(slot_count, HQ * HD)
    mean_square = jnp.mean(attended * attended, axis=-1, keepdims=True)
    normed = attended * lax.rsqrt(mean_square + 1e-06) * norm_gain[None, :]
    normed = jnp.where(alive[:, None] > 0, normed, 0.0).astype(jnp.bfloat16)
    gathered = lax.all_gather(normed, "dp", axis=0, tiled=True)
    gate = jnp.dot(gathered, gate_weight, preferred_element_type=jnp.float32)
    up_part = jnp.dot(gathered, up_weight, preferred_element_type=jnp.float32)
    hidden = (jax.nn.silu(gate) * up_part).astype(jnp.bfloat16)
    summed = lax.psum(jnp.dot(hidden, down_weight, preferred_element_type=jnp.float32), "dp")
    own_rows = lax.dynamic_slice_in_dim(summed, my_index * slot_count, slot_count, 0)
    return (own_rows.astype(jnp.bfloat16), keys_after, values_after)


def solution(mesh):
    placed = (
        P(("parts", "dp"), None, None),
        P(("parts", "dp"), None, None),
        P(("parts", "dp")),
        P(("parts", "dp")),
        P("parts"),
        P("parts"),
        P("parts"),
        P("parts"),
        P("parts"),
        P(("parts", "dp"), None),
        P(("parts", "dp"), None),
        P(("parts", "dp"), None),
        P(),
        P(None, "dp"),
        P(None, "dp"),
        P("dp", None),
    )
    return jax.shard_map(
        per_device,
        mesh=mesh,
        in_specs=placed,
        out_specs=(
            P(("parts", "dp"), None),
            P(("parts", "dp"), None, None),
            P(("parts", "dp"), None, None),
        ),
        check_vma=False,
    )
```

profile of v0, /device:TPU:0, one launch (start us, length us, event | category | flops | bytes accessed | tf_op | source)
XLA Modules:
  0.0 228.4 jit_solution(17487018691670327790)
XLA Ops:
  7.2 0.0 copy-start
  7.2 0.0 copy-start.1
  7.2 0.0 copy-start.4
  7.2 0.0 copy-start.5
  7.2 0.0 all-gather.6.cloned.1.call-start
  7.3 1.4 dynamic_slice.32
  10.5 1.7 constant_dynamic-slice_fusion
  12.2 0.0 all-gather.6.cloned.1.call-update
  12.2 0.0 all-gather.4.cloned.1.call-start
  12.3 1.7 constant_dynamic-slice_fusion.1
  14.0 0.0 all-gather.4.cloned.1.call-update
  14.0 1.2 dynamic_slice.35
  17.8 1.2 dynamic_slice.33
  19.7 1.2 dynamic_slice.34
  21.0 1.2 dynamic_slice.36
  22.2 1.9 fusion.26
  24.1 1.2 broadcast_select_fusion
  25.3 0.1 iota_compare_fusion.1
  25.4 40.3 %all-gather.6.cloned.1.call-done = bf16[16,256,512]{2,1,0:T(8,128)(2,1)} async-done(((bf16[1,256,512]{2,1,0:T(8,128)(2,1)}), bf16[16,256,512]{2,1,0:T(8,128)(2,1)}) %all-gather.6.cloned.1.call-update) | async-done | bytes 4194320 | tf_op jit(solution)/shard_map/all_gather | solution.py:40
  65.6 1.0 select_bitcast_fusion
  66.6 50.8 %all-gather.4.cloned.1.call-done = bf16[16,256,512]{2,1,0:T(8,128)(2,1)} async-done(((bf16[1,256,512]{2,1,0:T(8,128)(2,1)}), bf16[16,256,512]{2,1,0:T(8,128)(2,1)}) %all-gather.4.cloned.1.call-update) | async-done | bytes 4194320 | tf_op jit(solution)/shard_map/all_gather | solution.py:39
  117.5 1.0 select_bitcast_fusion.1
  118.4 0.0 copy-done.1
  118.4 0.0 copy-done.4
  118.5 0.0 copy-done.5
  118.5 0.0 copy-start.6
  118.5 2.5 %select_select_fusion.1 = (bf16[4,256,512]{2,1,0:T(8,128)(2,1)S(1)}, bf16[4,256,512]{2,1,0:T(8,128)(2,1)}) fusion(bf16[4,256,512]{2,1,0:T(8,128)(2,1)S(1)} %copy-done.1, pred[4]{0:T(512)(128)(4,1)S(1)} %get-tuple-element.4, pred[4,256]{1,0:T(4,128)(4,1)S(1)} %get-tuple-element.8, bf16[256,512]{1,0:T(8,128)(2,1)S(1)} %select_bitcast_fusion.1, ...), kind=kLoop, calls=%fused_computation.15 | loop fusion | flops 2097152 | bytes 4727812 | tf_op jit(solution)/shard_map/jit(_where)/select_n | solution.py:61
  121.0 0.0 copy-start.2
  121.0 0.0 copy-start.3
  121.0 1.0 copy-done.2
  122.0 0.0 copy-done.6
  122.0 0.4 fusion.4
  122.4 0.2 fusion.28
  122.6 1.6 multiply_reduce_fusion
  124.2 0.0 copy-done.3
  124.2 0.1 fusion.21
  124.3 20.3 %all-gather = bf16[16,4,4096]{2,1,0:T(4,128)(2,1)S(1)} all-gather(bf16[1,4,4096]{2,1,0:T(4,128)(2,1)S(1)} %fusion.21), channel_id=1, replica_groups=mesh['parts'=2,'dp'=16] {'dp'}, dimensions={0}, use_global_device_ids=true | all-gather | bytes 557056 | tf_op jit(solution)/shard_map/all_gather | solution.py:80
  144.7 0.1 reshape.93
  144.8 2.1 fusion.29
  146.8 0.0 copy-done
  146.9 4.0 %fusion.6 = f32[64,4096]{1,0:T(8,128)} fusion(bf16[256,4096]{1,0:T(8,128)(2,1)S(1)} %copy-done, bf16[64,4096]{1,0:T(8,128)(2,1)S(1)} %reshape.93, bf16[4096,256]{1,0:T(8,128)(2,1)} %param.30, f32[64,256]{1,0:T(8,128)S(1)} %fusion.29), kind=kOutput, calls=%fused_computation.8 | convolution fusion | flops 268533760 | bytes 5832704 | tf_op jit(solution)/shard_map/dot_general | solution.py:84
  150.8 70.0 %all-reduce.1 = bf16[64,4096]{1,0:T(8,128)(2,1)S(1)} all-reduce(f32[64,4096]{1,0:T(8,128)} %fusion.6), channel_id=1, replica_groups=mesh['parts'=2,'dp'=16] {'dp'}, use_global_device_ids=true, to_apply=%region_3.4 | all-reduce | flops 262144 | bytes 1572864 | tf_op jit(solution)/shard_map/psum | solution.py:84
  220.9 0.6 dynamic-slice_convert_fusion
  (1 shorter events, 0.0 us)
Async XLA Ops:
  7.2 139.7 %copy-start = (bf16[256,4096]{1,0:T(8,128)(2,1)S(1)}, bf16[256,4096]{1,0:T(8,128)(2,1)}, u32[]{:S(2)}) copy-start(bf16[256,4096]{1,0:T(8,128)(2,1)} %param.31) | copy-start | bytes 6291460
  7.2 111.3 %copy-start.1 = (bf16[4,256,512]{2,1,0:T(8,128)(2,1)S(1)}, bf16[4,256,512]{2,1,0:T(8,128)(2,1)}, u32[]{:S(2)}) copy-start(bf16[4,256,512]{2,1,0:T(8,128)(2,1)} %param.16) | copy-start | bytes 3145732
  7.2 111.3 %copy-start.4 = (bf16[4,512]{1,0:T(4,128)(2,1)S(1)}, bf16[4,512]{1,0:T(4,128)(2,1)}, u32[]{:S(2)}) copy-start(bf16[4,512]{1,0:T(4,128)(2,1)} %param.26) | copy-start | bytes 12292
  7.2 111.3 %copy-start.5 = (bf16[4,512]{1,0:T(4,128)(2,1)S(1)}, bf16[4,512]{1,0:T(4,128)(2,1)}, u32[]{:S(2)}) copy-start(bf16[4,512]{1,0:T(4,128)(2,1)} %param.27) | copy-start | bytes 12292
  7.2 58.4 %all-gather.6.cloned.1.call-start = ((), (), s32[]{:S(2)}) async-start(), calls=%async_computation.1 | async-start | bytes 4456448 | tf_op jit(solution)/shard_map/all_gather | solution.py:40
  12.2 105.2 %all-gather.4.cloned.1.call-start = ((), (), s32[]{:S(2)}) async-start(), calls=%async_computation | async-start | bytes 4456448 | tf_op jit(solution)/shard_map/all_gather | solution.py:39
  118.5 3.5 %copy-start.6 = (bf16[4,4096]{1,0:T(4,128)(2,1)S(1)}, bf16[4,4096]{1,0:T(4,128)(2,1)}, u32[]{:S(2)}) copy-start(bf16[4,4096]{1,0:T(4,128)(2,1)} %param.25) | copy-start | bytes 98308
  121.0 1.0 copy-start.2
  121.0 3.2 %copy-start.3 = (f32[4096]{0:T(1024)S(1)}, f32[4096]{0:T(1024)}, u32[]{:S(2)}) copy-start(f32[4096]{0:T(1024)} %param.28) | copy-start | bytes 49156
Sparse Core Ops, SparseCore 0:
  12.4 53.2 all-gather.5
  68.4 49.0 all-gather.3
where the time goes:
time: 229 us; the launch traced here: 228 us
  waiting for transfers between devices  91.1 us (40%)
  blocking collectives  90.4 us (39%)
  between operations  19.3 us (8%)
  local copies, waits for them, and re-layouts  11.4 us (5%)
  other arithmetic  8.01 us (3%)
  matrix products  8.01 us (3%)
    psum x1, blocking collectives, per_device(): lax.psum(jnp.dot(hidden, down_weight, preferred_element_type=jnp.float32)...  70 us
    all_gather x1, waiting for transfers between devices, per_device(): lax.all_gather(leaving_keys[None], 'dp', axis=0, tiled=True)  50.8 us
    all_gather x1, waiting for transfers between devices, per_device(): lax.all_gather(leaving_values[None], 'dp', axis=0, tiled=True)  40.3 us
    all_gather x1, blocking collectives, per_device(): gathered = lax.all_gather(normed, 'dp', axis=0, tiled=True)  20.3 us
  transfers between devices with their start and end apart: 2, of which 2 were waited for; matrix products, arithmetic and copies ran while one was open for 5% of the time, Pallas kernels for 0%

commit v1 on v0

v1 whole, which is shorter than its diff:
```python
import math

import jax
import jax.numpy as jnp
from jax import lax
from jax.sharding import PartitionSpec as P

HQ = 32
KVH = 4
HD = 128


def exchange(blocks, axis):
    return lax.all_to_all(blocks, axis, 0, 0, tiled=True)


def per_device(
    cache_keys,
    cache_values,
    lengths,
    unfinished,
    send_slot,
    send_to,
    receive_from,
    land_slot,
    land_length,
    queries,
    new_keys,
    new_values,
    norm_gain,
    gate_weight,
    up_weight,
    down_weight,
):
    group = ("chip", "core")
    me = lax.axis_index(group)
    chips, n = lax.axis_size("chip"), lax.axis_size(group)
    my_chip, my_core = lax.axis_index("chip"), lax.axis_index("core")
    slots, capacity, kv_width = cache_keys.shape
    width = queries.shape[1]
    slot_ids = jnp.arange(slots)
    target, source = send_to[me], receive_from[me]
    given_slot, taken_slot = send_slot[me], land_slot[me]
    giving, arriving = target != me, source != me
    landing = (slot_ids == taken_slot) & arriving
    vacated = (slot_ids == given_slot) & giving

    packet = jnp.concatenate(
        [
            lax.dynamic_index_in_dim(queries, taken_slot, 0, keepdims=False),
            lax.dynamic_index_in_dim(new_keys, taken_slot, 0, keepdims=False),
            lax.dynamic_index_in_dim(new_values, taken_slot, 0, keepdims=False),
        ]
    ).reshape(-1, 128)
    packets = exchange(jnp.broadcast_to(packet[None], (n,) + packet.shape), group)
    got = lax.dynamic_index_in_dim(packets, target, 0, keepdims=False).reshape(-1)

    rows = capacity // n
    leaving = jnp.concatenate(
        [
            lax.dynamic_index_in_dim(cache_keys, given_slot, 0, keepdims=False).reshape(n, rows, kv_width),
            lax.dynamic_index_in_dim(cache_values, given_slot, 0, keepdims=False).reshape(n, rows, kv_width),
        ],
        axis=1,
    )
    spread = exchange(leaving, group)

    row_queries = jnp.where(vacated[:, None], got[None, :width], queries)
    row_keys = jnp.where(vacated[:, None], got[None, width : width + kv_width], new_keys)
    row_values = jnp.where(vacated[:, None], got[None, width + kv_width :], new_values)
    row_alive = jnp.where(vacated, 1, jnp.where(landing, 0, unfinished)) > 0
    positions = jnp.arange(capacity)
    append = (positions[None, :] == lengths[:, None]) & row_alive[:, None]
    keys_here = jnp.where(append[:, :, None], row_keys[:, None, :], cache_keys)
    values_here = jnp.where(append[:, :, None], row_values[:, None, :], cache_values)
    query_heads = row_queries.reshape(slots, KVH, HQ // KVH, HD)
    key_heads = keys_here.reshape(slots, capacity, KVH, HD)
    value_heads = values_here.reshape(slots, capacity, KVH, HD)
    scores = jnp.einsum(
        "skgd,sckd->skgc", query_heads, key_heads, preferred_element_type=jnp.float32
    ) * (1.0 / math.sqrt(HD))
    visible = (positions[None, :] <= lengths[:, None])[:, None, None, :]
    scores = jnp.where(visible, scores, jnp.float32(-1e30))
    top = jnp.max(scores, axis=-1, keepdims=True)
    expo = jnp.exp(scores - top)
    probs = (expo / jnp.sum(expo, axis=-1, keepdims=True)).astype(jnp.bfloat16)
    attended = jnp.einsum(
        "skgc,sckd->skgd", probs, value_heads, preferred_element_type=jnp.float32
    ).reshape(slots, HQ * HD)
    mean_square = jnp.mean(attended * attended, axis=-1, keepdims=True)
    normed = attended * lax.rsqrt(mean_square + 1e-06) * norm_gain[None, :]
    normed = jnp.where(row_alive[:, None], normed, 0.0).astype(jnp.bfloat16)

    by_chip = exchange(jnp.broadcast_to(normed[None], (chips,) + normed.shape), "chip")
    other = lax.ppermute(by_chip, "core", [(0, 1), (1, 0)])

    chosen = jnp.take(spread, jnp.clip(receive_from, 0, n - 1), axis=0)
    arrived = exchange(chosen, group)
    arrived_keys = arrived[:, :rows].reshape(capacity, kv_width)
    arrived_values = arrived[:, rows:].reshape(capacity, kv_width)
    length_now = jnp.where(landing, land_length[me], lengths)
    alive = jnp.where(vacated, 0, jnp.where(landing, 1, unfinished)) > 0
    append_now = (positions[None, :] == length_now[:, None]) & alive[:, None]
    keys_after = jnp.where(landing[:, None, None], arrived_keys[None], cache_keys)
    values_after = jnp.where(landing[:, None, None], arrived_values[None], cache_values)
    keys_after = jnp.where(append_now[:, :, None], new_keys[:, None, :], keys_after)
    values_after = jnp.where(append_now[:, :, None], new_values[:, None, :], values_after)

    gathered = jnp.concatenate([by_chip, other], axis=0).reshape(n * slots, width)
    gate = jnp.dot(gathered, gate_weight, preferred_element_type=jnp.float32)
    up_part = jnp.dot(gathered, up_weight, preferred_element_type=jnp.float32)
    hidden = (jax.nn.silu(gate) * up_part).astype(jnp.bfloat16)
    everyone = jnp.arange(n)
    arrives = receive_from != everyone
    gives = send_to != everyone
    row_of = everyone[:, None] * slots + slot_ids[None, :]
    from_row = jnp.where(
        arrives[:, None] & (slot_ids[None, :] == land_slot[:, None]),
        (receive_from * slots + jnp.take(send_slot, jnp.clip(receive_from, 0, n - 1)))[:, None],
        row_of,
    )
    from_row = jnp.where(gives[:, None] & (slot_ids[None, :] == send_slot[:, None]), -1, from_row)
    order = jnp.concatenate([jnp.arange(chips) * 2 + 1 - my_core, jnp.arange(chips) * 2 + my_core])
    held = jnp.concatenate([jnp.arange(chips) * 2 + my_core, jnp.arange(chips) * 2 + 1 - my_core])
    wanted = jnp.take(from_row, order, axis=0).reshape(-1)
    held_row = (held[:, None] * slots + slot_ids[None, :]).reshape(-1)
    pick = (wanted[:, None] == held_row[None, :]).astype(jnp.bfloat16)
    placed_hidden = jnp.dot(pick, hidden, preferred_element_type=jnp.float32).astype(jnp.bfloat16)
    partial = jnp.dot(placed_hidden, down_weight, preferred_element_type=jnp.float32)
    half = chips * slots
    from_other = lax.ppermute(partial[:half].astype(jnp.bfloat16), "core", [(0, 1), (1, 0)])
    chip_sum = (partial[half:] + from_other.astype(jnp.float32)).astype(jnp.bfloat16)
    pieces = exchange(chip_sum.reshape(chips, slots, width), "chip")
    decoded = jnp.sum(pieces.astype(jnp.float32), axis=0).astype(jnp.bfloat16)
    return (decoded, keys_after, values_after)


def solution(mesh):
    parts, n = mesh.shape["parts"], mesh.shape["dp"]
    split = jax.sharding.Mesh(mesh.devices.reshape(parts, n // 2, 2), ("parts", "chip", "core"))
    every, own = ("parts", "chip", "core"), ("chip", "core")
    placed = (
        P(every, None, None),
        P(every, None, None),
        P(every),
        P(every),
        P("parts"),
        P("parts"),
        P("parts"),
        P("parts"),
        P("parts"),
        P(every, None),
        P(every, None),
        P(every, None),
        P(),
        P(None, own),
        P(None, own),
        P(own, None),
    )
    return jax.shard_map(
        per_device,
        mesh=split,
        in_specs=placed,
        out_specs=(P(every, None), P(every, None, None), P(every, None, None)),
        check_vma=False,
    )
```

time: 229 us -> 98.4 us (0.43)
  blocking collectives: 90.4 us -> 12.6 us
  waiting for transfers between devices: 91.1 us -> 36.1 us
  starting transfers between devices: 0.08 us -> 19.2 us
  between operations: 19.3 us -> 8.05 us
  matrix products: 8.01 us -> 4.07 us
  local copies, waits for them, and re-layouts: 11.4 us -> 8.8 us
    all_gather x2 -> x0, waiting for transfers between devices: 91.1 us -> none  [the longest x1 50.8 us: per_device(): lax.all_gather(leaving_keys[None], 'dp', axis=0, tiled=True)]
    psum x1 -> x0, blocking collectives: 70 us -> none  [per_device(): lax.psum(jnp.dot(hidden, down_weight, preferred_element_type=jnp.float32)...]
    all_to_all x0 -> x4, waiting for transfers between devices: none -> 33.5 us  [exchange(): return lax.all_to_all(blocks, axis, 0, 0, tiled=True)]
    all_gather x1 -> x0, blocking collectives: 20.3 us -> none  [per_device(): gathered = lax.all_gather(normed, 'dp', axis=0, tiled=True)]
    all_to_all x0 -> x4, starting transfers between devices: none -> 19 us  [exchange(): return lax.all_to_all(blocks, axis, 0, 0, tiled=True)]
    all_to_all x0 -> x1, blocking collectives: none -> 12.6 us  [exchange(): return lax.all_to_all(blocks, axis, 0, 0, tiled=True)]
    dynamic_slice x7 -> x8, local copies, waits for them, and re-layouts: 9.68 us -> 4.97 us  [the longest x2 2.02 us: per_device(): given_slot, taken_slot = (send_slot[me], land_slot[me])]
    ppermute x0 -> x2, waiting for transfers between devices: none -> 2.6 us  [the longest x1 1.4 us: per_device(): lax.ppermute(partial[:half].astype(jnp.bfloat16), 'core', [(0, 1), (1, 0)])]
  transfers between devices with their start and end apart: 2 -> 6, of which waited for: 2 -> 6; matrix products, arithmetic and copies ran while one was open for 5% -> 8% of each run, Pallas kernels for 0% -> 0%
where the time goes in v1:
time: 98.4 us; the launch traced here: 97.6 us
  waiting for transfers between devices  36.1 us (37%)
  starting transfers between devices  19.2 us (20%)
  blocking collectives  12.6 us (13%)
  local copies, waits for them, and re-layouts  8.8 us (9%)
  other arithmetic  8.77 us (9%)
  between operations  8.05 us (8%)
  matrix products  4.07 us (4%)
    all_to_all x4, waiting for transfers between devices, exchange(): return lax.all_to_all(blocks, axis, 0, 0, tiled=True)  33.5 us
    all_to_all x4, starting transfers between devices, exchange(): return lax.all_to_all(blocks, axis, 0, 0, tiled=True)  19 us
    all_to_all x1, blocking collectives, exchange(): return lax.all_to_all(blocks, axis, 0, 0, tiled=True)  12.6 us
    select_n x1, other arithmetic, per_device(): jnp.where(append_now[:, :, None], new_keys[:, None, :], keys_after)  2.8 us
    dot_general x1, matrix products, per_device(): up_part = jnp.dot(gathered, up_weight, preferred_element_type=jnp.float32)  2.2 us
    dynamic_slice x2, local copies, waits for them, and re-layouts, per_device(): given_slot, taken_slot = (send_slot[me], land_slot[me])  2.02 us
  transfers between devices with their start and end apart: 6, of which 6 were waited for; matrix products, arithmetic and copies ran while one was open for 8% of the time, Pallas kernels for 0%

profile of v1, /device:TPU:0, one launch (start us, length us, event | category | flops | bytes accessed | tf_op | source)
XLA Modules:
  0.0 97.6 jit_solution(1582574268393726365)
XLA Ops:
  0.6 0.0 copy-start
  0.7 0.0 copy-start.1
  0.7 0.0 copy-start.9
  0.7 0.0 copy-start.10
  0.7 0.0 copy-start.12
  0.7 0.0 copy-start.11
  0.8 1.4 %dynamic_slice.37 = s32[1]{0:T(128)} dynamic-slice(s32[16]{0:T(128)} %param.20, s32[]{:T(128)S(6)} %select_n.140), dynamic_slice_sizes={1} | dynamic-slice | bytes 12 | tf_op jit(solution)/shard_map/dynamic_slice | solution.py:43
  4.1 1.1 %constant_dynamic-slice_fusion.1 = (bf16[1,256,512]{2,1,0:T(8,128)(2,1)S(1)}, bf16[1,256,512]{2,1,0:T(8,128)(2,1)S(1)}) fusion(bf16[4,256,512]{2,1,0:T(8,128)(2,1)} %param.17, s32[]{:T(128)S(6)} %select_n.155, bf16[4,256,512]{2,1,0:T(8,128)(2,1)} %param.16), kind=kLoop, calls=%fused_computation.65 | loop fusion | bytes 1048580 | tf_op jit(solution)/shard_map/jit(dynamic_index_in_dim)/dynamic_slice | solution.py:62
  5.1 0.8 pad_maximum_fusion.1
  6.0 7.4 %all-to-all-start.3 = ((bf16[16,32,512]{2,1,0:T(8,128)(2,1)}), bf16[16,32,512]{2,1,0:T(8,128)(2,1)S(1)}, u32[]{:S(2)}, u32[]{:S(2)}) async-start(bf16[16,32,512]{2,1,0:T(8,128)(2,1)} %pad_maximum_fusion.1), calls=%async_computation.3 | async-start | bytes 1048576 | tf_op jit(solution)/shard_map/all_to_all | solution.py:14
  13.4 0.6 dynamic_slice.39
  15.3 0.6 dynamic_slice.38
  17.8 0.6 dynamic_slice.40
  19.1 0.6 dynamic_slice.45
  19.7 0.7 gather_fusion
  21.7 0.1 dynamic-slice_reduce_fusion
  21.7 0.0 copy-done.4
  21.8 1.3 %select_compare_fusion = (pred[4]{0:T(512)(128)(4,1)S(1)}, pred[4]{0:T(512)(128)(4,1)S(1)}, pred[4]{0:T(512)(128)(4,1)S(1)}) fusion(s32[4]{0:T(128)S(1)} %copy-done.8, pred[]{:T(512)S(6)} %ne.15, s32[]{:T(128)} %bitcast.5, pred[]{:T(512)S(6)} %ne.14, s32[]{:T(128)} %bitcast.3), kind=kLoop, calls=%fused_computation.76 | loop fusion | flops 28 | bytes 38 | tf_op jit(solution)/shard_map/gt | solution.py:102
  23.1 0.7 broadcast_select_fusion.4
  23.8 0.1 fusion.28
  23.9 0.1 iota_compare_fusion.4
  23.9 3.9 %all-to-all-done.3 = bf16[16,32,512]{2,1,0:T(8,128)(2,1)S(1)} async-done(((bf16[16,32,512]{2,1,0:T(8,128)(2,1)}), bf16[16,32,512]{2,1,0:T(8,128)(2,1)S(1)}, u32[]{:S(2)}, u32[]{:S(2)}) %all-to-all-start.3) | async-done | bytes 524320 | tf_op jit(solution)/shard_map/all_to_all | solution.py:14
  27.8 0.7 broadcast_in_dim.254
  28.5 4.1 %all-to-all-start = ((bf16[16,40,128]{2,1,0:T(8,128)(2,1)}), bf16[16,40,128]{2,1,0:T(8,128)(2,1)S(1)}, u32[]{:S(2)}, u32[]{:S(2)}) async-start(bf16[16,40,128]{2,1,0:T(8,128)(2,1)} %broadcast_in_dim.254), calls=%async_computation | async-start | bytes 327680 | tf_op jit(solution)/shard_map/all_to_all | solution.py:14
  32.6 0.6 gather_fusion.2
  33.2 0.9 broadcast_select_fusion
  34.1 7.0 %all-to-all-done = bf16[16,40,128]{2,1,0:T(8,128)(2,1)S(1)} async-done(((bf16[16,40,128]{2,1,0:T(8,128)(2,1)}), bf16[16,40,128]{2,1,0:T(8,128)(2,1)S(1)}, u32[]{:S(2)}, u32[]{:S(2)}) %all-to-all-start) | async-done | bytes 163872 | tf_op jit(solution)/shard_map/all_to_all | solution.py:14
  41.1 3.6 %all-to-all-start.4 = ((bf16[16,32,512]{2,1,0:T(8,128)(2,1)}), bf16[16,32,512]{2,1,0:T(8,128)(2,1)S(1)}, u32[]{:S(2)}, u32[]{:S(2)}) async-start(bf16[16,32,512]{2,1,0:T(8,128)(2,1)} %broadcast_select_fusion), calls=%async_computation.4 | async-start | bytes 1048576 | tf_op jit(solution)/shard_map/all_to_all | solution.py:14
  44.7 0.1 fusion.31
  44.7 0.1 select_select_fusion.2
  44.9 0.1 broadcast_select_fusion.3
  45.0 0.1 select_bitcast_fusion.2
  45.0 14.1 %all-to-all-done.4 = bf16[16,32,512]{2,1,0:T(8,128)(2,1)S(1)} async-done(((bf16[16,32,512]{2,1,0:T(8,128)(2,1)}), bf16[16,32,512]{2,1,0:T(8,128)(2,1)S(1)}, u32[]{:S(2)}, u32[]{:S(2)}) %all-to-all-start.4) | async-done | bytes 524320 | tf_op jit(solution)/shard_map/all_to_all | solution.py:14
  59.1 2.8 %select_select_fusion.1 = (bf16[4,256,512]{2,1,0:T(8,128)(2,1)}, bf16[4,32,4,8,128]{4,3,2,1,0:T(8,128)(2,1)S(1)}, bf16[4,32,4,8,128]{4,3,2,1,0:T(8,128)(2,1)S(1)}, bf16[4,256,512]{2,1,0:T(8,128)(2,1)}) fusion(bf16[4,256,512]{2,1,0:T(8,128)(2,1)} %param.16, pred[4]{0:T(512)(128)(4,1)S(1)} %get-tuple-element.4, pred[4,256]{1,0:T(4,128)(4,1)S(1)} %fusion.28, ...), kind=kLoop, calls=%fused_computation.16 | loop fusion | flops 3145728 | bytes 6834180 | tf_op jit(solution)/shard_map/jit(_where)/select_n | solution.py:106
  61.9 0.4 fusion.3
  62.3 0.2 fusion.38
  62.5 0.4 multiply_reduce_fusion
  62.9 0.1 fusion.13
  63.0 0.8 broadcast_in_dim.267
  63.8 3.9 %all-to-all-start.1 = ((bf16[8,4,4096]{2,1,0:T(4,128)(2,1)}), bf16[8,4,4096]{2,1,0:T(4,128)(2,1)S(1)}, u32[]{:S(2)}, u32[]{:S(2)}) async-start(bf16[8,4,4096]{2,1,0:T(4,128)(2,1)} %broadcast_in_dim.267), calls=%async_computation.1 | async-start | bytes 524288 | tf_op jit(solution)/shard_map/all_to_all | solution.py:14
  67.7 0.6 gather_fusion.1
  68.3 0.1 compare_and_fusion.3
  68.4 0.1 broadcast_select_fusion.1
  68.5 8.6 %all-to-all-done.1 = bf16[8,4,4096]{2,1,0:T(4,128)(2,1)S(1)} async-done(((bf16[8,4,4096]{2,1,0:T(4,128)(2,1)}), bf16[8,4,4096]{2,1,0:T(4,128)(2,1)S(1)}, u32[]{:S(2)}, u32[]{:S(2)}) %all-to-all-start.1) | async-done | bytes 262176 | tf_op jit(solution)/shard_map/all_to_all | solution.py:14
  77.1 0.0 collective-permute-start
  77.1 0.1 add_multiply_fusion
  77.2 0.1 select_n.139
  77.3 0.1 iota_add_fusion
  77.3 0.1 add.140
  77.4 1.2 %collective-permute-done = bf16[8,4,4096]{2,1,0:T(4,128)(2,1)S(1)} collective-permute-done((bf16[8,4,4096]{2,1,0:T(4,128)(2,1)S(1)}, bf16[8,4,4096]{2,1,0:T(4,128)(2,1)S(1)}, u32[]{:S(2)}, u32[]{:S(2)}) %collective-permute-start) | collective-permute-done | bytes 262176 | tf_op jit(solution)/shard_map/ppermute | solution.py:95
  78.6 0.3 pad_maximum_fusion
  79.0 0.1 reshape.324
  79.1 0.0 copy-start.2
  79.1 2.2 %fusion.40 = f32[64,256]{1,0:T(8,128)S(1)} fusion(bf16[64,4096]{1,0:T(8,128)(2,1)S(1)} %reshape.324, bf16[4096,256]{1,0:T(8,128)(2,1)} %param.30), kind=kOutput, calls=%fused_computation.93 | convolution fusion | flops 134217728 | bytes 2686976 | tf_op jit(solution)/shard_map/dot_general | solution.py:111
  81.3 0.0 copy-done.2
  81.3 0.5 fusion.39
  81.8 0.0 copy-done
  81.8 0.6 fusion.4
  82.5 0.2 collective-permute-start.1
  82.7 1.4 %collective-permute-done.1 = bf16[32,4096]{1,0:T(8,128)(2,1)S(1)} collective-permute-done((bf16[32,4096]{1,0:T(8,128)(2,1)S(1)}, bf16[32,4096]{1,0:T(8,128)(2,1)S(1)}, u32[]{:S(2)}, u32[]{:S(2)}) %collective-permute-start.1) | collective-permute-done | bytes 262176 | tf_op jit(solution)/shard_map/ppermute | solution.py:131
  84.1 0.1 fusion.10
  84.2 0.1 reshape.325
  84.3 12.6 %all_to_all.25 = bf16[8,4,4096]{2,1,0:T(4,128)(2,1)S(1)} all-to-all(bf16[8,4,4096]{2,1,0:T(4,128)(2,1)S(1)} %reshape.325), channel_id=1, replica_groups=mesh['parts'=2,'chip'=8,'core'=2] {'chip'}, dimensions={0} | all-to-all | bytes 524288 | tf_op jit(solution)/shard_map/all_to_all | solution.py:14
  96.9 0.7 reduce_sum.32
  (33 shorter events, 0.2 us)
Async XLA Ops:
  0.6 81.2 %copy-start = (bf16[256,4096]{1,0:T(8,128)(2,1)S(1)}, bf16[256,4096]{1,0:T(8,128)(2,1)}, u32[]{:S(2)}) copy-start(bf16[256,4096]{1,0:T(8,128)(2,1)} %param.31) | copy-start | bytes 6291460
  0.7 19.0 %copy-start.1 = (s32[16]{0:T(128)S(1)}, s32[16]{0:T(128)}, u32[]{:S(2)}) copy-start(s32[16]{0:T(128)} %param.20) | copy-start | bytes 196
  0.7 12.7 %copy-start.9 = (s32[16]{0:T(128)S(1)}, s32[16]{0:T(128)}, u32[]{:S(2)}) copy-start(s32[16]{0:T(128)} %param.23) | copy-start | bytes 196
  0.7 14.6 %copy-start.10 = (s32[16]{0:T(128)S(1)}, s32[16]{0:T(128)}, u32[]{:S(2)}) copy-start(s32[16]{0:T(128)} %param.21) | copy-start | bytes 196
  0.7 17.1 %copy-start.12 = (s32[16]{0:T(128)S(1)}, s32[16]{0:T(128)}, u32[]{:S(2)}) copy-start(s32[16]{0:T(128)} %param.22) | copy-start | bytes 196
  0.7 18.4 %copy-start.11 = (s32[16]{0:T(128)S(1)}, s32[16]{0:T(128)}, u32[]{:S(2)}) copy-start(s32[16]{0:T(128)} %param.24) | copy-start | bytes 196
  0.7 21.0 %copy-start.3 = (bf16[4,4096]{1,0:T(4,128)(2,1)S(1)}, bf16[4,4096]{1,0:T(4,128)(2,1)}, u32[]{:S(2)}) copy-start(bf16[4,4096]{1,0:T(4,128)(2,1)} %param.25) | copy-start | bytes 98308
  0.7 21.0 %copy-start.5 = (bf16[4,512]{1,0:T(4,128)(2,1)S(1)}, bf16[4,512]{1,0:T(4,128)(2,1)}, u32[]{:S(2)}) copy-start(bf16[4,512]{1,0:T(4,128)(2,1)} %param.27) | copy-start | bytes 12292
  0.7 21.0 %copy-start.4 = (bf16[4,512]{1,0:T(4,128)(2,1)S(1)}, bf16[4,512]{1,0:T(4,128)(2,1)}, u32[]{:S(2)}) copy-start(bf16[4,512]{1,0:T(4,128)(2,1)} %param.26) | copy-start | bytes 12292
  0.7 21.0 %copy-start.8 = (s32[4]{0:T(128)S(1)}, s32[4]{0:T(128)}, u32[]{:S(2)}) copy-start(s32[4]{0:T(128)} %param.19) | copy-start | bytes 52
  0.7 22.4 %copy-start.7 = (s32[4]{0:T(128)S(1)}, s32[4]{0:T(128)}, u32[]{:S(2)}) copy-start(s32[4]{0:T(128)} %param.18) | copy-start | bytes 52
  6.0 21.9 %all-to-all-start.3 = ((bf16[16,32,512]{2,1,0:T(8,128)(2,1)}), bf16[16,32,512]{2,1,0:T(8,128)(2,1)S(1)}, u32[]{:S(2)}, u32[]{:S(2)}) async-start(bf16[16,32,512]{2,1,0:T(8,128)(2,1)} %pad_maximum_fusion.1), calls=%async_computation.3 | async-start | bytes 1048576 | tf_op jit(solution)/shard_map/all_to_all | solution.py:14
  28.5 12.6 %all-to-all-start = ((bf16[16,40,128]{2,1,0:T(8,128)(2,1)}), bf16[16,40,128]{2,1,0:T(8,128)(2,1)S(1)}, u32[]{:S(2)}, u32[]{:S(2)}) async-start(bf16[16,40,128]{2,1,0:T(8,128)(2,1)} %broadcast_in_dim.254), calls=%async_computation | async-start | bytes 327680 | tf_op jit(solution)/shard_map/all_to_all | solution.py:14
  41.1 18.0 %all-to-all-start.4 = ((bf16[16,32,512]{2,1,0:T(8,128)(2,1)}), bf16[16,32,512]{2,1,0:T(8,128)(2,1)S(1)}, u32[]{:S(2)}, u32[]{:S(2)}) async-start(bf16[16,32,512]{2,1,0:T(8,128)(2,1)} %broadcast_select_fusion), calls=%async_computation.4 | async-start | bytes 1048576 | tf_op jit(solution)/shard_map/all_to_all | solution.py:14
  61.9 1.0 %copy-start.6 = (f32[4096]{0:T(1024)S(1)}, f32[4096]{0:T(1024)}, u32[]{:S(2)}) copy-start(f32[4096]{0:T(1024)} %param.28) | copy-start | bytes 49156
  63.8 13.3 %all-to-all-start.1 = ((bf16[8,4,4096]{2,1,0:T(4,128)(2,1)}), bf16[8,4,4096]{2,1,0:T(4,128)(2,1)S(1)}, u32[]{:S(2)}, u32[]{:S(2)}) async-start(bf16[8,4,4096]{2,1,0:T(4,128)(2,1)} %broadcast_in_dim.267), calls=%async_computation.1 | async-start | bytes 524288 | tf_op jit(solution)/shard_map/all_to_all | solution.py:14
  77.1 1.5 %collective-permute-start = (bf16[8,4,4096]{2,1,0:T(4,128)(2,1)S(1)}, bf16[8,4,4096]{2,1,0:T(4,128)(2,1)S(1)}, u32[]{:S(2)}, u32[]{:S(2)}) collective-permute-start(bf16[8,4,4096]{2,1,0:T(4,128)(2,1)S(1)} %all-to-all-done.1), channel_id=1, source_target_pairs={{0,1},{1,0},{2,3},{3,2},{4,5},{5,4},{6,7},{7,6},{8,9},{9,8},{10,11... | collective-permute-start | bytes 786440 | tf_op jit(solution)/shard_map/ppermute | solution.py:95
  79.1 2.2 %copy-start.2 = (bf16[4096,256]{1,0:T(8,128)(2,1)S(1)}, bf16[4096,256]{1,0:T(8,128)(2,1)}, u32[]{:S(2)}) copy-start(bf16[4096,256]{1,0:T(8,128)(2,1)} %param.29) | copy-start | bytes 6291460
  82.5 1.6 %collective-permute-start.1 = (bf16[32,4096]{1,0:T(8,128)(2,1)S(1)}, bf16[32,4096]{1,0:T(8,128)(2,1)S(1)}, u32[]{:S(2)}, u32[]{:S(2)}) collective-permute-start(bf16[32,4096]{1,0:T(8,128)(2,1)S(1)} %slice.46), channel_id=1, source_target_pairs={{0,1},{1,0},{2,3},{3,2},{4,5},{5,4},{6,7},{7,6},{8,9},{9,8},{10,11... | collective-permute-start | bytes 786440 | tf_op jit(solution)/shard_map/ppermute | solution.py:131

commit v2 on v1

--- a/solution.py
+++ b/solution.py
@@ -1,20 +1,302 @@
+import functools
 import math
 
 import jax
 import jax.numpy as jnp
 from jax import lax
+from jax.experimental import pallas as pl
+from jax.experimental.pallas import tpu as pltpu
 from jax.sharding import PartitionSpec as P
 
 HQ = 32
 KVH = 4
 HD = 128
+TILE = 16
+GROUP = ("chip", "core")
+SMEM, VMEM = pltpu.SMEM, pltpu.VMEM
 
 
 def exchange(blocks, axis):
     return lax.all_to_all(blocks, axis, 0, 0, tiled=True)
 
 
+def spec(space):
+    return pl.BlockSpec(memory_space=space)
+
+
+def cost(flops, moved):
+    return pl.CostEstimate(flops=flops, bytes_accessed=moved, transcendentals=0)
+
+
+def pack_kernel(send_slot, land_slot, q, nk, nv, ck, cv, packets, leaving, lines, sems):
+    me = lax.axis_index(GROUP)
+    n, slots = packets.shape[0], q.shape[1]
+    given, taken = send_slot[me], land_slot[me]
+    copies = [
+        pltpu.make_async_copy(ck.at[given], leaving.at[:, pl.ds(0, TILE)], sems.at[0]),
+        pltpu.make_async_copy(cv.at[given], leaving.at[:, pl.ds(TILE, TILE)], sems.at[1]),
+    ]
+    for copy in copies:
+        copy.start()
+    lines[...] = jnp.zeros_like(lines)
+    at = 0
+    for x in (q, nk, nv):
+        heads = x.shape[0]
+        mine = lax.broadcasted_iota(jnp.int32, (heads, slots, HD), 1) == taken
+        lines[at : at + heads] = jnp.sum(jnp.where(mine, x[...].astype(jnp.float32), 0.0), axis=1)
+        at += heads
+    packet = lines[...].astype(jnp.bfloat16)
+    for d in range(n):
+        packets[d] = packet
+    for copy in copies:
+        copy.wait()
+
+
+def attend_kernel(
+    send_slot, send_to, lengths, unfinished, packets, q, nk, nv, gain, ck, cv, out, kbuf, vbuf, q32, att, sems
+):
+    me = lax.axis_index(GROUP)
+    slots, capacity, _ = ck.shape
+    loads = []
+    for j in range(slots):
+        loads.append(
+            (
+                pltpu.make_async_copy(ck.at[j], kbuf.at[j], sems.at[0, j]),
+                pltpu.make_async_copy(cv.at[j], vbuf.at[j], sems.at[1, j]),
+            )
+        )
+        for copy in loads[j]:
+            copy.start()
+    target, given = send_to[me], send_slot[me]
+    packet = packets[target].astype(jnp.float32)
+    q32[...] = q[...].astype(jnp.float32)
+    nk32, nv32 = nk[...].astype(jnp.float32), nv[...].astype(jnp.float32)
+    scale = 1.0 / math.sqrt(HD)
+    per = HQ // KVH
+    for j in range(slots):
+        moved = (target != me) & (given == j)
+        alive = jnp.where(moved, 1, unfinished[j]) > 0
+        length = lengths[j]
+        base = pl.multiple_of((length // TILE) * TILE, TILE)
+        line = jnp.where(alive, length - base, -1)
+        here = lax.broadcasted_iota(jnp.int32, (TILE, HD), 0) == line
+        for copy in loads[j]:
+            copy.wait()
+        for k in range(KVH):
+            columns = slice(k * HD, (k + 1) * HD)
+            for buf, own, at in ((kbuf, nk32, HQ + k), (vbuf, nv32, HQ + KVH + k)):
+                fresh = jnp.where(moved, packet[at : at + 1], own[k, j : j + 1])
+                block = buf[j, pl.ds(base, TILE), columns].astype(jnp.float32)
+                buf[j, pl.ds(base, TILE), columns] = jnp.where(here, fresh, block).astype(jnp.bfloat16)
+        qj = jnp.where(moved, packet[:HQ], q32[:, j, :])
+        scores = jnp.concatenate(
+            [
+                lax.dot_general(
+                    qj[k * per : (k + 1) * per].astype(jnp.bfloat16),
+                    kbuf[j, :, k * HD : (k + 1) * HD],
+                    (((1,), (1,)), ((), ())),
+                    preferred_element_type=jnp.float32,
+                )
+                for k in range(KVH)
+            ],
+            axis=0,
+        )
+        visible = lax.broadcasted_iota(jnp.int32, scores.shape, 1) <= length
+        scores = jnp.where(visible, scores * scale, jnp.float32(-1e30))
+        expo = jnp.exp(scores - jnp.max(scores, axis=1, keepdims=True))
+        probs = expo / jnp.sum(expo, axis=1, keepdims=True)
+        attended = jnp.concatenate(
+            [
+                jnp.dot(
+                    probs[k * per : (k + 1) * per].astype(jnp.bfloat16),
+                    vbuf[j, :, k * HD : (k + 1) * HD],
+                    preferred_element_type=jnp.float32,
+                )
+                for k in range(KVH)
+            ],
+            axis=0,
+        )
+        mean = jnp.sum(attended * attended, keepdims=True) * (1.0 / (HQ * HD))
+        normed = attended * lax.rsqrt(mean + 1e-06) * gain[...]
+        att[:, j, :] = jnp.where(alive, normed, 0.0)
+    for h in range(HQ):
+        head = att[h].astype(jnp.bfloat16)
+        for c in range(out.shape[0]):
+            out[c, :, h * HD : (h + 1) * HD] = head
+
+
+def select_kernel(send_slot, send_to, receive_from, land_slot, spread, _, chosen, pick, sem):
+    n = chosen.shape[0]
+    rows = pick.shape[0]
+    half, slots = rows // 2, rows // n
+    core = lax.axis_index("core")
+
+    def copy(d):
+        return pltpu.make_async_copy(spread.at[receive_from[d]], chosen.at[d], sem.at[d])
+
+    for d in range(n):
+        pl.when(receive_from[d] != d)(lambda d=d: copy(d).start())
+    row = lax.broadcasted_iota(jnp.int32, (rows, HD), 0)
+    wanted = jnp.where(row < half, row + half, row - half)
+    for d in range(n):
+        same = lax.rem(d, 2) == core
+        there = jnp.where(same, half, 0) + (d // 2) * slots
+        source = receive_from[d]
+        held = jnp.where(lax.rem(source, 2) == core, 0, half) + (source // 2) * slots + send_slot[source]
+        landing = jnp.where(source != d, there + land_slot[d], -1)
+        vacated = jnp.where(send_to[d] != d, there + send_slot[d], -1)
+        wanted = jnp.where(row == landing, held, wanted)
+        wanted = jnp.where(row == vacated, -1, wanted)
+    column = lax.broadcasted_iota(jnp.int32, (rows, rows), 1)
+    pick[...] = (column == wanted[:, :1]).astype(jnp.float32).astype(jnp.bfloat16)
+    for d in range(n):
+        pl.when(receive_from[d] != d)(lambda d=d: copy(d).wait())
+
+
+def merge_kernel(
+    send_slot, send_to, receive_from, land_slot, land_length, lengths, unfinished, nk, nv, ck, cv, arrived, _,
+    keys, values, lines, sems
+):
+    me = lax.axis_index(GROUP)
+    slots = ck.shape[0]
+    source, target = receive_from[me], send_to[me]
+    plans = []
+    for j in range(slots):
+        landing = (source != me) & (land_slot[me] == j)
+        vacated = (target != me) & (send_slot[me] == j)
+        length = jnp.where(landing, land_length[me], lengths[j])
+        alive = jnp.where(vacated, 0, jnp.where(landing, 1, unfinished[j])) > 0
+        plans.append((landing, length // TILE, lax.rem(length, TILE), alive))
+
+    def copies(j, landed):
+        block = plans[j][1]
+        made = []
+        for i, (cache, out) in enumerate(((ck, keys), (cv, values))):
+            whole = arrived.at[:, pl.ds(i * TILE, TILE)] if landed else cache.at[j]
+            piece = arrived.at[block, pl.ds(i * TILE, TILE)] if landed else cache.at[j, block]
+            made.append(pltpu.make_async_copy(whole, out.at[j], sems.at[i, j]))
+            made.append(pltpu.make_async_copy(piece, lines.at[i, j], sems.at[2 + i, j]))
+        return made
+
+    def start(j, landed):
+        for copy in copies(j, landed):
+            copy.start()
+
+    for j in range(slots):
+        pl.when(plans[j][0])(functools.partial(start, j, True))
+        pl.when(jnp.logical_not(plans[j][0]))(functools.partial(start, j, False))
+    for j in range(slots):
+        _, block, line, alive = plans[j]
+        for copy in copies(j, False):
+            copy.wait()
+        here = lax.broadcasted_iota(jnp.int32, (TILE, HD), 0) == jnp.where(alive, line, -1)
+        for i, (fresh, out) in enumerate(((nk, keys), (nv, values))):
+            for k in range(KVH):
+                columns = slice(k * HD, (k + 1) * HD)
+                old = lines[i, j, :, columns].astype(jnp.float32)
+                new = fresh[k, j : j + 1].astype(jnp.float32)
+                lines[i, j, :, columns] = jnp.where(here, new, old).astype(jnp.bfloat16)
+            pltpu.make_async_copy(lines.at[i, j], out.at[j, block], sems.at[i, j]).start()
+    for j in range(slots):
+        for i, out in enumerate((keys, values)):
+            pltpu.make_async_copy(lines.at[i, j], out.at[j, plans[j][1]], sems.at[i, j]).wait()
+
+
 def per_device(
+    cache_keys, cache_values, lengths, unfinished, send_slot, send_to, receive_from, land_slot, land_length,
+    queries, new_keys, new_values, norm_gain, gate_weight, up_weight, down_weight
+):
+    chips, n = lax.axis_size("chip"), lax.axis_size(GROUP)
+    slots, capacity, kv_width = cache_keys.shape
+    if capacity != TILE * n:
+        return per_device_small_pieces(
+            cache_keys, cache_values, lengths, unfinished, send_slot, send_to, receive_from, land_slot, land_length,
+            queries, new_keys, new_values, norm_gain, gate_weight, up_weight, down_weight
+        )
+    width = queries.shape[1]
+    bf16 = jnp.bfloat16
+    dma = pltpu.SemaphoreType.DMA
+    pieces = (slots, n, TILE, kv_width)
+
+    def by_head(x):
+        return x.reshape(slots, -1, HD).transpose(1, 0, 2)
+
+    q, nk, nv = by_head(queries), by_head(new_keys), by_head(new_values)
+    lines = HQ + 4 * KVH
+    packets, leaving = pl.pallas_call(
+        pack_kernel,
+        out_shape=(
+            jax.ShapeDtypeStruct((n, lines, HD), bf16),
+            jax.ShapeDtypeStruct((n, 2 * TILE, kv_width), bf16),
+        ),
+        in_specs=[spec(SMEM)] * 2 + [spec(VMEM)] * 3 + [spec(pl.ANY)] * 2,
+        out_specs=(spec(VMEM), spec(pl.ANY)),
+        scratch_shapes=[VMEM((lines, HD), jnp.float32), dma((2,))],
+        cost_estimate=cost(0, 2**20),
+        name="pack",
+    )(send_slot, land_slot, q, nk, nv, cache_keys.reshape(pieces), cache_values.reshape(pieces))
+    packets = exchange(packets, GROUP)
+    spread = exchange(leaving, GROUP)
+    rows = pl.pallas_call(
+        attend_kernel,
+        out_shape=jax.ShapeDtypeStruct((chips, slots, width), bf16),
+        in_specs=[spec(SMEM)] * 4 + [spec(VMEM)] * 5 + [spec(pl.ANY)] * 2,
+        out_specs=spec(VMEM),
+        scratch_shapes=[
+            VMEM(cache_keys.shape, bf16),
+            VMEM(cache_keys.shape, bf16),
+            VMEM((HQ, slots, HD), jnp.float32),
+            VMEM((HQ, slots, HD), jnp.float32),
+            dma((2, slots)),
+        ],
+        compiler_params=pltpu.CompilerParams(vmem_limit_bytes=24 * 2**20),
+        cost_estimate=cost(2**24, 2**21),
+        name="attend",
+    )(
+        send_slot, send_to, lengths, unfinished, packets, q, nk, nv, norm_gain.reshape(HQ, HD), cache_keys, cache_values
+    )
+    by_chip = exchange(rows, "chip")
+    chosen, pick = pl.pallas_call(
+        select_kernel,
+        out_shape=(
+            jax.ShapeDtypeStruct((n, 2 * TILE, kv_width), bf16),
+            jax.ShapeDtypeStruct((n * slots, n * slots), bf16),
+        ),
+        in_specs=[spec(SMEM)] * 4 + [spec(pl.ANY)] * 2,
+        out_specs=(spec(pl.ANY), spec(VMEM)),
+        scratch_shapes=[dma((n,))],
+        cost_estimate=cost(0, 2**20),
+        name="select",
+    )(send_slot, send_to, receive_from, land_slot, spread, rows)
+    arrived = exchange(chosen, GROUP)
+    other = lax.ppermute(by_chip, "core", [(0, 1), (1, 0)])
+    gathered = jnp.concatenate([by_chip, other], axis=0).reshape(n * slots, width)
+    gate = jnp.dot(gathered, gate_weight, preferred_element_type=jnp.float32)
+    up_part = jnp.dot(gathered, up_weight, preferred_element_type=jnp.float32)
+    hidden = (jax.nn.silu(gate) * up_part).astype(bf16)
+    placed_hidden = jnp.dot(pick, hidden, preferred_element_type=jnp.float32).astype(bf16)
+    partial = jnp.dot(placed_hidden, down_weight, preferred_element_type=jnp.float32)
+    half = chips * slots
+    from_other = lax.ppermute(partial[:half].astype(bf16), "core", [(0, 1), (1, 0)])
+    chip_sum = (partial[half:] + from_other.astype(jnp.float32)).astype(bf16).reshape(chips, slots, width)
+    summed = exchange(chip_sum, "chip")
+    decoded = jnp.sum(summed.astype(jnp.float32), axis=0).astype(bf16)
+    keys_after, values_after = pl.pallas_call(
+        merge_kernel,
+        out_shape=(jax.ShapeDtypeStruct(pieces, bf16), jax.ShapeDtypeStruct(pieces, bf16)),
+        in_specs=[spec(SMEM)] * 7 + [spec(VMEM)] * 2 + [spec(pl.ANY)] * 4,
+        out_specs=(spec(pl.ANY), spec(pl.ANY)),
+        scratch_shapes=[VMEM((2, slots, TILE, kv_width), bf16), dma((4, slots))],
+        cost_estimate=cost(0, 2**23),
+        name="merge",
+    )(
+        send_slot, send_to, receive_from, land_slot, land_length, lengths, unfinished, nk, nv,
+        cache_keys.reshape(pieces), cache_values.reshape(pieces), arrived, chip_sum
+    )
+    return (decoded, keys_after.reshape(cache_keys.shape), values_after.reshape(cache_keys.shape))
+
+
+def per_device_small_pieces(
     cache_keys,
     cache_values,
     lengths,
@@ -32,7 +314,7 @@
     up_weight,
     down_weight,
 ):
-    group = ("chip", "core")
+    group = GROUP
     me = lax.axis_index(group)
     chips, n = lax.axis_size("chip"), lax.axis_size(group)
     my_chip, my_core = lax.axis_index("chip"), lax.axis_index("core")

time: 98.4 us -> 183 us (1.86)
  Pallas kernels: 0 us -> 94.7 us
  blocking collectives: 12.6 us -> 41.1 us
  starting transfers between devices: 19.2 us -> 7.87 us
  between operations: 8.05 us -> 0.93 us
  waiting for transfers between devices: 36.1 us -> 29.3 us
  other arithmetic: 8.77 us -> 2.16 us
  local copies, waits for them, and re-layouts: 8.8 us -> 3.16 us
    pallas_call x0 -> x4, Pallas kernels: none -> 94.7 us  [the longest x1 66.2 us: per_device(): pl.pallas_call(merge_kernel, out_shape=(jax.ShapeDtypeStruct(pieces, bf16...]
    all_to_all x1 -> x3, blocking collectives: 12.6 us -> 41.1 us  [exchange(): return lax.all_to_all(blocks, axis, 0, 0, tiled=True)]
    all_to_all x4 -> x2, starting transfers between devices: 19 us -> 7.38 us  [exchange(): return lax.all_to_all(blocks, axis, 0, 0, tiled=True)]
    all_to_all x4 -> x2, waiting for transfers between devices: 33.5 us -> 27.8 us  [exchange(): return lax.all_to_all(blocks, axis, 0, 0, tiled=True)]
    dynamic_slice x8 -> x0, local copies, waits for them, and re-layouts: 4.97 us -> none  [the longest x2 2.02 us: per_device(): given_slot, taken_slot = (send_slot[me], land_slot[me])]
    select_n x8 -> x0, other arithmetic: 4.67 us -> none  [the longest x1 2.8 us: per_device(): jnp.where(append_now[:, :, None], new_keys[:, None, :], keys_after)]
    unnamed x26 -> x36, local copies, waits for them, and re-layouts: 0.07 us -> 2.91 us
  transfers between devices with their start and end apart: 6 -> 4, of which waited for: 6 -> 3; matrix products, arithmetic and copies ran while one was open for 8% -> 0% of each run, Pallas kernels for 0% -> 4%
where the time goes in v2:
time: 183 us
  Pallas kernels  94.7 us (52%)
  blocking collectives  41.1 us (22%)
  waiting for transfers between devices  29.3 us (16%)
  starting transfers between devices  7.87 us (4%)
  matrix products  3.26 us (2%)
  local copies, waits for them, and re-layouts  3.16 us (2%)
  other arithmetic  2.16 us (1%)
    pallas_call x1, Pallas kernels, per_device(): pl.pallas_call(merge_kernel, out_shape=(jax.ShapeDtypeStruct(pieces, bf16...  66.2 us
    all_to_all x3, blocking collectives, exchange(): return lax.all_to_all(blocks, axis, 0, 0, tiled=True)  41.1 us
    all_to_all x2, waiting for transfers between devices, exchange(): return lax.all_to_all(blocks, axis, 0, 0, tiled=True)  27.8 us
    pallas_call x1, Pallas kernels, per_device(): pl.pallas_call(pack_kernel, out_shape=(jax.ShapeDtypeStruct((n, lines, HD...  18.6 us
    all_to_all x2, starting transfers between devices, exchange(): return lax.all_to_all(blocks, axis, 0, 0, tiled=True)  7.38 us
    pallas_call x1, Pallas kernels, per_device(): pl.pallas_call(select_kernel, out_shape=(jax.ShapeDtypeStruct((n, 2 * TIL...  6.54 us
  transfers between devices with their start and end apart: 4, of which 3 were waited for; matrix products, arithmetic and copies ran while one was open for 0% of the time, Pallas kernels for 4%

profile of v2, /device:TPU:0, one launch (start us, length us, event | category | flops | bytes accessed | tf_op | source)
XLA Modules:
  0.0 182.5 jit_solution(5879799011940836685)
XLA Ops:
  0.6 0.0 copy-start
  0.6 0.0 copy-start.5
  0.7 0.0 copy-start.6
  0.7 0.0 copy-start.4
  0.7 0.0 copy-start.1
  0.7 0.0 copy-start.8
  0.7 0.0 copy-start.7
  0.7 0.0 copy-start.10
  0.7 0.0 copy-start.11
  0.7 0.0 copy-start.9
  0.8 18.6 %pack.1 = (bf16[16,48,128]{2,1,0:T(8,128)(2,1)}, bf16[16,32,512]{2,1,0:T(8,128)(2,1)}) custom-call(s32[16]{0:T(128)} %send_slot.7, s32[16]{0:T(128)} %land_slot.5, bf16[32,4,128]{2,1,0:T(4,128)(2,1)} %bitcast.24, bf16[4,4,128]{2,1,0:T(4,128)(2,1)} %bitcast.26, bf16[4,4,128]{2,1,0:T(4,128)(2,1)} %bitcast.29, bf16[4,16,16,512]{3,2,1,0:T(8,128)(2,1)} %bitcast.20, ...), custom_call_target="tpu_custom_call" | custom-call | bytes 1048576 | tf_op jit(solution)/shard_map/pack/pallas_call | solution.py:226
  19.4 16.4 %all_to_all.25.packets = bf16[16,48,128]{2,1,0:T(8,128)(2,1)S(1)} all-to-all(bf16[16,48,128]{2,1,0:T(8,128)(2,1)} %get-tuple-element.10), channel_id=1, replica_groups=mesh['parts'=2,'chip'=8,'core'=2] {'chip','core'}, dimensions={0} | all-to-all | bytes 393216 | tf_op jit(solution)/shard_map/all_to_all | solution.py:20
  35.8 0.0 copy-done.5
  35.8 0.0 copy-done.6
  35.8 0.0 copy-done.4
  35.8 0.0 copy-done.1
  35.8 0.0 copy-done.8
  35.8 0.0 copy-done.7
  35.8 0.0 copy-done.10
  35.8 0.0 copy-done.11
  35.8 0.0 copy-done.9
  35.8 0.0 copy-start.2
  35.8 1.2 copy-done.2
  37.1 3.4 %attend.1._ = bf16[8,4,4096]{2,1,0:T(4,128)(2,1)S(1)} custom-call(s32[16]{0:T(128)S(1)} %copy-done.8, s32[16]{0:T(128)S(1)} %copy-done.9, s32[4]{0:T(128)S(1)} %copy-done.10, s32[4]{0:T(128)S(1)} %copy-done.11, bf16[16,48,128]{2,1,0:T(8,128)(2,1)S(1)} %all_to_all.25.packets, bf16[32,4,128]{2,1,0:T(4,128)(2,1)S(1)} %bitcast.25, ...), custom_call_target="tpu_custom_call" | custom-call | flops 16777216 | bytes 2097152 | tf_op jit(solution)/shard_map/attend/pallas_call | solution.py:240
  40.4 0.0 copy-start.3
  40.4 11.6 %all_to_all.26 = bf16[8,4,4096]{2,1,0:T(4,128)(2,1)S(1)} all-to-all(bf16[8,4,4096]{2,1,0:T(4,128)(2,1)S(1)} %attend.1._), channel_id=1, replica_groups=mesh['parts'=2,'chip'=8,'core'=2] {'chip'}, dimensions={0} | all-to-all | bytes 524288 | tf_op jit(solution)/shard_map/all_to_all | solution.py:20
  52.0 0.0 copy-start.16
  52.0 3.7 %all-to-all-start = ((bf16[16,32,512]{2,1,0:T(8,128)(2,1)}), bf16[16,32,512]{2,1,0:T(8,128)(2,1)S(1)}, u32[]{:S(2)}, u32[]{:S(2)}) async-start(bf16[16,32,512]{2,1,0:T(8,128)(2,1)} %get-tuple-element.9), calls=%async_computation | async-start | bytes 1048576 | tf_op jit(solution)/shard_map/all_to_all | solution.py:20
  55.7 0.4 collective-permute-start
  56.1 14.1 %all-to-all-done.spread = bf16[16,32,512]{2,1,0:T(8,128)(2,1)S(1)} async-done(((bf16[16,32,512]{2,1,0:T(8,128)(2,1)}), bf16[16,32,512]{2,1,0:T(8,128)(2,1)S(1)}, u32[]{:S(2)}, u32[]{:S(2)}) %all-to-all-start) | async-done | bytes 524320 | tf_op jit(solution)/shard_map/all_to_all | solution.py:20
  70.2 0.0 copy-done.3
  70.2 0.0 copy-start.15
  70.2 0.8 copy-done.15
  71.0 6.5 %select.1 = (bf16[16,32,512]{2,1,0:T(8,128)(2,1)}, bf16[64,64]{1,0:T(8,128)(2,1)}) custom-call(s32[16]{0:T(128)} %send_slot.7, s32[16]{0:T(128)} %send_to.5, s32[16]{0:T(128)} %receive_from.3, s32[16]{0:T(128)} %land_slot.5, bf16[16,32,512]{2,1,0:T(8,128)(2,1)} %copy-done.15, bf16[8,4,4096]{2,1,0:T(4,128)(2,1)} %copy-done.3), custom_call_target="tpu_custom_call" | custom-call | bytes 1048576 | tf_op jit(solution)/shard_map/select/pallas_call | solution.py:259
  77.5 0.0 copy-done.16
  77.6 0.0 collective-permute-done
  77.6 1.4 pad_maximum_fusion
  78.9 0.1 reshape.44
  79.1 0.0 copy-start.14
  79.1 0.0 copy-start.17
  79.1 2.2 %fusion.6 = f32[64,256]{1,0:T(8,128)S(1)} fusion(bf16[64,4096]{1,0:T(8,128)(2,1)S(1)} %reshape.44, bf16[4096,256]{1,0:T(8,128)(2,1)} %param.29), kind=kOutput, calls=%fused_computation.9 | convolution fusion | flops 134217728 | bytes 2686976 | tf_op jit(solution)/shard_map/dot_general | solution.py:274
  81.3 0.0 copy-done.14
  81.3 0.5 fusion.7
  81.8 0.0 copy-done
  81.8 0.0 copy-done.17
  81.8 0.6 fusion
  82.4 0.1 collective-permute-start.1
  82.5 1.5 collective-permute-done.1
  84.0 0.1 fusion.1
  84.1 0.1 reshape.45._
  84.2 0.0 copy-start.12
  84.2 13.2 %all_to_all.27 = bf16[8,4,4096]{2,1,0:T(4,128)(2,1)S(1)} all-to-all(bf16[8,4,4096]{2,1,0:T(4,128)(2,1)S(1)} %reshape.45._), channel_id=1, replica_groups=mesh['parts'=2,'chip'=8,'core'=2] {'chip'}, dimensions={0} | all-to-all | bytes 524288 | tf_op jit(solution)/shard_map/all_to_all | solution.py:20
  97.4 3.7 %all-to-all-start.4 = ((bf16[16,32,512]{2,1,0:T(8,128)(2,1)}), bf16[16,32,512]{2,1,0:T(8,128)(2,1)S(1)}, u32[]{:S(2)}, u32[]{:S(2)}) async-start(bf16[16,32,512]{2,1,0:T(8,128)(2,1)} %get-tuple-element.12), calls=%async_computation.4 | async-start | bytes 1048576 | tf_op jit(solution)/shard_map/all_to_all | solution.py:20
  101.1 0.7 reduce_sum.12
  101.8 13.7 %all-to-all-done.4.arrived = bf16[16,32,512]{2,1,0:T(8,128)(2,1)S(1)} async-done(((bf16[16,32,512]{2,1,0:T(8,128)(2,1)}), bf16[16,32,512]{2,1,0:T(8,128)(2,1)S(1)}, u32[]{:S(2)}, u32[]{:S(2)}) %all-to-all-start.4) | async-done | bytes 524320 | tf_op jit(solution)/shard_map/all_to_all | solution.py:20
  115.6 0.0 copy-done.12
  115.6 0.0 copy-start.13
  115.6 0.8 copy-done.13
  116.4 66.2 %merge.1 = (bf16[4,16,16,512]{3,2,1,0:T(8,128)(2,1)}, bf16[4,16,16,512]{3,2,1,0:T(8,128)(2,1)}) custom-call(s32[16]{0:T(128)} %send_slot.7, s32[16]{0:T(128)} %send_to.5, s32[16]{0:T(128)} %receive_from.3, s32[16]{0:T(128)} %land_slot.5, s32[16]{0:T(128)} %land_length.1, s32[4]{0:T(128)} %lengths.3, s32[4]{0:T(128)} %unfinished.3, ...), custom_call_target="tpu_custom_call" | custom-call | bytes 8388608 | tf_op jit(solution)/shard_map/merge/pallas_call | solution.py:284
  (1 shorter events, 0.0 us)
Async XLA Ops:
  0.6 81.1 %copy-start = (bf16[256,4096]{1,0:T(8,128)(2,1)S(1)}, bf16[256,4096]{1,0:T(8,128)(2,1)}, u32[]{:S(2)}) copy-start(bf16[256,4096]{1,0:T(8,128)(2,1)} %param.31) | copy-start | bytes 6291460
  0.6 35.1 %copy-start.5 = (bf16[4,512]{1,0:T(4,128)(2,1)S(1)}, bf16[4,512]{1,0:T(4,128)(2,1)}, u32[]{:S(2)}) copy-start(bf16[4,512]{1,0:T(4,128)(2,1)} %param.26) | copy-start | bytes 12292
  0.7 35.1 %copy-start.6 = (bf16[4,512]{1,0:T(4,128)(2,1)S(1)}, bf16[4,512]{1,0:T(4,128)(2,1)}, u32[]{:S(2)}) copy-start(bf16[4,512]{1,0:T(4,128)(2,1)} %param.27) | copy-start | bytes 12292
  0.7 35.1 %copy-start.4 = (bf16[4,4096]{1,0:T(4,128)(2,1)S(1)}, bf16[4,4096]{1,0:T(4,128)(2,1)}, u32[]{:S(2)}) copy-start(bf16[4,4096]{1,0:T(4,128)(2,1)} %param.25) | copy-start | bytes 98308
  0.7 35.1 %copy-start.1 = (bf16[4,256,512]{2,1,0:T(8,128)(2,1)S(1)}, bf16[4,256,512]{2,1,0:T(8,128)(2,1)}, u32[]{:S(2)}) copy-start(bf16[4,256,512]{2,1,0:T(8,128)(2,1)} %ck.1) | copy-start | bytes 3145732
  0.7 35.1 %copy-start.8 = (s32[16]{0:T(128)S(1)}, s32[16]{0:T(128)}, u32[]{:S(2)}) copy-start(s32[16]{0:T(128)} %send_slot.7) | copy-start | bytes 196
  0.7 35.1 %copy-start.7 = (f32[4096]{0:T(1024)S(1)}, f32[4096]{0:T(1024)}, u32[]{:S(2)}) copy-start(f32[4096]{0:T(1024)} %param.28) | copy-start | bytes 49156
  0.7 35.1 %copy-start.10 = (s32[4]{0:T(128)S(1)}, s32[4]{0:T(128)}, u32[]{:S(2)}) copy-start(s32[4]{0:T(128)} %lengths.3) | copy-start | bytes 52
  0.7 35.1 %copy-start.11 = (s32[4]{0:T(128)S(1)}, s32[4]{0:T(128)}, u32[]{:S(2)}) copy-start(s32[4]{0:T(128)} %unfinished.3) | copy-start | bytes 52
  0.7 35.1 %copy-start.9 = (s32[16]{0:T(128)S(1)}, s32[16]{0:T(128)}, u32[]{:S(2)}) copy-start(s32[16]{0:T(128)} %send_to.5) | copy-start | bytes 196
  35.8 1.2 copy-start.2
  40.4 29.8 %copy-start.3 = (bf16[8,4,4096]{2,1,0:T(4,128)(2,1)}, bf16[8,4,4096]{2,1,0:T(4,128)(2,1)S(1)}, u32[]{:S(2)}) copy-start(bf16[8,4,4096]{2,1,0:T(4,128)(2,1)S(1)} %attend.1._) | copy-start | bytes 786436
  52.0 25.5 %copy-start.16 = (bf16[8,4,4096]{2,1,0:T(4,128)(2,1)}, bf16[8,4,4096]{2,1,0:T(4,128)(2,1)S(1)}, u32[]{:S(2)}) copy-start(bf16[8,4,4096]{2,1,0:T(4,128)(2,1)S(1)} %all_to_all.26) | copy-start | bytes 786436
  52.0 18.2 %all-to-all-start = ((bf16[16,32,512]{2,1,0:T(8,128)(2,1)}), bf16[16,32,512]{2,1,0:T(8,128)(2,1)S(1)}, u32[]{:S(2)}, u32[]{:S(2)}) async-start(bf16[16,32,512]{2,1,0:T(8,128)(2,1)} %get-tuple-element.9), calls=%async_computation | async-start | bytes 1048576 | tf_op jit(solution)/shard_map/all_to_all | solution.py:20
  55.7 21.8 %collective-permute-start = (bf16[8,4,4096]{2,1,0:T(4,128)(2,1)S(1)}, bf16[8,4,4096]{2,1,0:T(4,128)(2,1)}, u32[]{:S(2)}, u32[]{:S(2)}) collective-permute-start(bf16[8,4,4096]{2,1,0:T(4,128)(2,1)S(1)} %all_to_all.26), channel_id=1, source_target_pairs={{0,1},{1,0},{2,3},{3,2},{4,5},{5,4},{6,7},{7,6},{8,9},{9,8},{10,11... | collective-permute-start | bytes 786440 | tf_op jit(solution)/shard_map/ppermute | solution.py:272
  70.2 0.8 copy-start.15
  79.1 2.2 %copy-start.14 = (bf16[4096,256]{1,0:T(8,128)(2,1)S(1)}, bf16[4096,256]{1,0:T(8,128)(2,1)}, u32[]{:S(2)}) copy-start(bf16[4096,256]{1,0:T(8,128)(2,1)} %param.30) | copy-start | bytes 6291460
  79.1 2.7 %copy-start.17 = (bf16[64,64]{1,0:T(8,128)(2,1)S(1)}, bf16[64,64]{1,0:T(8,128)(2,1)}, u32[]{:S(2)}) copy-start(bf16[64,64]{1,0:T(8,128)(2,1)} %get-tuple-element.11) | copy-start | bytes 24580
  82.4 1.6 collective-permute-start.1
  84.2 31.4 %copy-start.12 = (bf16[8,4,4096]{2,1,0:T(4,128)(2,1)}, bf16[8,4,4096]{2,1,0:T(4,128)(2,1)S(1)}, u32[]{:S(2)}) copy-start(bf16[8,4,4096]{2,1,0:T(4,128)(2,1)S(1)} %reshape.45._) | copy-start | bytes 786436
  97.4 18.2 %all-to-all-start.4 = ((bf16[16,32,512]{2,1,0:T(8,128)(2,1)}), bf16[16,32,512]{2,1,0:T(8,128)(2,1)S(1)}, u32[]{:S(2)}, u32[]{:S(2)}) async-start(bf16[16,32,512]{2,1,0:T(8,128)(2,1)} %get-tuple-element.12), calls=%async_computation.4 | async-start | bytes 1048576 | tf_op jit(solution)/shard_map/all_to_all | solution.py:20
  115.6 0.8 copy-start.13

commit v3 on v1

--- a/solution.py
+++ b/solution.py
@@ -3,18 +3,409 @@
 import jax
 import jax.numpy as jnp
 from jax import lax
+from jax.experimental import pallas as pl
+from jax.experimental.pallas import tpu as pltpu
 from jax.sharding import PartitionSpec as P
 
 HQ = 32
 KVH = 4
 HD = 128
+PER = HQ // KVH
+TILE = 16
+GROUP = ("chip", "core")
+SMEM, VMEM = pltpu.SMEM, pltpu.VMEM
 
 
 def exchange(blocks, axis):
     return lax.all_to_all(blocks, axis, 0, 0, tiled=True)
 
 
+def spec(space):
+    return pl.BlockSpec(memory_space=space)
+
+
+def cost(flops, moved):
+    return pl.CostEstimate(flops=flops, bytes_accessed=moved, transcendentals=0)
+
+
+def pack_kernel(send_slot, send_to, receive_from, land_slot, q, nk, nv, ck, cv, leaving, packet, sems):
+    me = lax.axis_index(GROUP)
+    slots = q.shape[1]
+    giving = send_to[me] != me
+    copies = [
+        pltpu.make_async_copy(cache.at[send_slot[me]], leaving.at[:, pl.ds(i * TILE, TILE)], sems.at[i])
+        for i, cache in enumerate((ck, cv))
+    ]
+
+    @pl.when(giving)
+    def _():
+        for copy in copies:
+            copy.start()
+        for copy in copies:
+            copy.wait()
+
+    @pl.when(jnp.logical_not(giving))
+    def _():
+        taken = land_slot[me]
+
+        def line(x):
+            mine = lax.broadcasted_iota(jnp.int32, (x.shape[0], slots, HD), 1) == taken
+            return jnp.sum(jnp.where(mine, x[...].astype(jnp.float32), 0.0), axis=1)
+
+        heads, key, value = line(q), line(nk), line(nv)
+        packet[...] = jnp.zeros_like(packet)
+        for k in range(KVH):
+            columns = slice(k * HD, (k + 1) * HD)
+            packet[0:PER, columns] = heads[k * PER : (k + 1) * PER]
+            packet[PER : PER + 1, columns] = key[k : k + 1]
+            packet[PER + 1 : PER + 2, columns] = value[k : k + 1]
+        leaving[receive_from[me], 0:TILE] = packet[...].astype(jnp.bfloat16)
+
+
+def put_line(buf, at, base, line, fresh):
+    here = lax.broadcasted_iota(jnp.int32, (TILE, HD), 0) == line
+    for k in range(KVH):
+        columns = slice(k * HD, (k + 1) * HD)
+        old = buf[at, pl.ds(base, TILE), columns].astype(jnp.float32)
+        buf[at, pl.ds(base, TILE), columns] = jnp.where(here, fresh[k], old).astype(jnp.bfloat16)
+
+
+def attend_kernel(
+    send_slot, send_to, lengths, unfinished, q, nk, nv, gain, spread, ck, cv, out,
+    kbuf, vbuf, tile, q32, att, sems, tile_sem
+):
+    me = lax.axis_index(GROUP)
+    slots = ck.shape[0]
+    target, given = send_to[me], send_slot[me]
+    fetch = pltpu.make_async_copy(spread.at[target, pl.ds(0, TILE)], tile, tile_sem)
+    fetch.start()
+    loads = []
+    for j in range(slots):
+        loads.append(
+            (
+                pltpu.make_async_copy(ck.at[j], kbuf.at[j], sems.at[0, j]),
+                pltpu.make_async_copy(cv.at[j], vbuf.at[j], sems.at[1, j]),
+            )
+        )
+        for copy in loads[j]:
+            copy.start()
+    q32[...] = q[...].astype(jnp.float32)
+    nk32, nv32 = nk[...].astype(jnp.float32), nv[...].astype(jnp.float32)
+    fetch.wait()
+    packet = tile[...].astype(jnp.float32)
+    scale = 1.0 / math.sqrt(HD)
+    for j in range(slots):
+        moved = (target != me) & (given == j)
+        alive = jnp.where(moved, 1, unfinished[j]) > 0
+        length = lengths[j]
+        block = length // TILE
+        base = pl.multiple_of(block * TILE, TILE)
+        line = jnp.where(alive, length - block * TILE, -1)
+
+        def fresh(row, own):
+            return [
+                jnp.where(moved, packet[row : row + 1, k * HD : (k + 1) * HD], own[k, j : j + 1]) for k in range(KVH)
+            ]
+
+        for copy in loads[j]:
+            copy.wait()
+        put_line(kbuf, j, base, line, fresh(PER, nk32))
+        put_line(vbuf, j, base, line, fresh(PER + 1, nv32))
+        own_heads = q32[:, j, :]
+        scores = jnp.concatenate(
+            [
+                lax.dot_general(
+                    jnp.where(moved, packet[0:PER, k * HD : (k + 1) * HD], own_heads[k * PER : (k + 1) * PER]).astype(
+                        jnp.bfloat16
+                    ),
+                    kbuf[j, :, k * HD : (k + 1) * HD],
+                    (((1,), (1,)), ((), ())),
+                    preferred_element_type=jnp.float32,
+                )
+                for k in range(KVH)
+            ],
+            axis=0,
+        )
+        visible = lax.broadcasted_iota(jnp.int32, scores.shape, 1) <= length
+        scores = jnp.where(visible, scores * scale, jnp.float32(-1e30))
+        expo = jnp.exp(scores - jnp.max(scores, axis=1, keepdims=True))
+        probs = expo / jnp.sum(expo, axis=1, keepdims=True)
+        attended = jnp.concatenate(
+            [
+                jnp.dot(
+                    probs[k * PER : (k + 1) * PER].astype(jnp.bfloat16),
+                    vbuf[j, :, k * HD : (k + 1) * HD],
+                    preferred_element_type=jnp.float32,
+                )
+                for k in range(KVH)
+            ],
+            axis=0,
+        )
+        mean = jnp.sum(attended * attended, keepdims=True) * (1.0 / (HQ * HD))
+        normed = attended * lax.rsqrt(mean + 1e-06) * gain[...]
+        att[:, j, :] = jnp.where(alive, normed, 0.0)
+    for h in range(HQ):
+        head = att[h].astype(jnp.bfloat16)
+        for c in range(out.shape[0]):
+            out[c, :, h * HD : (h + 1) * HD] = head
+
+
+def aside_kernel(
+    send_slot, send_to, receive_from, land_slot, lengths, unfinished, nk, nv, ck, cv, spread, _,
+    keys, values, outgoing, pick, kbuf, vbuf, sems, piece_sem
+):
+    me = lax.axis_index(GROUP)
+    core = lax.axis_index("core")
+    slots, n, rows = ck.shape[0], outgoing.shape[0], pick.shape[0]
+    half = rows // 2
+    pairs = ((ck, kbuf, keys), (cv, vbuf, values))
+
+    def piece(d):
+        return pltpu.make_async_copy(spread.at[receive_from[d]], outgoing.at[d, pl.ds(0, 2 * TILE)], piece_sem.at[d])
+
+    def load(i, j):
+        return pltpu.make_async_copy(pairs[i][0].at[j], pairs[i][1].at[j], sems.at[i, j])
+
+    def store(i, j):
+        return pltpu.make_async_copy(pairs[i][1].at[j], pairs[i][2].at[j], sems.at[i, j])
+
+    for j in range(slots):
+        for i in range(2):
+            load(i, j).start()
+    for d in range(n):
+        pl.when(receive_from[d] != d)(lambda d=d: piece(d).start())
+    row = lax.broadcasted_iota(jnp.int32, (rows, HD), 0)
+    device = row // slots
+    wanted = jnp.where((device & 1) == core, 0, half) + (device >> 1) * slots + (row & (slots - 1))
+    for d in range(n):
+        source = receive_from[d]
+        held = jnp.where(lax.rem(source, 2) == core, 0, half) + (source // 2) * slots + send_slot[source]
+        landing = jnp.where(source != d, d * slots + land_slot[d], -1)
+        vacated = jnp.where(send_to[d] != d, d * slots + send_slot[d], -1)
+        wanted = jnp.where(row == landing, held, wanted)
+        wanted = jnp.where(row == vacated, -1, wanted)
+    column = lax.broadcasted_iota(jnp.int32, (rows, rows), 1)
+    pick[...] = (column == wanted[:, :1]).astype(jnp.float32).astype(jnp.bfloat16)
+    for j in range(slots):
+        vacated = (send_to[me] != me) & (send_slot[me] == j)
+        alive = jnp.where(vacated, 0, unfinished[j]) > 0
+        length = lengths[j]
+        block = length // TILE
+        base = pl.multiple_of(block * TILE, TILE)
+        line = jnp.where(alive, length - block * TILE, -1)
+        for i, own in enumerate((nk, nv)):
+            load(i, j).wait()
+            put_line(pairs[i][1], j, base, line, [own[k, j : j + 1].astype(jnp.float32) for k in range(KVH)])
+            store(i, j).start()
+    for d in range(n):
+        pl.when(receive_from[d] != d)(lambda d=d: piece(d).wait())
+    for j in range(slots):
+        for i in range(2):
+            store(i, j).wait()
+
+
+def ffn_kernel(near, far, gate_weight, up_weight, pick, down_weight, mine, theirs):
+    core = lax.axis_index("core")
+    x = jnp.concatenate([near[...], far[...]], axis=0)
+    gate = jnp.dot(x, gate_weight[...], preferred_element_type=jnp.float32)
+    up_part = jnp.dot(x, up_weight[...], preferred_element_type=jnp.float32)
+    hidden = (gate / (1.0 + jnp.exp(-gate)) * up_part).astype(jnp.bfloat16)
+    hidden = jnp.dot(pick[...], hidden, preferred_element_type=jnp.float32).astype(jnp.bfloat16)
+    width = mine.shape[1]
+
+    def down(side):
+        columns = pl.ds(pl.multiple_of(side * width, width), width)
+        return jnp.dot(hidden, down_weight[:, columns], preferred_element_type=jnp.float32)
+
+    theirs[...] = down(1 - core).astype(jnp.bfloat16)
+    mine[...] = down(core)
+
+
+def place_kernel(mine, theirs, outgoing, out, rows, sem):
+    n, _, wide = rows.shape
+    slots = mine.shape[0] // n
+    for d in range(n):
+        at = slice(d * slots, (d + 1) * slots)
+        both = mine[at] + theirs[at].astype(jnp.float32)
+        rows[d] = jnp.concatenate(
+            [both[:, g * wide : (g + 1) * wide] for g in range(both.shape[1] // wide)], axis=0
+        ).astype(jnp.bfloat16)
+    copy = pltpu.make_async_copy(rows, out.at[:, pl.ds(2 * TILE, TILE)], sem)
+    copy.start()
+    copy.wait()
+
+
+def finish_kernel(
+    receive_from, land_slot, land_length, nk, nv, arrived, keys_in, values_in, decoded, keys, values,
+    kbuf, vbuf, sums, sems
+):
+    me = lax.axis_index(GROUP)
+    n, wide = sums.shape[0], sums.shape[2]
+    slots, slot = decoded.shape[0], land_slot[me]
+    arriving = receive_from[me] != me
+    bring = pltpu.make_async_copy(arrived.at[:, pl.ds(2 * TILE, TILE)], sums, sems.at[2])
+    bring.start()
+    pairs = ((kbuf, keys, nk), (vbuf, values, nv))
+    loads = [
+        pltpu.make_async_copy(arrived.at[:, pl.ds(i * TILE, TILE)], pairs[i][0].at[0], sems.at[i]) for i in range(2)
+    ]
+    stores = [pltpu.make_async_copy(pairs[i][0].at[0], pairs[i][1].at[slot], sems.at[i]) for i in range(2)]
+
+    @pl.when(arriving)
+    def _():
+        for copy in loads:
+            copy.start()
+        length = land_length[me]
+        block = length // TILE
+        for i, (buf, _, own) in enumerate(pairs):
+            loads[i].wait()
+            mine = lax.broadcasted_iota(jnp.int32, (KVH, slots, HD), 1) == slot
+            token = jnp.sum(jnp.where(mine, own[...].astype(jnp.float32), 0.0), axis=1)
+            here = lax.broadcasted_iota(jnp.int32, (TILE, HD), 0) == length - block * TILE
+            for k in range(KVH):
+                columns = slice(k * HD, (k + 1) * HD)
+                old = buf[0, block, :, columns].astype(jnp.float32)
+                buf[0, block, :, columns] = jnp.where(here, token[k : k + 1], old).astype(jnp.bfloat16)
+            stores[i].start()
+
+    bring.wait()
+    for side in range(2):
+        total = sums[side].astype(jnp.float32)
+        for c in range(1, n // 2):
+            total += sums[2 * c + side].astype(jnp.float32)
+        for g in range(TILE // slots):
+            at = (side * (TILE // slots) + g) * wide
+            decoded[:, at : at + wide] = total[g * slots : (g + 1) * slots].astype(jnp.bfloat16)
+
+    @pl.when(arriving)
+    def _():
+        for copy in stores:
+            copy.wait()
+
+
 def per_device(
+    cache_keys, cache_values, lengths, unfinished, send_slot, send_to, receive_from, land_slot, land_length,
+    queries, new_keys, new_values, norm_gain, gate_weight, up_weight, down_weight
+):
+    chips, n = lax.axis_size("chip"), lax.axis_size(GROUP)
+    slots, capacity, kv_width = cache_keys.shape
+    width = queries.shape[1]
+    if capacity != TILE * n or slots * width != 2 * TILE * kv_width:
+        return per_device_small_pieces(
+            cache_keys, cache_values, lengths, unfinished, send_slot, send_to, receive_from, land_slot, land_length,
+            queries, new_keys, new_values, norm_gain, gate_weight, up_weight, down_weight
+        )
+    bf16, f32 = jnp.bfloat16, jnp.float32
+    dma = pltpu.SemaphoreType.DMA
+    pieces = (slots, n, TILE, kv_width)
+    room = pltpu.CompilerParams(vmem_limit_bytes=16 * 2**20)
+
+    def shape(dims, kind=bf16):
+        return jax.ShapeDtypeStruct(dims, kind)
+
+    def by_head(x):
+        return x.reshape(slots, -1, HD).transpose(1, 0, 2)
+
+    q, nk, nv = by_head(queries), by_head(new_keys), by_head(new_values)
+    leaving = pl.pallas_call(
+        pack_kernel,
+        out_shape=shape((n, 2 * TILE, kv_width)),
+        in_specs=[spec(SMEM)] * 4 + [spec(VMEM)] * 3 + [spec(pl.ANY)] * 2,
+        out_specs=spec(VMEM),
+        scratch_shapes=[VMEM((TILE, kv_width), f32), dma((2,))],
+        compiler_params=room,
+        cost_estimate=cost(0, 2**20),
+        name="pack",
+    )(
+        send_slot, send_to, receive_from, land_slot, q, nk, nv, cache_keys.reshape(pieces), cache_values.reshape(pieces)
+    )
+    spread = exchange(leaving, GROUP)
+    rows = pl.pallas_call(
+        attend_kernel,
+        out_shape=shape((chips, slots, width)),
+        in_specs=[spec(SMEM)] * 4 + [spec(VMEM)] * 4 + [spec(pl.ANY)] * 3,
+        out_specs=spec(VMEM),
+        scratch_shapes=[
+            VMEM(cache_keys.shape, bf16),
+            VMEM(cache_keys.shape, bf16),
+            VMEM((TILE, kv_width), bf16),
+            VMEM((HQ, slots, HD), f32),
+            VMEM((HQ, slots, HD), f32),
+            dma((2, slots)),
+            dma,
+        ],
+        compiler_params=room,
+        cost_estimate=cost(2**24, 2**21),
+        name="attend",
+    )(
+        send_slot, send_to, lengths, unfinished, q, nk, nv, norm_gain.reshape(HQ, HD), spread, cache_keys, cache_values
+    )
+    near = exchange(rows, "chip")
+    keys_own, values_own, outgoing, pick = pl.pallas_call(
+        aside_kernel,
+        out_shape=(
+            shape(cache_keys.shape),
+            shape(cache_keys.shape),
+            shape((n, 3 * TILE, kv_width)),
+            shape((n * slots, n * slots)),
+        ),
+        in_specs=[spec(SMEM)] * 6 + [spec(VMEM)] * 2 + [spec(pl.ANY)] * 4,
+        out_specs=(spec(pl.ANY), spec(pl.ANY), spec(pl.ANY), spec(VMEM)),
+        scratch_shapes=[VMEM(cache_keys.shape, bf16), VMEM(cache_keys.shape, bf16), dma((2, slots)), dma((n,))],
+        compiler_params=room,
+        cost_estimate=cost(0, 2**23),
+        name="aside",
+    )(
+        send_slot, send_to, receive_from, land_slot, lengths, unfinished, nk, nv, cache_keys, cache_values, spread, rows
+    )
+    near, pick = lax.optimization_barrier((near, pick))
+    far = lax.ppermute(near, "core", [(0, 1), (1, 0)])
+    mine, theirs = pl.pallas_call(
+        ffn_kernel,
+        out_shape=(shape((n * slots, width // 2), f32), shape((n * slots, width // 2))),
+        in_specs=[spec(VMEM)] * 6,
+        out_specs=(spec(VMEM), spec(VMEM)),
+        compiler_params=room,
+        cost_estimate=cost(6 * n * slots * width * gate_weight.shape[1], 3 * 2**21),
+        name="ffn",
+    )(
+        near.reshape(chips * slots, width), far.reshape(chips * slots, width), gate_weight, up_weight, pick, down_weight
+    )
+    theirs = lax.ppermute(theirs, "core", [(0, 1), (1, 0)])
+    outgoing = pl.pallas_call(
+        place_kernel,
+        out_shape=shape((n, 3 * TILE, kv_width)),
+        in_specs=[spec(VMEM)] * 2 + [spec(pl.ANY)],
+        out_specs=spec(pl.ANY),
+        scratch_shapes=[VMEM((n, TILE, kv_width), bf16), dma],
+        input_output_aliases={2: 0},
+        compiler_params=room,
+        cost_estimate=cost(0, 2**20),
+        name="place",
+    )(mine, theirs, outgoing)
+    arrived = exchange(outgoing, GROUP)
+    decoded, keys_after, values_after = pl.pallas_call(
+        finish_kernel,
+        out_shape=(shape((slots, width)), shape(pieces), shape(pieces)),
+        in_specs=[spec(SMEM)] * 3 + [spec(VMEM)] * 2 + [spec(pl.ANY)] * 3,
+        out_specs=(spec(VMEM), spec(pl.ANY), spec(pl.ANY)),
+        scratch_shapes=[
+            VMEM((1, n, TILE, kv_width), bf16),
+            VMEM((1, n, TILE, kv_width), bf16),
+            VMEM((n, TILE, kv_width), bf16),
+            dma((3,)),
+        ],
+        input_output_aliases={6: 1, 7: 2},
+        compiler_params=room,
+        cost_estimate=cost(0, 2**20),
+        name="finish",
+    )(
+        receive_from, land_slot, land_length, nk, nv, arrived, keys_own.reshape(pieces), values_own.reshape(pieces)
+    )
+    return (decoded, keys_after.reshape(cache_keys.shape), values_after.reshape(cache_keys.shape))
+
+
+def per_device_small_pieces(
     cache_keys,
     cache_values,
     lengths,
@@ -32,7 +423,7 @@
     up_weight,
     down_weight,
 ):
-    group = ("chip", "core")
+    group = GROUP
     me = lax.axis_index(group)
     chips, n = lax.axis_size("chip"), lax.axis_size(group)
     my_chip, my_core = lax.axis_index("chip"), lax.axis_index("core")

time: 98.4 us -> 84.1 us (0.85)
  blocking collectives: 12.6 us -> 45.5 us
  waiting for transfers between devices: 36.1 us -> 8.76 us
  starting transfers between devices: 19.2 us -> 4.26 us
  Pallas kernels: 0 us -> 11.1 us
  other arithmetic: 8.77 us -> 0 us
  between operations: 8.05 us -> 0.87 us
  local copies, waits for them, and re-layouts: 8.8 us -> 13.1 us
  matrix products: 4.07 us -> 0 us
    all_to_all x1 -> x2, blocking collectives: 12.6 us -> 45.5 us  [exchange(): return lax.all_to_all(blocks, axis, 0, 0, tiled=True)]
    all_to_all x4 -> x1, waiting for transfers between devices: 33.5 us -> 6.63 us  [exchange(): return lax.all_to_all(blocks, axis, 0, 0, tiled=True)]
    all_to_all x4 -> x1, starting transfers between devices: 19 us -> 4.05 us  [exchange(): return lax.all_to_all(blocks, axis, 0, 0, tiled=True)]
    unnamed x26 -> x50, local copies, waits for them, and re-layouts: 0.07 us -> 12 us
    pallas_call x0 -> x6, Pallas kernels: none -> 11.1 us  [the longest x1 4.12 us: per_device(): pl.pallas_call(attend_kernel, out_shape=shape((chips, slots, width)), in_...]
    dynamic_slice x8 -> x0, local copies, waits for them, and re-layouts: 4.97 us -> none  [the longest x2 2.02 us: per_device(): given_slot, taken_slot = (send_slot[me], land_slot[me])]
    select_n x8 -> x0, other arithmetic: 4.67 us -> none  [the longest x1 2.8 us: per_device(): jnp.where(append_now[:, :, None], new_keys[:, None, :], keys_after)]
    dot_general x5 -> x0, matrix products: 4.07 us -> none  [the longest x1 2.2 us: per_device(): up_part = jnp.dot(gathered, up_weight, preferred_element_type=jnp.float32)]
  transfers between devices with their start and end apart: 6 -> 3, of which waited for: 6 -> 3; matrix products, arithmetic and copies ran while one was open for 8% -> 1% of each run, Pallas kernels for 0% -> 3%
where the time goes in v3:
time: 84.1 us; the launch traced here: 83.7 us
  blocking collectives  45.5 us (54%)
  local copies, waits for them, and re-layouts  13.1 us (16%)
  Pallas kernels  11.1 us (13%)
  waiting for transfers between devices  8.76 us (10%)
  starting transfers between devices  4.26 us (5%)
  between operations  0.87 us (1%)
    all_to_all x2, blocking collectives, exchange(): return lax.all_to_all(blocks, axis, 0, 0, tiled=True)  45.5 us
    unnamed x50, local copies, waits for them, and re-layouts  12 us
    all_to_all x1, waiting for transfers between devices, exchange(): return lax.all_to_all(blocks, axis, 0, 0, tiled=True)  6.63 us
    pallas_call x1, Pallas kernels, per_device(): pl.pallas_call(attend_kernel, out_shape=shape((chips, slots, width)), in_...  4.12 us
    all_to_all x1, starting transfers between devices, exchange(): return lax.all_to_all(blocks, axis, 0, 0, tiled=True)  4.05 us
    pallas_call x1, Pallas kernels, per_device(): pl.pallas_call(aside_kernel, out_shape=(shape(cache_keys.shape), shape(ca...  2.73 us
    pallas_call x1, Pallas kernels, per_device(): pl.pallas_call(finish_kernel, out_shape=(shape((slots, width)), shape(pie...  2.07 us
  transfers between devices with their start and end apart: 3, of which 3 were waited for; matrix products, arithmetic and copies ran while one was open for 1% of the time, Pallas kernels for 3%

profile of v3, /device:TPU:0, one launch (start us, length us, event | category | flops | bytes accessed | tf_op | source)
XLA Modules:
  0.0 83.7 jit_solution(14464486892625420886)
XLA Ops:
  0.6 0.0 copy-start.23
  0.6 0.0 copy-start.22
  0.7 0.0 copy-start
  0.7 1.2 %copy-done = bf16[4,256,512]{2,1,0:T(8,128)(2,1)S(1)} copy-done((bf16[4,256,512]{2,1,0:T(8,128)(2,1)S(1)}, bf16[4,256,512]{2,1,0:T(8,128)(2,1)}, u32[]{:S(2)}) %copy-start) | copy-done | bytes 1048600
  1.9 0.0 copy-start.2
  1.9 1.2 %copy-done.2 = bf16[4,256,512]{2,1,0:T(8,128)(2,1)S(1)} copy-done((bf16[4,256,512]{2,1,0:T(8,128)(2,1)S(1)}, bf16[4,256,512]{2,1,0:T(8,128)(2,1)}, u32[]{:S(2)}) %copy-start.2) | copy-done | bytes 1048600
  3.1 0.0 copy-start.7
  3.1 0.8 copy-done.7
  3.9 0.0 copy-start.9
  3.9 0.7 copy-done.9
  4.6 0.0 copy-start.11
  4.6 0.7 copy-done.11
  5.2 0.0 copy-start.14
  5.2 0.7 copy-done.14
  5.9 0.0 copy-start.16
  5.9 0.7 copy-done.16
  6.6 0.0 copy-start.18
  6.6 0.7 copy-done.18
  7.2 0.0 copy-start.20
  7.2 0.7 copy-done.20
  7.9 0.0 copy-start.1
  7.9 0.0 copy-start.3
  7.9 0.0 copy-start.8
  7.9 0.0 copy-start.13
  7.9 0.7 pack.1
  8.6 0.0 copy-start.10
  8.6 0.0 copy-start.12
  8.6 0.0 copy-start.15
  8.6 0.0 copy-start.17
  8.6 0.0 copy-start.19
  8.6 0.0 copy-start.21
  8.6 21.8 %all_to_all.15.spread = bf16[16,32,512]{2,1,0:T(8,128)(2,1)S(1)} all-to-all(bf16[16,32,512]{2,1,0:T(8,128)(2,1)S(1)} %pack.1), channel_id=1, replica_groups=mesh['parts'=2,'chip'=8,'core'=2] {'chip','core'}, dimensions={0} | all-to-all | bytes 1048576 | tf_op jit(solution)/shard_map/all_to_all | solution.py:20
  30.4 0.0 copy-done.23
  30.4 0.0 copy-done.22
  30.4 0.0 copy-done.1
  30.4 0.0 copy-done.3
  30.4 0.0 copy-done.8
  30.4 0.0 copy-done.13
  30.4 4.1 %attend.1._ = bf16[8,4,4096]{2,1,0:T(4,128)(2,1)} custom-call(s32[16]{0:T(128)S(1)} %copy-done.14, s32[16]{0:T(128)S(1)} %copy-done.16, s32[4]{0:T(128)S(1)} %copy-done.22, s32[4]{0:T(128)S(1)} %copy-done.23, bf16[32,4,128]{2,1,0:T(4,128)(2,1)S(1)} %bitcast.19, bf16[4,4,128]{2,1,0:T(4,128)(2,1)S(1)} %bitcast.21, bf16[4,4,128]{2,1,0:T(4,128)(2,1)S(1)} %bitcast.25, ...), custom_call_target="tpu_custom_call" | custom-call | flops 16777216 | bytes 2097152 | tf_op jit(solution)/shard_map/attend/pallas_call | solution.py:323
  34.6 4.1 %all-to-all-start.1 = ((bf16[8,4,4096]{2,1,0:T(4,128)(2,1)}), bf16[8,4,4096]{2,1,0:T(4,128)(2,1)}, u32[]{:S(2)}, u32[]{:S(2)}) async-start(bf16[8,4,4096]{2,1,0:T(4,128)(2,1)} %attend.1._), calls=%async_computation.1 | async-start | bytes 524288 | tf_op jit(solution)/shard_map/all_to_all | solution.py:20
  38.6 0.0 copy-done.10
  38.6 0.0 copy-done.12
  38.7 0.0 copy-done.15
  38.7 0.0 copy-done.17
  38.7 0.0 copy-done.19
  38.7 0.0 copy-done.21
  38.7 2.7 %aside.1 = (bf16[4,256,512]{2,1,0:T(8,128)(2,1)}, bf16[4,256,512]{2,1,0:T(8,128)(2,1)}, bf16[16,48,512]{2,1,0:T(8,128)(2,1)S(1)}, bf16[64,64]{1,0:T(8,128)(2,1)S(1)}) custom-call(s32[16]{0:T(128)S(1)} %copy-done.15, s32[16]{0:T(128)S(1)} %copy-done.17, s32[16]{0:T(128)S(1)} %copy-done.19, s32[16]{0:T(128)S(1)} %copy-done.21, s32[4]{0:T(128)S(1)} %copy-done.22, ...), custom_call_target="tpu_custom_call" | custom-call | bytes 8388608 | tf_op jit(solution)/shard_map/aside/pallas_call | solution.py:344
  41.4 6.6 %all-to-all-done.1 = bf16[8,4,4096]{2,1,0:T(4,128)(2,1)} async-done(((bf16[8,4,4096]{2,1,0:T(4,128)(2,1)}), bf16[8,4,4096]{2,1,0:T(4,128)(2,1)}, u32[]{:S(2)}, u32[]{:S(2)}) %all-to-all-start.1) | async-done | bytes 262176 | tf_op jit(solution)/shard_map/all_to_all | solution.py:20
  48.1 0.0 collective-permute-start
  48.1 1.0 %reshape.48.near = bf16[32,4096]{1,0:T(8,128)(2,1)S(1)} reshape(bf16[8,4,4096]{2,1,0:T(4,128)(2,1)} %all-to-all-done.1) | data formatting | bytes 524288 | tf_op jit(solution)/shard_map/reshape | solution.py:372
  49.1 0.7 collective-permute-done
  49.8 0.1 reshape.49.far
  49.9 0.0 copy-start.4
  49.9 1.6 %copy-done.4 = bf16[4096,256]{1,0:T(8,128)(2,1)S(1)} copy-done((bf16[4096,256]{1,0:T(8,128)(2,1)S(1)}, bf16[4096,256]{1,0:T(8,128)(2,1)}, u32[]{:S(2)}) %copy-start.4) | copy-done | bytes 2097176
  51.5 1.6 %copy-done.5 = bf16[4096,256]{1,0:T(8,128)(2,1)S(1)} copy-done((bf16[4096,256]{1,0:T(8,128)(2,1)S(1)}, bf16[4096,256]{1,0:T(8,128)(2,1)}, u32[]{:S(2)}) %copy-start.5) | copy-done | bytes 2097176
  53.1 1.6 %copy-done.6 = bf16[256,4096]{1,0:T(8,128)(2,1)S(1)} copy-done((bf16[256,4096]{1,0:T(8,128)(2,1)S(1)}, bf16[256,4096]{1,0:T(8,128)(2,1)}, u32[]{:S(2)}) %copy-start.6) | copy-done | bytes 2097176
  54.7 1.4 %ffn.1 = (f32[64,2048]{1,0:T(8,128)S(1)}, bf16[64,2048]{1,0:T(8,128)(2,1)S(1)}) custom-call(bf16[32,4096]{1,0:T(8,128)(2,1)S(1)} %reshape.48.near, bf16[32,4096]{1,0:T(8,128)(2,1)S(1)} %reshape.49.far, bf16[4096,256]{1,0:T(8,128)(2,1)S(1)} %copy-done.4, bf16[4096,256]{1,0:T(8,128)(2,1)S(1)} %copy-done.5, bf16[64,64]{1,0:T(8,128)(2,1)S(1)} %get-tuple-element.16.pick, ...), custom_call_target="tpu_custom_call" | custom-call | flops 402653184 | bytes 6291456 | tf_op jit(solution)/shard_map/ffn/pallas_call | solution.py:363
  56.1 0.0 copy-start.24
  56.1 0.2 collective-permute-start.1
  56.3 1.4 %collective-permute-done.1.theirs = bf16[64,2048]{1,0:T(8,128)(2,1)S(1)} collective-permute-done((bf16[64,2048]{1,0:T(8,128)(2,1)S(1)}, bf16[64,2048]{1,0:T(8,128)(2,1)S(1)}, u32[]{:S(2)}, u32[]{:S(2)}) %collective-permute-start.1) | collective-permute-done | bytes 262176 | tf_op jit(solution)/shard_map/ppermute | solution.py:374
  57.7 0.1 place.1
  57.8 23.8 %all_to_all.16.arrived = bf16[16,48,512]{2,1,0:T(8,128)(2,1)S(1)} all-to-all(bf16[16,48,512]{2,1,0:T(8,128)(2,1)S(1)} %place.1), channel_id=1, replica_groups=mesh['parts'=2,'chip'=8,'core'=2] {'chip','core'}, dimensions={0} | all-to-all | bytes 1572864 | tf_op jit(solution)/shard_map/all_to_all | solution.py:20
  81.6 0.0 copy-done.24
  81.6 2.1 %finish.1 = (bf16[4,4096]{1,0:T(4,128)(2,1)}, bf16[4,16,16,512]{3,2,1,0:T(8,128)(2,1)}, bf16[4,16,16,512]{3,2,1,0:T(8,128)(2,1)}) custom-call(s32[16]{0:T(128)S(1)} %copy-done.19, s32[16]{0:T(128)S(1)} %copy-done.21, s32[16]{0:T(128)S(1)} %copy-done.24, bf16[4,4,128]{2,1,0:T(4,128)(2,1)S(1)} %bitcast.23, ...), custom_call_target="tpu_custom_call", output_to_operand_aliasing={{1}: (6, {}), {2}: (7, {})} | custom-call | bytes 1048576 | tf_op jit(solution)/shard_map/finish/pallas_call | solution.py:387
  (2 shorter events, 0.0 us)
Async XLA Ops:
  0.6 29.8 %copy-start.23 = (s32[4]{0:T(128)S(1)}, s32[4]{0:T(128)}, u32[]{:S(2)}) copy-start(s32[4]{0:T(128)} %unfinished.3) | copy-start | bytes 52
  0.6 29.8 %copy-start.22 = (s32[4]{0:T(128)S(1)}, s32[4]{0:T(128)}, u32[]{:S(2)}) copy-start(s32[4]{0:T(128)} %lengths.3) | copy-start | bytes 52
  0.7 1.2 %copy-start = (bf16[4,256,512]{2,1,0:T(8,128)(2,1)S(1)}, bf16[4,256,512]{2,1,0:T(8,128)(2,1)}, u32[]{:S(2)}) copy-start(bf16[4,256,512]{2,1,0:T(8,128)(2,1)} %ck.3) | copy-start | bytes 3145732
  1.9 1.2 %copy-start.2 = (bf16[4,256,512]{2,1,0:T(8,128)(2,1)S(1)}, bf16[4,256,512]{2,1,0:T(8,128)(2,1)}, u32[]{:S(2)}) copy-start(bf16[4,256,512]{2,1,0:T(8,128)(2,1)} %cv.3) | copy-start | bytes 3145732
  3.1 0.8 copy-start.7
  3.9 0.7 copy-start.9
  4.6 0.7 copy-start.11
  5.2 0.7 copy-start.14
  5.9 0.7 copy-start.16
  6.6 0.7 copy-start.18
  7.2 0.7 copy-start.20
  7.9 22.5 %copy-start.1 = (bf16[4,256,512]{2,1,0:T(8,128)(2,1)S(1)}, bf16[4,256,512]{2,1,0:T(8,128)(2,1)}, u32[]{:S(2)}) copy-start(bf16[4,256,512]{2,1,0:T(8,128)(2,1)} %ck.3) | copy-start | bytes 3145732
  7.9 22.5 %copy-start.3 = (bf16[4,256,512]{2,1,0:T(8,128)(2,1)S(1)}, bf16[4,256,512]{2,1,0:T(8,128)(2,1)}, u32[]{:S(2)}) copy-start(bf16[4,256,512]{2,1,0:T(8,128)(2,1)} %cv.3) | copy-start | bytes 3145732
  7.9 22.6 %copy-start.8 = (bf16[4,4096]{1,0:T(4,128)(2,1)S(1)}, bf16[4,4096]{1,0:T(4,128)(2,1)}, u32[]{:S(2)}) copy-start(bf16[4,4096]{1,0:T(4,128)(2,1)} %param.25) | copy-start | bytes 98308
  7.9 22.6 %copy-start.13 = (f32[4096]{0:T(1024)S(1)}, f32[4096]{0:T(1024)}, u32[]{:S(2)}) copy-start(f32[4096]{0:T(1024)} %param.28) | copy-start | bytes 49156
  8.6 30.1 %copy-start.10 = (bf16[4,512]{1,0:T(4,128)(2,1)S(1)}, bf16[4,512]{1,0:T(4,128)(2,1)}, u32[]{:S(2)}) copy-start(bf16[4,512]{1,0:T(4,128)(2,1)} %param.26) | copy-start | bytes 12292
  8.6 30.1 %copy-start.12 = (bf16[4,512]{1,0:T(4,128)(2,1)S(1)}, bf16[4,512]{1,0:T(4,128)(2,1)}, u32[]{:S(2)}) copy-start(bf16[4,512]{1,0:T(4,128)(2,1)} %param.27) | copy-start | bytes 12292
  8.6 30.1 %copy-start.15 = (s32[16]{0:T(128)S(1)}, s32[16]{0:T(128)}, u32[]{:S(2)}) copy-start(s32[16]{0:T(128)} %send_slot.5) | copy-start | bytes 196
  8.6 30.1 %copy-start.17 = (s32[16]{0:T(128)S(1)}, s32[16]{0:T(128)}, u32[]{:S(2)}) copy-start(s32[16]{0:T(128)} %send_to.5) | copy-start | bytes 196
  8.6 30.1 %copy-start.19 = (s32[16]{0:T(128)S(1)}, s32[16]{0:T(128)}, u32[]{:S(2)}) copy-start(s32[16]{0:T(128)} %receive_from.5) | copy-start | bytes 196
  8.6 30.1 %copy-start.21 = (s32[16]{0:T(128)S(1)}, s32[16]{0:T(128)}, u32[]{:S(2)}) copy-start(s32[16]{0:T(128)} %land_slot.5) | copy-start | bytes 196
  34.6 13.5 %all-to-all-start.1 = ((bf16[8,4,4096]{2,1,0:T(4,128)(2,1)}), bf16[8,4,4096]{2,1,0:T(4,128)(2,1)}, u32[]{:S(2)}, u32[]{:S(2)}) async-start(bf16[8,4,4096]{2,1,0:T(4,128)(2,1)} %attend.1._), calls=%async_computation.1 | async-start | bytes 524288 | tf_op jit(solution)/shard_map/all_to_all | solution.py:20
  48.1 1.7 %collective-permute-start = (bf16[8,4,4096]{2,1,0:T(4,128)(2,1)}, bf16[8,4,4096]{2,1,0:T(4,128)(2,1)S(1)}, u32[]{:S(2)}, u32[]{:S(2)}) collective-permute-start(bf16[8,4,4096]{2,1,0:T(4,128)(2,1)} %all-to-all-done.1), channel_id=1, source_target_pairs={{0,1},{1,0},{2,3},{3,2},{4,5},{5,4},{6,7},{7,6},{8,9},{9,8},{10,11... | collective-permute-start | bytes 786440 | tf_op jit(solution)/shard_map/ppermute | solution.py:362
  49.9 1.6 %copy-start.4 = (bf16[4096,256]{1,0:T(8,128)(2,1)S(1)}, bf16[4096,256]{1,0:T(8,128)(2,1)}, u32[]{:S(2)}) copy-start(bf16[4096,256]{1,0:T(8,128)(2,1)} %gate_weight.1) | copy-start | bytes 6291460
  51.5 1.6 %copy-start.5 = (bf16[4096,256]{1,0:T(8,128)(2,1)S(1)}, bf16[4096,256]{1,0:T(8,128)(2,1)}, u32[]{:S(2)}) copy-start(bf16[4096,256]{1,0:T(8,128)(2,1)} %up_weight.1) | copy-start | bytes 6291460
  53.1 1.6 %copy-start.6 = (bf16[256,4096]{1,0:T(8,128)(2,1)S(1)}, bf16[256,4096]{1,0:T(8,128)(2,1)}, u32[]{:S(2)}) copy-start(bf16[256,4096]{1,0:T(8,128)(2,1)} %down_weight.1) | copy-start | bytes 6291460
  56.1 25.5 %copy-start.24 = (s32[16]{0:T(128)S(1)}, s32[16]{0:T(128)}, u32[]{:S(2)}) copy-start(s32[16]{0:T(128)} %land_length.1) | copy-start | bytes 196
  56.1 1.6 %collective-permute-start.1 = (bf16[64,2048]{1,0:T(8,128)(2,1)S(1)}, bf16[64,2048]{1,0:T(8,128)(2,1)S(1)}, u32[]{:S(2)}, u32[]{:S(2)}) collective-permute-start(bf16[64,2048]{1,0:T(8,128)(2,1)S(1)} %get-tuple-element.18), channel_id=1, source_target_pairs={{0,1},{1,0},{2,3},{3,2},{4,5},{5,4},{6,7},{7,6},{8,9},{9,8},{10,11... | collective-permute-start | bytes 786440 | tf_op jit(solution)/shard_map/ppermute | solution.py:374

commit v4 on v3

--- a/solution.py
+++ b/solution.py
@@ -12,6 +12,7 @@
 HD = 128
 PER = HQ // KVH
 TILE = 16
+CHUNKS = 4
 GROUP = ("chip", "core")
 SMEM, VMEM = pltpu.SMEM, pltpu.VMEM
 
@@ -28,12 +29,28 @@
     return pl.CostEstimate(flops=flops, bytes_accessed=moved, transcendentals=0)
 
 
-def pack_kernel(send_slot, send_to, receive_from, land_slot, q, nk, nv, ck, cv, leaving, packet, sems):
+def pack_kernel(
+    send_slot, send_to, receive_from, land_slot, q, nk, nv, ck, cv, leaving,
+    slot_s, to_s, from_s, land_s, qb, kb, vb, packet, sems
+):
     me = lax.axis_index(GROUP)
     slots = q.shape[1]
-    giving = send_to[me] != me
+    fetches = [
+        pltpu.make_async_copy(a, b, sems.at[2 + i])
+        for i, (a, b) in enumerate(
+            (
+                (send_slot, slot_s), (send_to, to_s), (receive_from, from_s), (land_slot, land_s),
+                (q, qb), (nk, kb), (nv, vb),
+            )
+        )
+    ]
+    for fetch in fetches:
+        fetch.start()
+    for fetch in fetches[:4]:
+        fetch.wait()
+    giving = to_s[me] != me
     copies = [
-        pltpu.make_async_copy(cache.at[send_slot[me]], leaving.at[:, pl.ds(i * TILE, TILE)], sems.at[i])
+        pltpu.make_async_copy(cache.at[slot_s[me]], leaving.at[:, pl.ds(i * TILE, TILE)], sems.at[i])
         for i, cache in enumerate((ck, cv))
     ]
 
@@ -41,25 +58,31 @@
     def _():
         for copy in copies:
             copy.start()
+
+    for fetch in fetches[4:]:
+        fetch.wait()
+
+    @pl.when(giving)
+    def _():
         for copy in copies:
             copy.wait()
 
     @pl.when(jnp.logical_not(giving))
     def _():
-        taken = land_slot[me]
+        taken = land_s[me]
 
         def line(x):
             mine = lax.broadcasted_iota(jnp.int32, (x.shape[0], slots, HD), 1) == taken
             return jnp.sum(jnp.where(mine, x[...].astype(jnp.float32), 0.0), axis=1)
 
-        heads, key, value = line(q), line(nk), line(nv)
+        heads, key, value = line(qb), line(kb), line(vb)
         packet[...] = jnp.zeros_like(packet)
         for k in range(KVH):
             columns = slice(k * HD, (k + 1) * HD)
             packet[0:PER, columns] = heads[k * PER : (k + 1) * PER]
             packet[PER : PER + 1, columns] = key[k : k + 1]
             packet[PER + 1 : PER + 2, columns] = value[k : k + 1]
-        leaving[receive_from[me], 0:TILE] = packet[...].astype(jnp.bfloat16)
+        leaving[from_s[me], 0:TILE] = packet[...].astype(jnp.bfloat16)
 
 
 def put_line(buf, at, base, line, fresh):
@@ -70,98 +93,64 @@
         buf[at, pl.ds(base, TILE), columns] = jnp.where(here, fresh[k], old).astype(jnp.bfloat16)
 
 
-def attend_kernel(
-    send_slot, send_to, lengths, unfinished, q, nk, nv, gain, spread, ck, cv, out,
-    kbuf, vbuf, tile, q32, att, sems, tile_sem
-):
-    me = lax.axis_index(GROUP)
-    slots = ck.shape[0]
-    target, given = send_to[me], send_slot[me]
-    fetch = pltpu.make_async_copy(spread.at[target, pl.ds(0, TILE)], tile, tile_sem)
-    fetch.start()
-    loads = []
-    for j in range(slots):
-        loads.append(
-            (
-                pltpu.make_async_copy(ck.at[j], kbuf.at[j], sems.at[0, j]),
-                pltpu.make_async_copy(cv.at[j], vbuf.at[j], sems.at[1, j]),
+def place_of(length, alive):
+    block = length // TILE
+    return pl.multiple_of(block * TILE, TILE), jnp.where(alive, length - block * TILE, -1)
+
+
+def attend(heads, kbuf, vbuf, at, length, gain):
+    scores = jnp.concatenate(
+        [
+            lax.dot_general(
+                heads[k].astype(jnp.bfloat16),
+                kbuf[at, :, k * HD : (k + 1) * HD],
+                (((1,), (1,)), ((), ())),
+                preferred_element_type=jnp.float32,
             )
-        )
-        for copy in loads[j]:
-            copy.start()
-    q32[...] = q[...].astype(jnp.float32)
-    nk32, nv32 = nk[...].astype(jnp.float32), nv[...].astype(jnp.float32)
-    fetch.wait()
-    packet = tile[...].astype(jnp.float32)
-    scale = 1.0 / math.sqrt(HD)
-    for j in range(slots):
-        moved = (target != me) & (given == j)
-        alive = jnp.where(moved, 1, unfinished[j]) > 0
-        length = lengths[j]
-        block = length // TILE
-        base = pl.multiple_of(block * TILE, TILE)
-        line = jnp.where(alive, length - block * TILE, -1)
-
-        def fresh(row, own):
-            return [
-                jnp.where(moved, packet[row : row + 1, k * HD : (k + 1) * HD], own[k, j : j + 1]) for k in range(KVH)
-            ]
-
-        for copy in loads[j]:
-            copy.wait()
-        put_line(kbuf, j, base, line, fresh(PER, nk32))
-        put_line(vbuf, j, base, line, fresh(PER + 1, nv32))
-        own_heads = q32[:, j, :]
-        scores = jnp.concatenate(
-            [
-                lax.dot_general(
-                    jnp.where(moved, packet[0:PER, k * HD : (k + 1) * HD], own_heads[k * PER : (k + 1) * PER]).astype(
-                        jnp.bfloat16
-                    ),
-                    kbuf[j, :, k * HD : (k + 1) * HD],
-                    (((1,), (1,)), ((), ())),
-                    preferred_element_type=jnp.float32,
-                )
-                for k in range(KVH)
-            ],
-            axis=0,
-        )
-        visible = lax.broadcasted_iota(jnp.int32, scores.shape, 1) <= length
-        scores = jnp.where(visible, scores * scale, jnp.float32(-1e30))
-        expo = jnp.exp(scores - jnp.max(scores, axis=1, keepdims=True))
-        probs = expo / jnp.sum(expo, axis=1, keepdims=True)
-        attended = jnp.concatenate(
-            [
-                jnp.dot(
-                    probs[k * PER : (k + 1) * PER].astype(jnp.bfloat16),
-                    vbuf[j, :, k * HD : (k + 1) * HD],
-                    preferred_element_type=jnp.float32,
-                )
-                for k in range(KVH)
-            ],
-            axis=0,
-        )
-        mean = jnp.sum(attended * attended, keepdims=True) * (1.0 / (HQ * HD))
-        normed = attended * lax.rsqrt(mean + 1e-06) * gain[...]
-        att[:, j, :] = jnp.where(alive, normed, 0.0)
-    for h in range(HQ):
-        head = att[h].astype(jnp.bfloat16)
-        for c in range(out.shape[0]):
-            out[c, :, h * HD : (h + 1) * HD] = head
-
-
-def aside_kernel(
-    send_slot, send_to, receive_from, land_slot, lengths, unfinished, nk, nv, ck, cv, spread, _,
-    keys, values, outgoing, pick, kbuf, vbuf, sems, piece_sem
+            for k in range(KVH)
+        ],
+        axis=0,
+    )
+    visible = lax.broadcasted_iota(jnp.int32, scores.shape, 1) <= length
+    scores = jnp.where(visible, scores * (1.0 / math.sqrt(HD)), jnp.float32(-1e30))
+    expo = jnp.exp(scores - jnp.max(scores, axis=1, keepdims=True))
+    probs = expo / jnp.sum(expo, axis=1, keepdims=True)
+    attended = jnp.concatenate(
+        [
+            jnp.dot(
+                probs[k * PER : (k + 1) * PER].astype(jnp.bfloat16),
+                vbuf[at, :, k * HD : (k + 1) * HD],
+                preferred_element_type=jnp.float32,
+            )
+            for k in range(KVH)
+        ],
+        axis=0,
+    )
+    mean = jnp.sum(attended * attended, keepdims=True) * (1.0 / (HQ * HD))
+    return attended * lax.rsqrt(mean + 1e-06) * gain
+
+
+def local_kernel(
+    send_slot, send_to, receive_from, land_slot, lengths, unfinished, q, nk, nv, gain, ck, cv,
+    att, keys, values, given_row, pick,
+    slot_s, to_s, from_s, land_s, length_s, left_s, qb, kb, vb, gb, q32, kbuf, vbuf, sems, small, big
 ):
     me = lax.axis_index(GROUP)
     core = lax.axis_index("core")
-    slots, n, rows = ck.shape[0], outgoing.shape[0], pick.shape[0]
+    slots, n, rows = ck.shape[0], slot_s.shape[0], pick.shape[0]
     half = rows // 2
     pairs = ((ck, kbuf, keys), (cv, vbuf, values))
-
-    def piece(d):
-        return pltpu.make_async_copy(spread.at[receive_from[d]], outgoing.at[d, pl.ds(0, 2 * TILE)], piece_sem.at[d])
+    fetches = [
+        pltpu.make_async_copy(a, b, small.at[i])
+        for i, (a, b) in enumerate(
+            (
+                (send_slot, slot_s), (send_to, to_s), (receive_from, from_s), (land_slot, land_s),
+                (lengths, length_s), (unfinished, left_s), (q, qb), (nk, kb), (nv, vb), (gain, gb),
+            )
+        )
+    ]
+    for fetch in fetches:
+        fetch.start()
 
     def load(i, j):
         return pltpu.make_async_copy(pairs[i][0].at[j], pairs[i][1].at[j], sems.at[i, j])
@@ -172,53 +161,110 @@
     for j in range(slots):
         for i in range(2):
             load(i, j).start()
-    for d in range(n):
-        pl.when(receive_from[d] != d)(lambda d=d: piece(d).start())
+    for fetch in fetches:
+        fetch.wait()
+    large = [pltpu.make_async_copy(pairs[i][0].at[slot_s[me]], given_row.at[i], big.at[i]) for i in range(2)]
+    for copy in large:
+        copy.start()
     row = lax.broadcasted_iota(jnp.int32, (rows, HD), 0)
     device = row // slots
     wanted = jnp.where((device & 1) == core, 0, half) + (device >> 1) * slots + (row & (slots - 1))
     for d in range(n):
-        source = receive_from[d]
-        held = jnp.where(lax.rem(source, 2) == core, 0, half) + (source // 2) * slots + send_slot[source]
-        landing = jnp.where(source != d, d * slots + land_slot[d], -1)
-        vacated = jnp.where(send_to[d] != d, d * slots + send_slot[d], -1)
+        source = from_s[d]
+        held = jnp.where(lax.rem(source, 2) == core, 0, half) + (source // 2) * slots + slot_s[source]
+        landing = jnp.where(source != d, d * slots + land_s[d], -1)
+        vacated = jnp.where(to_s[d] != d, d * slots + slot_s[d], -1)
         wanted = jnp.where(row == landing, held, wanted)
         wanted = jnp.where(row == vacated, -1, wanted)
     column = lax.broadcasted_iota(jnp.int32, (rows, rows), 1)
     pick[...] = (column == wanted[:, :1]).astype(jnp.float32).astype(jnp.bfloat16)
+    q32[...] = qb[...].astype(jnp.float32)
     for j in range(slots):
-        vacated = (send_to[me] != me) & (send_slot[me] == j)
-        alive = jnp.where(vacated, 0, unfinished[j]) > 0
-        length = lengths[j]
-        block = length // TILE
-        base = pl.multiple_of(block * TILE, TILE)
-        line = jnp.where(alive, length - block * TILE, -1)
-        for i, own in enumerate((nk, nv)):
+        vacated = (to_s[me] != me) & (slot_s[me] == j)
+        alive = jnp.where(vacated, 0, left_s[j]) > 0
+        length = length_s[j]
+        base, line = place_of(length, alive)
+        for i, own in enumerate((kb, vb)):
             load(i, j).wait()
             put_line(pairs[i][1], j, base, line, [own[k, j : j + 1].astype(jnp.float32) for k in range(KVH)])
             store(i, j).start()
-    for d in range(n):
-        pl.when(receive_from[d] != d)(lambda d=d: piece(d).wait())
+        own_heads = q32[:, j, :]
+        normed = attend([own_heads[k * PER : (k + 1) * PER] for k in range(KVH)], kbuf, vbuf, j, length, gb[...])
+        att[:, j, :] = jnp.where(alive, normed, 0.0)
     for j in range(slots):
         for i in range(2):
             store(i, j).wait()
-
-
-def ffn_kernel(near, far, gate_weight, up_weight, pick, down_weight, mine, theirs):
+    for copy in large:
+        copy.wait()
+
+
+def moved_kernel(send_slot, send_to, lengths, gain, att, given_row, spread, out, mine, kv, tile, sem):
+    me = lax.axis_index(GROUP)
+    mine[...] = att[...]
+
+    @pl.when(send_to[me] != me)
+    def _():
+        fetch = pltpu.make_async_copy(spread.at[send_to[me], pl.ds(0, TILE)], tile, sem)
+        fetch.start()
+        kv[...] = given_row[...]
+        slots = mine.shape[1]
+        given = send_slot[me]
+        length = lengths[given]
+        base, line = place_of(length, True)
+        fetch.wait()
+        packet = tile[...].astype(jnp.float32)
+        for i in range(2):
+            put_line(kv, i, base, line, [packet[PER + i : PER + i + 1, k * HD : (k + 1) * HD] for k in range(KVH)])
+        heads = [packet[0:PER, k * HD : (k + 1) * HD] for k in range(KVH)]
+        normed = attend(heads, kv.at[0:1], kv.at[1:2], 0, length, gain[...])
+        for j in range(slots):
+            pl.when(given == j)(lambda j=j: mine.__setitem__((slice(None), j, slice(None)), normed))
+
+    for h in range(HQ):
+        head = mine[h].astype(jnp.bfloat16)
+        for c in range(out.shape[0]):
+            out[c, :, h * HD : (h + 1) * HD] = head
+
+
+def select_kernel(receive_from, spread, _, outgoing, piece_sem):
+    n = outgoing.shape[0]
+
+    def piece(d):
+        return pltpu.make_async_copy(spread.at[receive_from[d]], outgoing.at[d, pl.ds(0, 2 * TILE)], piece_sem.at[d])
+
+    for d in range(n):
+        pl.when(receive_from[d] != d)(lambda d=d: piece(d).start())
+    for d in range(n):
+        pl.when(receive_from[d] != d)(lambda d=d: piece(d).wait())
+
+
+def ffn_kernel(near, far, pick, gate_weight, up_weight, down_weight, mine, theirs, gate_v, up_v, down_v, sems):
     core = lax.axis_index("core")
-    x = jnp.concatenate([near[...], far[...]], axis=0)
-    gate = jnp.dot(x, gate_weight[...], preferred_element_type=jnp.float32)
-    up_part = jnp.dot(x, up_weight[...], preferred_element_type=jnp.float32)
+    width = mine.shape[1]
+    step = gate_v.shape[0] // CHUNKS
+    sides = [pl.ds(pl.multiple_of(side * width, width), width) for side in (1 - core, core)]
+    loads = []
+    for c in range(CHUNKS):
+        at = pl.ds(c * step, step)
+        loads.append(pltpu.make_async_copy(gate_weight.at[at], gate_v.at[at], sems.at[0, c]))
+        loads.append(pltpu.make_async_copy(up_weight.at[at], up_v.at[at], sems.at[1, c]))
+    downs = [pltpu.make_async_copy(down_weight.at[:, at], down_v.at[:, at], sems.at[2, i]) for i, at in enumerate(sides)]
+    for load in loads + downs:
+        load.start()
+    gate = up_part = 0.0
+    for c in range(CHUNKS):
+        at = slice(c * step, (c + 1) * step)
+        x = jnp.concatenate([near[:, at], far[:, at]], axis=0)
+        loads[2 * c].wait()
+        gate += jnp.dot(x, gate_v[at], preferred_element_type=jnp.float32)
+        loads[2 * c + 1].wait()
+        up_part += jnp.dot(x, up_v[at], preferred_element_type=jnp.float32)
     hidden = (gate / (1.0 + jnp.exp(-gate)) * up_part).astype(jnp.bfloat16)
     hidden = jnp.dot(pick[...], hidden, preferred_element_type=jnp.float32).astype(jnp.bfloat16)
-    width = mine.shape[1]
-
-    def down(side):
-        columns = pl.ds(pl.multiple_of(side * width, width), width)
-        return jnp.dot(hidden, down_weight[:, columns], preferred_element_type=jnp.float32)
-
-    theirs[...] = down(1 - core).astype(jnp.bfloat16)
-    mine[...] = down(core)
+    downs[0].wait()
+    theirs[...] = jnp.dot(hidden, down_v[:, sides[0]], preferred_element_type=jnp.float32).astype(jnp.bfloat16)
+    downs[1].wait()
+    mine[...] = jnp.dot(hidden, down_v[:, sides[1]], preferred_element_type=jnp.float32)
 
 
 def place_kernel(mine, theirs, outgoing, out, rows, sem):
@@ -295,10 +341,11 @@
             cache_keys, cache_values, lengths, unfinished, send_slot, send_to, receive_from, land_slot, land_length,
             queries, new_keys, new_values, norm_gain, gate_weight, up_weight, down_weight
         )
-    bf16, f32 = jnp.bfloat16, jnp.float32
+    bf16, f32, i32 = jnp.bfloat16, jnp.float32, jnp.int32
     dma = pltpu.SemaphoreType.DMA
     pieces = (slots, n, TILE, kv_width)
     room = pltpu.CompilerParams(vmem_limit_bytes=16 * 2**20)
+    hbm = spec(pltpu.HBM)
 
     def shape(dims, kind=bf16):
         return jax.ShapeDtypeStruct(dims, kind)
@@ -307,69 +354,90 @@
         return x.reshape(slots, -1, HD).transpose(1, 0, 2)
 
     q, nk, nv = by_head(queries), by_head(new_keys), by_head(new_values)
+    gain = norm_gain.reshape(HQ, HD)
+    tokens = [VMEM(q.shape, bf16), VMEM(nk.shape, bf16), VMEM(nv.shape, bf16)]
     leaving = pl.pallas_call(
         pack_kernel,
         out_shape=shape((n, 2 * TILE, kv_width)),
-        in_specs=[spec(SMEM)] * 4 + [spec(VMEM)] * 3 + [spec(pl.ANY)] * 2,
+        in_specs=[hbm] * 9,
         out_specs=spec(VMEM),
-        scratch_shapes=[VMEM((TILE, kv_width), f32), dma((2,))],
-        compiler_params=room,
+        scratch_shapes=[SMEM((n,), i32)] * 4 + tokens + [VMEM((TILE, kv_width), f32), dma((9,))],
+        compiler_params=pltpu.CompilerParams(vmem_limit_bytes=60 * 2**20),
         cost_estimate=cost(0, 2**20),
         name="pack",
     )(
         send_slot, send_to, receive_from, land_slot, q, nk, nv, cache_keys.reshape(pieces), cache_values.reshape(pieces)
     )
     spread = exchange(leaving, GROUP)
+    att, keys_own, values_own, given_row, pick = pl.pallas_call(
+        local_kernel,
+        out_shape=(
+            shape((HQ, slots, HD), f32),
+            shape(cache_keys.shape),
+            shape(cache_keys.shape),
+            shape((2, capacity, kv_width)),
+            shape((n * slots, n * slots)),
+        ),
+        in_specs=[hbm] * 12,
+        out_specs=(spec(VMEM), hbm, hbm, spec(VMEM), spec(VMEM)),
+        scratch_shapes=[SMEM((n,), i32)] * 4 + [SMEM((slots,), i32)] * 2 + tokens + [
+            VMEM((HQ, HD), f32),
+            VMEM((HQ, slots, HD), f32),
+            VMEM(cache_keys.shape, bf16),
+            VMEM(cache_keys.shape, bf16),
+            dma((2, slots)),
+            dma((10,)),
+            dma((2,)),
+        ],
+        compiler_params=room,
+        cost_estimate=cost(2**24, 2**24),
+        name="local",
+    )(
+        send_slot, send_to, receive_from, land_slot, lengths, unfinished, q, nk, nv, gain, cache_keys, cache_values
+    )
     rows = pl.pallas_call(
-        attend_kernel,
+        moved_kernel,
         out_shape=shape((chips, slots, width)),
-        in_specs=[spec(SMEM)] * 4 + [spec(VMEM)] * 4 + [spec(pl.ANY)] * 3,
+        in_specs=[spec(SMEM)] * 3 + [spec(VMEM)] * 3 + [spec(pl.ANY)],
         out_specs=spec(VMEM),
         scratch_shapes=[
-            VMEM(cache_keys.shape, bf16),
-            VMEM(cache_keys.shape, bf16),
+            VMEM((HQ, slots, HD), f32),
+            VMEM((2, capacity, kv_width), bf16),
             VMEM((TILE, kv_width), bf16),
-            VMEM((HQ, slots, HD), f32),
-            VMEM((HQ, slots, HD), f32),
-            dma((2, slots)),
             dma,
         ],
         compiler_params=room,
-        cost_estimate=cost(2**24, 2**21),
-        name="attend",
-    )(
-        send_slot, send_to, lengths, unfinished, q, nk, nv, norm_gain.reshape(HQ, HD), spread, cache_keys, cache_values
-    )
+        cost_estimate=cost(2**22, 2**20),
+        name="moved",
+    )(send_slot, send_to, lengths, gain, att, given_row, spread)
     near = exchange(rows, "chip")
-    keys_own, values_own, outgoing, pick = pl.pallas_call(
-        aside_kernel,
-        out_shape=(
-            shape(cache_keys.shape),
-            shape(cache_keys.shape),
-            shape((n, 3 * TILE, kv_width)),
-            shape((n * slots, n * slots)),
-        ),
-        in_specs=[spec(SMEM)] * 6 + [spec(VMEM)] * 2 + [spec(pl.ANY)] * 4,
-        out_specs=(spec(pl.ANY), spec(pl.ANY), spec(pl.ANY), spec(VMEM)),
-        scratch_shapes=[VMEM(cache_keys.shape, bf16), VMEM(cache_keys.shape, bf16), dma((2, slots)), dma((n,))],
+    far = lax.ppermute(near, "core", [(0, 1), (1, 0)])
+    outgoing = pl.pallas_call(
+        select_kernel,
+        out_shape=shape((n, 3 * TILE, kv_width)),
+        in_specs=[spec(SMEM)] + [spec(pl.ANY)] * 2,
+        out_specs=spec(pl.ANY),
+        scratch_shapes=[dma((n,))],
         compiler_params=room,
-        cost_estimate=cost(0, 2**23),
-        name="aside",
-    )(
-        send_slot, send_to, receive_from, land_slot, lengths, unfinished, nk, nv, cache_keys, cache_values, spread, rows
-    )
-    near, pick = lax.optimization_barrier((near, pick))
-    far = lax.ppermute(near, "core", [(0, 1), (1, 0)])
+        cost_estimate=cost(0, 2**20),
+        name="select",
+    )(receive_from, spread, near)
     mine, theirs = pl.pallas_call(
         ffn_kernel,
         out_shape=(shape((n * slots, width // 2), f32), shape((n * slots, width // 2))),
-        in_specs=[spec(VMEM)] * 6,
+        in_specs=[spec(VMEM)] * 3 + [hbm] * 3,
         out_specs=(spec(VMEM), spec(VMEM)),
-        compiler_params=room,
+        scratch_shapes=[
+            VMEM(gate_weight.shape, bf16),
+            VMEM(up_weight.shape, bf16),
+            VMEM(down_weight.shape, bf16),
+            dma((3, CHUNKS)),
+        ],
+        compiler_params=pltpu.CompilerParams(vmem_limit_bytes=50 * 2**20),
         cost_estimate=cost(6 * n * slots * width * gate_weight.shape[1], 3 * 2**21),
         name="ffn",
     )(
-        near.reshape(chips * slots, width), far.reshape(chips * slots, width), gate_weight, up_weight, pick, down_weight
+        near.reshape(chips * slots, width), far.reshape(chips * slots, width), pick, gate_weight, up_weight, down_weight
     )
     theirs = lax.ppermute(theirs, "core", [(0, 1), (1, 0)])
     outgoing = pl.pallas_call(

time: 84.1 us -> 72.8 us (0.87)
  the two profiles are of different devices: /device:TPU:0 before, /device:TPU:1 now
where the time goes in v4:
time: 72.8 us; the launch traced here: 72.4 us
  blocking collectives  36.1 us (50%)
  Pallas kernels  13 us (18%)
  waiting for transfers between devices  11.5 us (16%)
  starting transfers between devices  9.76 us (13%)
  local copies, waits for them, and re-layouts  1.14 us (2%)
  between operations  0.91 us (1%)
    all_to_all x2, blocking collectives, exchange(): return lax.all_to_all(blocks, axis, 0, 0, tiled=True)  36.1 us
    all_to_all x1, waiting for transfers between devices, exchange(): return lax.all_to_all(blocks, axis, 0, 0, tiled=True)  10.2 us
    all_to_all x1, starting transfers between devices, exchange(): return lax.all_to_all(blocks, axis, 0, 0, tiled=True)  7.36 us
    pallas_call x1, Pallas kernels, per_device(): pl.pallas_call(local_kernel, out_shape=(shape((HQ, slots, HD), f32), shap...  3.76 us
    pallas_call x1, Pallas kernels, per_device(): pl.pallas_call(ffn_kernel, out_shape=(shape((n * slots, width // 2), f32)...  3.48 us
    pallas_call x1, Pallas kernels, per_device(): pl.pallas_call(finish_kernel, out_shape=(shape((slots, width)), shape(pie...  2.07 us
    ppermute x1, starting transfers between devices, per_device(): far = lax.ppermute(near, 'core', [(0, 1), (1, 0)])  1.96 us
    pallas_call x1, Pallas kernels, per_device(): pl.pallas_call(pack_kernel, out_shape=shape((n, 2 * TILE, kv_width)), in_...  1.84 us
  transfers between devices with their start and end apart: 3, of which 3 were waited for; matrix products, arithmetic and copies ran while one was open for 0% of the time, Pallas kernels for 7%

profile of v4, /device:TPU:1, one launch (start us, length us, event | category | flops | bytes accessed | tf_op | source)
XLA Modules:
  0.0 72.4 jit_solution(13841482982788476573)
XLA Ops:
  0.6 0.0 copy-start.7
  0.6 0.0 copy-start.10
  0.7 0.0 copy-start.9
  0.7 0.0 copy-start.8
  0.7 0.0 copy-start
  0.7 0.0 copy-start.1
  0.7 0.0 copy-start.6
  0.7 0.0 copy-start.5
  0.7 0.0 copy-start.3
  0.7 0.0 copy-start.11
  0.7 0.0 copy-start.4
  0.7 0.0 copy-start.12
  0.8 1.8 %pack.1 = bf16[16,32,512]{2,1,0:T(8,128)(2,1)} custom-call(s32[16]{0:T(128)} %send_slot.5, s32[16]{0:T(128)} %send_to.5, s32[16]{0:T(128)} %receive_from.7, s32[16]{0:T(128)} %land_slot.5, bf16[32,4,128]{2,1,0:T(4,128)(2,1)} %bitcast.18, bf16[4,4,128]{2,1,0:T(4,128)(2,1)} %bitcast.22, bf16[4,4,128]{2,1,0:T(4,128)(2,1)} %bitcast.25, ...), custom_call_target="tpu_custom_call" | custom-call | bytes 1048576 | tf_op jit(solution)/shard_map/pack/pallas_call | solution.py:359
  2.6 7.4 %all-to-all-start = ((bf16[16,32,512]{2,1,0:T(8,128)(2,1)}), bf16[16,32,512]{2,1,0:T(8,128)(2,1)S(1)}, u32[]{:S(2)}, u32[]{:S(2)}) async-start(bf16[16,32,512]{2,1,0:T(8,128)(2,1)} %pack.1), calls=%async_computation | async-start | bytes 1048576 | tf_op jit(solution)/shard_map/all_to_all | solution.py:21
  10.0 0.0 copy-done.7
  10.0 0.0 copy-done.10
  10.0 0.0 copy-done.9
  10.0 0.0 copy-done.8
  10.0 0.0 copy-done
  10.0 0.0 copy-done.1
  10.0 0.0 copy-done.6
  10.0 0.0 copy-done.5
  10.0 0.0 copy-done.3
  10.0 0.0 copy-done.11
  10.1 0.0 copy-done.4
  10.1 0.0 copy-done.12
  10.1 3.8 %local.1 = (f32[32,4,128]{2,1,0:T(4,128)S(1)}, bf16[4,256,512]{2,1,0:T(8,128)(2,1)}, bf16[4,256,512]{2,1,0:T(8,128)(2,1)}, bf16[2,256,512]{2,1,0:T(8,128)(2,1)S(1)}, bf16[64,64]{1,0:T(8,128)(2,1)S(1)}) custom-call(s32[16]{0:T(128)S(1)} %copy-done.8, s32[16]{0:T(128)S(1)} %copy-done.9, s32[16]{0:T(128)S(1)} %copy-done.7, s32[16]{0:T(128)S(1)} %copy-done.10, ...), custom_call_target="tpu_custom_call" | custom-call | flops 16777216 | bytes 16777216 | tf_op jit(solution)/shard_map/local/pallas_call | solution.py:372
  13.8 0.0 copy-start.2
  13.9 10.2 %all-to-all-done.spread = bf16[16,32,512]{2,1,0:T(8,128)(2,1)S(1)} async-done(((bf16[16,32,512]{2,1,0:T(8,128)(2,1)}), bf16[16,32,512]{2,1,0:T(8,128)(2,1)S(1)}, u32[]{:S(2)}, u32[]{:S(2)}) %all-to-all-start) | async-done | bytes 524320 | tf_op jit(solution)/shard_map/all_to_all | solution.py:21
  24.0 0.6 moved.1
  24.7 11.7 %all_to_all.15._ = bf16[8,4,4096]{2,1,0:T(4,128)(2,1)S(1)} all-to-all(bf16[8,4,4096]{2,1,0:T(4,128)(2,1)S(1)} %moved.1), channel_id=1, replica_groups=mesh['parts'=2,'chip'=8,'core'=2] {'chip'}, dimensions={0} | all-to-all | bytes 524288 | tf_op jit(solution)/shard_map/all_to_all | solution.py:21
  36.4 2.0 %collective-permute-start = (bf16[8,4,4096]{2,1,0:T(4,128)(2,1)S(1)}, bf16[8,4,4096]{2,1,0:T(4,128)(2,1)}, u32[]{:S(2)}, u32[]{:S(2)}) collective-permute-start(bf16[8,4,4096]{2,1,0:T(4,128)(2,1)S(1)} %all_to_all.15._), channel_id=1, source_target_pairs={{0,1},{1,0},{2,3},{3,2},{4,5},{5,4},{6,7},{7,6},{8,9},{9,8},{10,11... | collective-permute-start | bytes 786440 | tf_op jit(solution)/shard_map/ppermute | solution.py:414
  38.4 0.1 reshape.48.near
  38.4 1.2 %collective-permute-done = bf16[8,4,4096]{2,1,0:T(4,128)(2,1)} collective-permute-done((bf16[8,4,4096]{2,1,0:T(4,128)(2,1)S(1)}, bf16[8,4,4096]{2,1,0:T(4,128)(2,1)}, u32[]{:S(2)}, u32[]{:S(2)}) %collective-permute-start) | collective-permute-done | bytes 262176 | tf_op jit(solution)/shard_map/ppermute | solution.py:414
  39.7 1.0 %reshape.49.far = bf16[32,4096]{1,0:T(8,128)(2,1)S(1)} reshape(bf16[8,4,4096]{2,1,0:T(4,128)(2,1)} %collective-permute-done) | data formatting | bytes 524288 | tf_op jit(solution)/shard_map/reshape | solution.py:440
  40.7 0.0 copy-done.2
  40.7 3.5 %ffn.1 = (f32[64,2048]{1,0:T(8,128)S(1)}, bf16[64,2048]{1,0:T(8,128)(2,1)S(1)}) custom-call(bf16[32,4096]{1,0:T(8,128)(2,1)S(1)} %reshape.48.near, bf16[32,4096]{1,0:T(8,128)(2,1)S(1)} %reshape.49.far, bf16[64,64]{1,0:T(8,128)(2,1)S(1)} %get-tuple-element.15.pick, bf16[4096,256]{1,0:T(8,128)(2,1)S(1)} %copy-done.2, bf16[4096,256]{1,0:T(8,128)(2,1)} %up_weight.1, ...), custom_call_target="tpu_custom_call" | custom-call | flops 402653184 | bytes 6291456 | tf_op jit(solution)/shard_map/ffn/pallas_call | solution.py:425
  44.2 0.4 collective-permute-start.1
  44.6 1.1 %select.1.outgoing = bf16[16,48,512]{2,1,0:T(8,128)(2,1)S(1)} custom-call(s32[16]{0:T(128)S(1)} %copy-done.7, bf16[16,32,512]{2,1,0:T(8,128)(2,1)S(1)} %all-to-all-done.spread, bf16[8,4,4096]{2,1,0:T(4,128)(2,1)S(1)} %all_to_all.15._), custom_call_target="tpu_custom_call" | custom-call | bytes 1048576 | tf_op jit(solution)/shard_map/select/pallas_call | solution.py:415
  45.7 0.0 copy-start.13
  45.7 0.1 collective-permute-done.1.theirs
  45.8 0.1 place.1
  45.9 24.4 %all_to_all.16.arrived = bf16[16,48,512]{2,1,0:T(8,128)(2,1)S(1)} all-to-all(bf16[16,48,512]{2,1,0:T(8,128)(2,1)S(1)} %place.1), channel_id=1, replica_groups=mesh['parts'=2,'chip'=8,'core'=2] {'chip','core'}, dimensions={0} | all-to-all | bytes 1572864 | tf_op jit(solution)/shard_map/all_to_all | solution.py:21
  70.3 0.0 copy-done.13
  70.3 2.1 %finish.1 = (bf16[4,4096]{1,0:T(4,128)(2,1)}, bf16[4,16,16,512]{3,2,1,0:T(8,128)(2,1)}, bf16[4,16,16,512]{3,2,1,0:T(8,128)(2,1)}) custom-call(s32[16]{0:T(128)S(1)} %copy-done.7, s32[16]{0:T(128)S(1)} %copy-done.10, s32[16]{0:T(128)S(1)} %copy-done.13, bf16[4,4,128]{2,1,0:T(4,128)(2,1)S(1)} %bitcast.24, ...), custom_call_target="tpu_custom_call", output_to_operand_aliasing={{1}: (6, {}), {2}: (7, {})} | custom-call | bytes 1048576 | tf_op jit(solution)/shard_map/finish/pallas_call | solution.py:455
Async XLA Ops:
  0.6 9.3 %copy-start.7 = (s32[16]{0:T(128)S(1)}, s32[16]{0:T(128)}, u32[]{:S(2)}) copy-start(s32[16]{0:T(128)} %receive_from.7) | copy-start | bytes 196
  0.6 9.3 %copy-start.10 = (s32[16]{0:T(128)S(1)}, s32[16]{0:T(128)}, u32[]{:S(2)}) copy-start(s32[16]{0:T(128)} %land_slot.5) | copy-start | bytes 196
  0.7 9.3 %copy-start.9 = (s32[16]{0:T(128)S(1)}, s32[16]{0:T(128)}, u32[]{:S(2)}) copy-start(s32[16]{0:T(128)} %send_to.5) | copy-start | bytes 196
  0.7 9.3 %copy-start.8 = (s32[16]{0:T(128)S(1)}, s32[16]{0:T(128)}, u32[]{:S(2)}) copy-start(s32[16]{0:T(128)} %send_slot.5) | copy-start | bytes 196
  0.7 9.3 %copy-start = (bf16[4,256,512]{2,1,0:T(8,128)(2,1)S(1)}, bf16[4,256,512]{2,1,0:T(8,128)(2,1)}, u32[]{:S(2)}) copy-start(bf16[4,256,512]{2,1,0:T(8,128)(2,1)} %ck.1) | copy-start | bytes 3145732
  0.7 9.3 %copy-start.1 = (bf16[4,256,512]{2,1,0:T(8,128)(2,1)S(1)}, bf16[4,256,512]{2,1,0:T(8,128)(2,1)}, u32[]{:S(2)}) copy-start(bf16[4,256,512]{2,1,0:T(8,128)(2,1)} %cv.1) | copy-start | bytes 3145732
  0.7 9.3 %copy-start.6 = (bf16[4,512]{1,0:T(4,128)(2,1)S(1)}, bf16[4,512]{1,0:T(4,128)(2,1)}, u32[]{:S(2)}) copy-start(bf16[4,512]{1,0:T(4,128)(2,1)} %param.27) | copy-start | bytes 12292
  0.7 9.3 %copy-start.5 = (bf16[4,512]{1,0:T(4,128)(2,1)S(1)}, bf16[4,512]{1,0:T(4,128)(2,1)}, u32[]{:S(2)}) copy-start(bf16[4,512]{1,0:T(4,128)(2,1)} %param.26) | copy-start | bytes 12292
  0.7 9.3 %copy-start.3 = (bf16[4,4096]{1,0:T(4,128)(2,1)S(1)}, bf16[4,4096]{1,0:T(4,128)(2,1)}, u32[]{:S(2)}) copy-start(bf16[4,4096]{1,0:T(4,128)(2,1)} %param.25) | copy-start | bytes 98308
  0.7 9.3 %copy-start.11 = (s32[4]{0:T(128)S(1)}, s32[4]{0:T(128)}, u32[]{:S(2)}) copy-start(s32[4]{0:T(128)} %lengths.3) | copy-start | bytes 52
  0.7 9.3 %copy-start.4 = (f32[4096]{0:T(1024)S(1)}, f32[4096]{0:T(1024)}, u32[]{:S(2)}) copy-start(f32[4096]{0:T(1024)} %param.28) | copy-start | bytes 49156
  0.7 9.3 %copy-start.12 = (s32[4]{0:T(128)S(1)}, s32[4]{0:T(128)}, u32[]{:S(2)}) copy-start(s32[4]{0:T(128)} %unfinished.1) | copy-start | bytes 52
  2.6 21.4 %all-to-all-start = ((bf16[16,32,512]{2,1,0:T(8,128)(2,1)}), bf16[16,32,512]{2,1,0:T(8,128)(2,1)S(1)}, u32[]{:S(2)}, u32[]{:S(2)}) async-start(bf16[16,32,512]{2,1,0:T(8,128)(2,1)} %pack.1), calls=%async_computation | async-start | bytes 1048576 | tf_op jit(solution)/shard_map/all_to_all | solution.py:21
  13.8 26.8 %copy-start.2 = (bf16[4096,256]{1,0:T(8,128)(2,1)S(1)}, bf16[4096,256]{1,0:T(8,128)(2,1)}, u32[]{:S(2)}) copy-start(bf16[4096,256]{1,0:T(8,128)(2,1)} %gate_weight.1) | copy-start | bytes 6291460
  36.4 3.3 %collective-permute-start = (bf16[8,4,4096]{2,1,0:T(4,128)(2,1)S(1)}, bf16[8,4,4096]{2,1,0:T(4,128)(2,1)}, u32[]{:S(2)}, u32[]{:S(2)}) collective-permute-start(bf16[8,4,4096]{2,1,0:T(4,128)(2,1)S(1)} %all_to_all.15._), channel_id=1, source_target_pairs={{0,1},{1,0},{2,3},{3,2},{4,5},{5,4},{6,7},{7,6},{8,9},{9,8},{10,11... | collective-permute-start | bytes 786440 | tf_op jit(solution)/shard_map/ppermute | solution.py:414
  44.2 1.6 %collective-permute-start.1 = (bf16[64,2048]{1,0:T(8,128)(2,1)S(1)}, bf16[64,2048]{1,0:T(8,128)(2,1)S(1)}, u32[]{:S(2)}, u32[]{:S(2)}) collective-permute-start(bf16[64,2048]{1,0:T(8,128)(2,1)S(1)} %get-tuple-element.17), channel_id=1, source_target_pairs={{0,1},{1,0},{2,3},{3,2},{4,5},{5,4},{6,7},{7,6},{8,9},{9,8},{10,11... | collective-permute-start | bytes 786440 | tf_op jit(solution)/shard_map/ppermute | solution.py:442
  45.7 24.7 %copy-start.13 = (s32[16]{0:T(128)S(1)}, s32[16]{0:T(128)}, u32[]{:S(2)}) copy-start(s32[16]{0:T(128)} %land_length.1) | copy-start | bytes 196

commit v5 on v4

--- a/solution.py
+++ b/solution.py
@@ -31,7 +31,7 @@
 
 def pack_kernel(
     send_slot, send_to, receive_from, land_slot, q, nk, nv, ck, cv, leaving,
-    slot_s, to_s, from_s, land_s, qb, kb, vb, packet, sems
+    slot_s, to_s, from_s, land_s, qb, kb, vb, whole, packet, tile, sems
 ):
     me = lax.axis_index(GROUP)
     slots = q.shape[1]
@@ -49,9 +49,9 @@
     for fetch in fetches[:4]:
         fetch.wait()
     giving = to_s[me] != me
-    copies = [
-        pltpu.make_async_copy(cache.at[slot_s[me]], leaving.at[:, pl.ds(i * TILE, TILE)], sems.at[i])
-        for i, cache in enumerate((ck, cv))
+    copies = [pltpu.make_async_copy(cache.at[slot_s[me]], whole.at[i], sems.at[i]) for i, cache in enumerate((ck, cv))]
+    stores = [
+        pltpu.make_async_copy(whole.at[i], leaving.at[:, pl.ds(i * TILE, TILE)], sems.at[9 + i]) for i in range(2)
     ]
 
     @pl.when(giving)
@@ -64,8 +64,11 @@
 
     @pl.when(giving)
     def _():
-        for copy in copies:
+        for copy, store in zip(copies, stores):
             copy.wait()
+            store.start()
+        for store in stores:
+            store.wait()
 
     @pl.when(jnp.logical_not(giving))
     def _():
@@ -82,7 +85,10 @@
             packet[0:PER, columns] = heads[k * PER : (k + 1) * PER]
             packet[PER : PER + 1, columns] = key[k : k + 1]
             packet[PER + 1 : PER + 2, columns] = value[k : k + 1]
-        leaving[from_s[me], 0:TILE] = packet[...].astype(jnp.bfloat16)
+        tile[...] = packet[...].astype(jnp.bfloat16)
+        send = pltpu.make_async_copy(tile, leaving.at[from_s[me], pl.ds(0, TILE)], sems.at[0])
+        send.start()
+        send.wait()
 
 
 def put_line(buf, at, base, line, fresh):
@@ -198,21 +204,18 @@
         copy.wait()
 
 
-def moved_kernel(send_slot, send_to, lengths, gain, att, given_row, spread, out, mine, kv, tile, sem):
+def moved_kernel(send_slot, send_to, lengths, gain, att, given_row, spread, out, mine, kv):
     me = lax.axis_index(GROUP)
     mine[...] = att[...]
 
     @pl.when(send_to[me] != me)
     def _():
-        fetch = pltpu.make_async_copy(spread.at[send_to[me], pl.ds(0, TILE)], tile, sem)
-        fetch.start()
         kv[...] = given_row[...]
         slots = mine.shape[1]
         given = send_slot[me]
         length = lengths[given]
         base, line = place_of(length, True)
-        fetch.wait()
-        packet = tile[...].astype(jnp.float32)
+        packet = spread[send_to[me], 0:TILE].astype(jnp.float32)
         for i in range(2):
             put_line(kv, i, base, line, [packet[PER + i : PER + i + 1, k * HD : (k + 1) * HD] for k in range(KVH)])
         heads = [packet[0:PER, k * HD : (k + 1) * HD] for k in range(KVH)]
@@ -238,26 +241,23 @@
         pl.when(receive_from[d] != d)(lambda d=d: piece(d).wait())
 
 
-def ffn_kernel(near, far, pick, gate_weight, up_weight, down_weight, mine, theirs, gate_v, up_v, down_v, sems):
+def ffn_kernel(near, far, pick, gate_weight, up_weight, down_weight, mine, theirs, up_v, down_v, sems):
     core = lax.axis_index("core")
     width = mine.shape[1]
-    step = gate_v.shape[0] // CHUNKS
+    step = up_v.shape[0] // CHUNKS
     sides = [pl.ds(pl.multiple_of(side * width, width), width) for side in (1 - core, core)]
-    loads = []
-    for c in range(CHUNKS):
-        at = pl.ds(c * step, step)
-        loads.append(pltpu.make_async_copy(gate_weight.at[at], gate_v.at[at], sems.at[0, c]))
-        loads.append(pltpu.make_async_copy(up_weight.at[at], up_v.at[at], sems.at[1, c]))
-    downs = [pltpu.make_async_copy(down_weight.at[:, at], down_v.at[:, at], sems.at[2, i]) for i, at in enumerate(sides)]
-    for load in loads + downs:
+    chunks = [pl.ds(c * step, step) for c in range(CHUNKS)]
+    ups = [pltpu.make_async_copy(up_weight.at[at], up_v.at[at], sems.at[0, c]) for c, at in enumerate(chunks)]
+    downs = [pltpu.make_async_copy(down_weight.at[:, at], down_v.at[:, at], sems.at[1, i]) for i, at in enumerate(sides)]
+    for load in ups + downs:
         load.start()
-    gate = up_part = 0.0
+    x = jnp.concatenate([near[...], far[...]], axis=0)
+    gate = jnp.dot(x, gate_weight[...], preferred_element_type=jnp.float32)
+    up_part = 0.0
     for c in range(CHUNKS):
         at = slice(c * step, (c + 1) * step)
         x = jnp.concatenate([near[:, at], far[:, at]], axis=0)
-        loads[2 * c].wait()
-        gate += jnp.dot(x, gate_v[at], preferred_element_type=jnp.float32)
-        loads[2 * c + 1].wait()
+        ups[c].wait()
         up_part += jnp.dot(x, up_v[at], preferred_element_type=jnp.float32)
     hidden = (gate / (1.0 + jnp.exp(-gate)) * up_part).astype(jnp.bfloat16)
     hidden = jnp.dot(pick[...], hidden, preferred_element_type=jnp.float32).astype(jnp.bfloat16)
@@ -282,51 +282,44 @@
 
 
 def finish_kernel(
-    receive_from, land_slot, land_length, nk, nv, arrived, keys_in, values_in, decoded, keys, values,
-    kbuf, vbuf, sums, sems
+    receive_from, land_slot, land_length, nk, nv, arrived, keys_in, values_in, decoded, keys, values, whole, sems
 ):
     me = lax.axis_index(GROUP)
-    n, wide = sums.shape[0], sums.shape[2]
+    n, wide = arrived.shape[0], arrived.shape[2]
     slots, slot = decoded.shape[0], land_slot[me]
     arriving = receive_from[me] != me
-    bring = pltpu.make_async_copy(arrived.at[:, pl.ds(2 * TILE, TILE)], sums, sems.at[2])
-    bring.start()
-    pairs = ((kbuf, keys, nk), (vbuf, values, nv))
-    loads = [
-        pltpu.make_async_copy(arrived.at[:, pl.ds(i * TILE, TILE)], pairs[i][0].at[0], sems.at[i]) for i in range(2)
-    ]
-    stores = [pltpu.make_async_copy(pairs[i][0].at[0], pairs[i][1].at[slot], sems.at[i]) for i in range(2)]
+    length = land_length[me]
+    block = length // TILE
+    outs = ((keys, nk), (values, nv))
+    stores = [pltpu.make_async_copy(whole.at[i], outs[i][0].at[slot], sems.at[i]) for i in range(2)]
 
     @pl.when(arriving)
     def _():
-        for copy in loads:
-            copy.start()
-        length = land_length[me]
-        block = length // TILE
-        for i, (buf, _, own) in enumerate(pairs):
-            loads[i].wait()
+        here = lax.broadcasted_iota(jnp.int32, (TILE, HD), 0) == length - block * TILE
+        for i in range(2):
+            own = outs[i][1]
             mine = lax.broadcasted_iota(jnp.int32, (KVH, slots, HD), 1) == slot
             token = jnp.sum(jnp.where(mine, own[...].astype(jnp.float32), 0.0), axis=1)
-            here = lax.broadcasted_iota(jnp.int32, (TILE, HD), 0) == length - block * TILE
+            for d in range(n):
+                whole[i, d] = arrived[d, i * TILE : (i + 1) * TILE]
             for k in range(KVH):
                 columns = slice(k * HD, (k + 1) * HD)
-                old = buf[0, block, :, columns].astype(jnp.float32)
-                buf[0, block, :, columns] = jnp.where(here, token[k : k + 1], old).astype(jnp.bfloat16)
+                old = arrived[block, i * TILE : (i + 1) * TILE, columns].astype(jnp.float32)
+                whole[i, block, :, columns] = jnp.where(here, token[k : k + 1], old).astype(jnp.bfloat16)
             stores[i].start()
 
-    bring.wait()
     for side in range(2):
-        total = sums[side].astype(jnp.float32)
+        total = arrived[side, 2 * TILE : 3 * TILE].astype(jnp.float32)
         for c in range(1, n // 2):
-            total += sums[2 * c + side].astype(jnp.float32)
+            total += arrived[2 * c + side, 2 * TILE : 3 * TILE].astype(jnp.float32)
         for g in range(TILE // slots):
             at = (side * (TILE // slots) + g) * wide
             decoded[:, at : at + wide] = total[g * slots : (g + 1) * slots].astype(jnp.bfloat16)
 
     @pl.when(arriving)
     def _():
-        for copy in stores:
-            copy.wait()
+        for store in stores:
+            store.wait()
 
 
 def per_device(
@@ -360,8 +353,10 @@
         pack_kernel,
         out_shape=shape((n, 2 * TILE, kv_width)),
         in_specs=[hbm] * 9,
-        out_specs=spec(VMEM),
-        scratch_shapes=[SMEM((n,), i32)] * 4 + tokens + [VMEM((TILE, kv_width), f32), dma((9,))],
+        out_specs=hbm,
+        scratch_shapes=[SMEM((n,), i32)] * 4 + tokens + [
+            VMEM((2, n, TILE, kv_width), bf16), VMEM((TILE, kv_width), f32), VMEM((TILE, kv_width), bf16), dma((11,))
+        ],
         compiler_params=pltpu.CompilerParams(vmem_limit_bytes=60 * 2**20),
         cost_estimate=cost(0, 2**20),
         name="pack",
@@ -398,19 +393,15 @@
     rows = pl.pallas_call(
         moved_kernel,
         out_shape=shape((chips, slots, width)),
-        in_specs=[spec(SMEM)] * 3 + [spec(VMEM)] * 3 + [spec(pl.ANY)],
+        in_specs=[spec(SMEM)] * 3 + [spec(VMEM)] * 4,
         out_specs=spec(VMEM),
-        scratch_shapes=[
-            VMEM((HQ, slots, HD), f32),
-            VMEM((2, capacity, kv_width), bf16),
-            VMEM((TILE, kv_width), bf16),
-            dma,
-        ],
+        scratch_shapes=[VMEM((HQ, slots, HD), f32), VMEM((2, capacity, kv_width), bf16)],
         compiler_params=room,
         cost_estimate=cost(2**22, 2**20),
         name="moved",
     )(send_slot, send_to, lengths, gain, att, given_row, spread)
     near = exchange(rows, "chip")
+    near = near.reshape(chips * slots, width)
     far = lax.ppermute(near, "core", [(0, 1), (1, 0)])
     outgoing = pl.pallas_call(
         select_kernel,
@@ -422,22 +413,22 @@
         cost_estimate=cost(0, 2**20),
         name="select",
     )(receive_from, spread, near)
+    far, outgoing = lax.optimization_barrier((far, outgoing))
     mine, theirs = pl.pallas_call(
         ffn_kernel,
         out_shape=(shape((n * slots, width // 2), f32), shape((n * slots, width // 2))),
-        in_specs=[spec(VMEM)] * 3 + [hbm] * 3,
+        in_specs=[spec(VMEM)] * 4 + [hbm] * 2,
         out_specs=(spec(VMEM), spec(VMEM)),
         scratch_shapes=[
-            VMEM(gate_weight.shape, bf16),
             VMEM(up_weight.shape, bf16),
             VMEM(down_weight.shape, bf16),
-            dma((3, CHUNKS)),
+            dma((2, CHUNKS)),
         ],
         compiler_params=pltpu.CompilerParams(vmem_limit_bytes=50 * 2**20),
         cost_estimate=cost(6 * n * slots * width * gate_weight.shape[1], 3 * 2**21),
         name="ffn",
     )(
-        near.reshape(chips * slots, width), far.reshape(chips * slots, width), pick, gate_weight, up_weight, down_weight
+        near, far, pick, gate_weight, up_weight, down_weight
     )
     theirs = lax.ppermute(theirs, "core", [(0, 1), (1, 0)])
     outgoing = pl.pallas_call(
@@ -455,14 +446,9 @@
     decoded, keys_after, values_after = pl.pallas_call(
         finish_kernel,
         out_shape=(shape((slots, width)), shape(pieces), shape(pieces)),
-        in_specs=[spec(SMEM)] * 3 + [spec(VMEM)] * 2 + [spec(pl.ANY)] * 3,
+        in_specs=[spec(SMEM)] * 3 + [spec(VMEM)] * 3 + [spec(pl.ANY)] * 2,
         out_specs=(spec(VMEM), spec(pl.ANY), spec(pl.ANY)),
-        scratch_shapes=[
-            VMEM((1, n, TILE, kv_width), bf16),
-            VMEM((1, n, TILE, kv_width), bf16),
-            VMEM((n, TILE, kv_width), bf16),
-            dma((3,)),
-        ],
+        scratch_shapes=[VMEM((2, n, TILE, kv_width), bf16), dma((2,))],
         input_output_aliases={6: 1, 7: 2},
         compiler_params=room,
         cost_estimate=cost(0, 2**20),

time: 72.8 us -> 71.8 us (0.986)
  the two profiles are of different devices: /device:TPU:1 before, /device:TPU:0 now
where the time goes in v5:
time: 71.8 us; the launch traced here: 71.2 us
  blocking collectives  37.6 us (52%)
  waiting for transfers between devices  12.4 us (17%)
  Pallas kernels  11.4 us (16%)
  starting transfers between devices  8.7 us (12%)
  between operations  0.91 us (1%)
    all_to_all x2, blocking collectives, exchange(): return lax.all_to_all(blocks, axis, 0, 0, tiled=True)  37.6 us
    all_to_all x1, waiting for transfers between devices, exchange(): return lax.all_to_all(blocks, axis, 0, 0, tiled=True)  10.6 us
    all_to_all x1, starting transfers between devices, exchange(): return lax.all_to_all(blocks, axis, 0, 0, tiled=True)  8.42 us
    pallas_call x1, Pallas kernels, per_device(): pl.pallas_call(local_kernel, out_shape=(shape((HQ, slots, HD), f32), shap...  3.76 us
    pallas_call x1, Pallas kernels, per_device(): pl.pallas_call(ffn_kernel, out_shape=(shape((n * slots, width // 2), f32)...  2.9 us
    pallas_call x1, Pallas kernels, per_device(): pl.pallas_call(pack_kernel, out_shape=shape((n, 2 * TILE, kv_width)), in_...  1.66 us
  transfers between devices with their start and end apart: 3, of which 3 were waited for; matrix products, arithmetic and copies ran while one was open for 0% of the time, Pallas kernels for 7%

profile of v5, /device:TPU:0, one launch (start us, length us, event | category | flops | bytes accessed | tf_op | source)
XLA Modules:
  0.0 71.2 jit_solution(4537159008401280216)
XLA Ops:
  0.6 0.0 copy-start.7
  0.6 0.0 copy-start.10
  0.7 0.0 copy-start.9
  0.7 0.0 copy-start.8
  0.7 0.0 copy-start
  0.7 0.0 copy-start.1
  0.7 0.0 copy-start.6
  0.7 0.0 copy-start.5
  0.7 0.0 copy-start.3
  0.7 0.0 copy-start.11
  0.7 0.0 copy-start.4
  0.7 0.0 copy-start.12
  0.8 1.7 %pack.1 = bf16[16,32,512]{2,1,0:T(8,128)(2,1)} custom-call(s32[16]{0:T(128)} %send_slot.5, s32[16]{0:T(128)} %send_to.5, s32[16]{0:T(128)} %receive_from.7, s32[16]{0:T(128)} %land_slot.5, bf16[32,4,128]{2,1,0:T(4,128)(2,1)} %bitcast.18, bf16[4,4,128]{2,1,0:T(4,128)(2,1)} %bitcast.22, bf16[4,4,128]{2,1,0:T(4,128)(2,1)} %bitcast.25, ...), custom_call_target="tpu_custom_call" | custom-call | bytes 1048576 | tf_op jit(solution)/shard_map/pack/pallas_call | solution.py:352
  2.4 8.4 %all-to-all-start = ((bf16[16,32,512]{2,1,0:T(8,128)(2,1)}), bf16[16,32,512]{2,1,0:T(8,128)(2,1)S(1)}, u32[]{:S(2)}, u32[]{:S(2)}) async-start(bf16[16,32,512]{2,1,0:T(8,128)(2,1)} %pack.1), calls=%async_computation | async-start | bytes 1048576 | tf_op jit(solution)/shard_map/all_to_all | solution.py:21
  10.9 0.0 copy-done.7
  10.9 0.0 copy-done.10
  10.9 0.0 copy-done.9
  10.9 0.0 copy-done.8
  10.9 0.0 copy-done
  10.9 0.0 copy-done.1
  10.9 0.0 copy-done.6
  10.9 0.0 copy-done.5
  10.9 0.0 copy-done.3
  10.9 0.0 copy-done.11
  11.0 0.0 copy-done.4
  11.0 0.0 copy-done.12
  11.0 3.8 %local.1 = (f32[32,4,128]{2,1,0:T(4,128)S(1)}, bf16[4,256,512]{2,1,0:T(8,128)(2,1)}, bf16[4,256,512]{2,1,0:T(8,128)(2,1)}, bf16[2,256,512]{2,1,0:T(8,128)(2,1)S(1)}, bf16[64,64]{1,0:T(8,128)(2,1)S(1)}) custom-call(s32[16]{0:T(128)S(1)} %copy-done.8, s32[16]{0:T(128)S(1)} %copy-done.9, s32[16]{0:T(128)S(1)} %copy-done.7, s32[16]{0:T(128)S(1)} %copy-done.10, ...), custom_call_target="tpu_custom_call" | custom-call | flops 16777216 | bytes 16777216 | tf_op jit(solution)/shard_map/local/pallas_call | solution.py:367
  14.7 0.0 copy-start.2
  14.7 10.6 %all-to-all-done.spread = bf16[16,32,512]{2,1,0:T(8,128)(2,1)S(1)} async-done(((bf16[16,32,512]{2,1,0:T(8,128)(2,1)}), bf16[16,32,512]{2,1,0:T(8,128)(2,1)S(1)}, u32[]{:S(2)}, u32[]{:S(2)}) %all-to-all-start) | async-done | bytes 524320 | tf_op jit(solution)/shard_map/all_to_all | solution.py:21
  25.3 0.6 moved.1
  26.0 13.8 %all_to_all.15 = bf16[8,4,4096]{2,1,0:T(4,128)(2,1)S(1)} all-to-all(bf16[8,4,4096]{2,1,0:T(4,128)(2,1)S(1)} %moved.1), channel_id=1, replica_groups=mesh['parts'=2,'chip'=8,'core'=2] {'chip'}, dimensions={0} | all-to-all | bytes 524288 | tf_op jit(solution)/shard_map/all_to_all | solution.py:21
  39.8 0.1 reshape.45._.near
  39.9 0.1 collective-permute-start
  39.9 1.1 %select.1.outgoing = bf16[16,48,512]{2,1,0:T(8,128)(2,1)S(1)} custom-call(s32[16]{0:T(128)S(1)} %copy-done.7, bf16[16,32,512]{2,1,0:T(8,128)(2,1)S(1)} %all-to-all-done.spread, bf16[32,4096]{1,0:T(8,128)(2,1)S(1)} %reshape.45._.near), custom_call_target="tpu_custom_call" | custom-call | bytes 1048576 | tf_op jit(solution)/shard_map/select/pallas_call | solution.py:406
  41.0 0.5 collective-permute-done.far
  41.5 0.0 copy-done.2
  41.5 2.9 %ffn.1 = (f32[64,2048]{1,0:T(8,128)S(1)}, bf16[64,2048]{1,0:T(8,128)(2,1)S(1)}) custom-call(bf16[32,4096]{1,0:T(8,128)(2,1)S(1)} %reshape.45._.near, bf16[32,4096]{1,0:T(8,128)(2,1)S(1)} %collective-permute-done.far, bf16[64,64]{1,0:T(8,128)(2,1)S(1)} %get-tuple-element.18.pick, bf16[4096,256]{1,0:T(8,128)(2,1)S(1)} %copy-done.2, ...), custom_call_target="tpu_custom_call" | custom-call | flops 402653184 | bytes 6291456 | tf_op jit(solution)/shard_map/ffn/pallas_call | solution.py:417
  44.4 0.0 copy-start.13
  44.4 0.2 collective-permute-start.1
  44.6 1.4 %collective-permute-done.1.theirs = bf16[64,2048]{1,0:T(8,128)(2,1)S(1)} collective-permute-done((bf16[64,2048]{1,0:T(8,128)(2,1)S(1)}, bf16[64,2048]{1,0:T(8,128)(2,1)S(1)}, u32[]{:S(2)}, u32[]{:S(2)}) %collective-permute-start.1) | collective-permute-done | bytes 262176 | tf_op jit(solution)/shard_map/ppermute | solution.py:433
  46.0 0.1 place.1
  46.1 23.8 %all_to_all.16.arrived = bf16[16,48,512]{2,1,0:T(8,128)(2,1)S(1)} all-to-all(bf16[16,48,512]{2,1,0:T(8,128)(2,1)S(1)} %place.1), channel_id=1, replica_groups=mesh['parts'=2,'chip'=8,'core'=2] {'chip','core'}, dimensions={0} | all-to-all | bytes 1572864 | tf_op jit(solution)/shard_map/all_to_all | solution.py:21
  69.9 0.0 copy-done.13
  69.9 1.2 %finish.1 = (bf16[4,4096]{1,0:T(4,128)(2,1)}, bf16[4,16,16,512]{3,2,1,0:T(8,128)(2,1)}, bf16[4,16,16,512]{3,2,1,0:T(8,128)(2,1)}) custom-call(s32[16]{0:T(128)S(1)} %copy-done.7, s32[16]{0:T(128)S(1)} %copy-done.10, s32[16]{0:T(128)S(1)} %copy-done.13, bf16[4,4,128]{2,1,0:T(4,128)(2,1)S(1)} %bitcast.24, ...), custom_call_target="tpu_custom_call", output_to_operand_aliasing={{1}: (6, {}), {2}: (7, {})} | custom-call | bytes 1048576 | tf_op jit(solution)/shard_map/finish/pallas_call | solution.py:446
Async XLA Ops:
  0.6 10.2 %copy-start.7 = (s32[16]{0:T(128)S(1)}, s32[16]{0:T(128)}, u32[]{:S(2)}) copy-start(s32[16]{0:T(128)} %receive_from.7) | copy-start | bytes 196
  0.6 10.2 %copy-start.10 = (s32[16]{0:T(128)S(1)}, s32[16]{0:T(128)}, u32[]{:S(2)}) copy-start(s32[16]{0:T(128)} %land_slot.5) | copy-start | bytes 196
  0.7 10.2 %copy-start.9 = (s32[16]{0:T(128)S(1)}, s32[16]{0:T(128)}, u32[]{:S(2)}) copy-start(s32[16]{0:T(128)} %send_to.5) | copy-start | bytes 196
  0.7 10.2 %copy-start.8 = (s32[16]{0:T(128)S(1)}, s32[16]{0:T(128)}, u32[]{:S(2)}) copy-start(s32[16]{0:T(128)} %send_slot.5) | copy-start | bytes 196
  0.7 10.2 %copy-start = (bf16[4,256,512]{2,1,0:T(8,128)(2,1)S(1)}, bf16[4,256,512]{2,1,0:T(8,128)(2,1)}, u32[]{:S(2)}) copy-start(bf16[4,256,512]{2,1,0:T(8,128)(2,1)} %ck.1) | copy-start | bytes 3145732
  0.7 10.2 %copy-start.1 = (bf16[4,256,512]{2,1,0:T(8,128)(2,1)S(1)}, bf16[4,256,512]{2,1,0:T(8,128)(2,1)}, u32[]{:S(2)}) copy-start(bf16[4,256,512]{2,1,0:T(8,128)(2,1)} %cv.1) | copy-start | bytes 3145732
  0.7 10.2 %copy-start.6 = (bf16[4,512]{1,0:T(4,128)(2,1)S(1)}, bf16[4,512]{1,0:T(4,128)(2,1)}, u32[]{:S(2)}) copy-start(bf16[4,512]{1,0:T(4,128)(2,1)} %param.27) | copy-start | bytes 12292
  0.7 10.2 %copy-start.5 = (bf16[4,512]{1,0:T(4,128)(2,1)S(1)}, bf16[4,512]{1,0:T(4,128)(2,1)}, u32[]{:S(2)}) copy-start(bf16[4,512]{1,0:T(4,128)(2,1)} %param.26) | copy-start | bytes 12292
  0.7 10.2 %copy-start.3 = (bf16[4,4096]{1,0:T(4,128)(2,1)S(1)}, bf16[4,4096]{1,0:T(4,128)(2,1)}, u32[]{:S(2)}) copy-start(bf16[4,4096]{1,0:T(4,128)(2,1)} %param.25) | copy-start | bytes 98308
  0.7 10.2 %copy-start.11 = (s32[4]{0:T(128)S(1)}, s32[4]{0:T(128)}, u32[]{:S(2)}) copy-start(s32[4]{0:T(128)} %lengths.3) | copy-start | bytes 52
  0.7 10.2 %copy-start.4 = (f32[4096]{0:T(1024)S(1)}, f32[4096]{0:T(1024)}, u32[]{:S(2)}) copy-start(f32[4096]{0:T(1024)} %param.28) | copy-start | bytes 49156
  0.7 10.2 %copy-start.12 = (s32[4]{0:T(128)S(1)}, s32[4]{0:T(128)}, u32[]{:S(2)}) copy-start(s32[4]{0:T(128)} %unfinished.1) | copy-start | bytes 52
  2.4 22.9 %all-to-all-start = ((bf16[16,32,512]{2,1,0:T(8,128)(2,1)}), bf16[16,32,512]{2,1,0:T(8,128)(2,1)S(1)}, u32[]{:S(2)}, u32[]{:S(2)}) async-start(bf16[16,32,512]{2,1,0:T(8,128)(2,1)} %pack.1), calls=%async_computation | async-start | bytes 1048576 | tf_op jit(solution)/shard_map/all_to_all | solution.py:21
  14.7 26.7 %copy-start.2 = (bf16[4096,256]{1,0:T(8,128)(2,1)S(1)}, bf16[4096,256]{1,0:T(8,128)(2,1)}, u32[]{:S(2)}) copy-start(bf16[4096,256]{1,0:T(8,128)(2,1)} %gate_weight.1) | copy-start | bytes 6291460
  39.9 1.6 %collective-permute-start = (bf16[32,4096]{1,0:T(8,128)(2,1)S(1)}, bf16[32,4096]{1,0:T(8,128)(2,1)S(1)}, u32[]{:S(2)}, u32[]{:S(2)}) collective-permute-start(bf16[32,4096]{1,0:T(8,128)(2,1)S(1)} %reshape.45._.near), channel_id=1, source_target_pairs={{0,1},{1,0},{2,3},{3,2},{4,5},{5,4},{6,7},{7,6},{8,9},{9,8},{10,11... | collective-permute-start | bytes 786440 | tf_op jit(solution)/shard_map/ppermute | solution.py:405
  44.4 25.5 %copy-start.13 = (s32[16]{0:T(128)S(1)}, s32[16]{0:T(128)}, u32[]{:S(2)}) copy-start(s32[16]{0:T(128)} %land_length.1) | copy-start | bytes 196
  44.4 1.6 %collective-permute-start.1 = (bf16[64,2048]{1,0:T(8,128)(2,1)S(1)}, bf16[64,2048]{1,0:T(8,128)(2,1)S(1)}, u32[]{:S(2)}, u32[]{:S(2)}) collective-permute-start(bf16[64,2048]{1,0:T(8,128)(2,1)S(1)} %get-tuple-element.20), channel_id=1, source_target_pairs={{0,1},{1,0},{2,3},{3,2},{4,5},{5,4},{6,7},{7,6},{8,9},{9,8},{10,11... | collective-permute-start | bytes 786440 | tf_op jit(solution)/shard_map/ppermute | solution.py:433

commit v6 on v5

--- a/solution.py
+++ b/solution.py
@@ -46,27 +46,22 @@
     ]
     for fetch in fetches:
         fetch.start()
-    for fetch in fetches[:4]:
+    loads = [pltpu.make_async_copy(cache, whole.at[i], sems.at[i]) for i, cache in enumerate((ck, cv))]
+    for load in loads:
+        load.start()
+    for fetch in fetches:
         fetch.wait()
     giving = to_s[me] != me
-    copies = [pltpu.make_async_copy(cache.at[slot_s[me]], whole.at[i], sems.at[i]) for i, cache in enumerate((ck, cv))]
     stores = [
-        pltpu.make_async_copy(whole.at[i], leaving.at[:, pl.ds(i * TILE, TILE)], sems.at[9 + i]) for i in range(2)
+        pltpu.make_async_copy(whole.at[i, slot_s[me]], leaving.at[:, pl.ds(i * TILE, TILE)], sems.at[9 + i]) for i in range(2)
     ]
+
+    for load, store in zip(loads, stores):
+        load.wait()
+        pl.when(giving)(store.start)
 
     @pl.when(giving)
     def _():
-        for copy in copies:
-            copy.start()
-
-    for fetch in fetches[4:]:
-        fetch.wait()
-
-    @pl.when(giving)
-    def _():
-        for copy, store in zip(copies, stores):
-            copy.wait()
-            store.start()
         for store in stores:
             store.wait()
 
@@ -104,7 +99,7 @@
     return pl.multiple_of(block * TILE, TILE), jnp.where(alive, length - block * TILE, -1)
 
 
-def attend(heads, kbuf, vbuf, at, length, gain):
+def attend(heads, kbuf, vbuf, at, length, gain, token=None):
     scores = jnp.concatenate(
         [
             lax.dot_general(
@@ -117,21 +112,28 @@
         ],
         axis=0,
     )
-    visible = lax.broadcasted_iota(jnp.int32, scores.shape, 1) <= length
-    scores = jnp.where(visible, scores * (1.0 / math.sqrt(HD)), jnp.float32(-1e30))
+    position = lax.broadcasted_iota(jnp.int32, scores.shape, 1)
+    if token is not None:
+        fresh = [jnp.sum(heads[k] * token[0][k], axis=1, keepdims=True) for k in range(KVH)]
+        scores = jnp.where(position == length, jnp.concatenate(fresh, axis=0), scores)
+    scores = jnp.where(position <= length, scores * (1.0 / math.sqrt(HD)), jnp.float32(-1e30))
     expo = jnp.exp(scores - jnp.max(scores, axis=1, keepdims=True))
     probs = expo / jnp.sum(expo, axis=1, keepdims=True)
-    attended = jnp.concatenate(
-        [
-            jnp.dot(
-                probs[k * PER : (k + 1) * PER].astype(jnp.bfloat16),
-                vbuf[at, :, k * HD : (k + 1) * HD],
-                preferred_element_type=jnp.float32,
-            )
-            for k in range(KVH)
-        ],
-        axis=0,
-    )
+    if token is not None:
+        last = jnp.sum(jnp.where(position == length, probs, 0.0), axis=1, keepdims=True)
+        last = last.astype(jnp.bfloat16).astype(jnp.float32)
+        probs = jnp.where(position == length, 0.0, probs)
+    parts = [
+        jnp.dot(
+            probs[k * PER : (k + 1) * PER].astype(jnp.bfloat16),
+            vbuf[at, :, k * HD : (k + 1) * HD],
+            preferred_element_type=jnp.float32,
+        )
+        for k in range(KVH)
+    ]
+    if token is not None:
+        parts = [parts[k] + last[k * PER : (k + 1) * PER] * token[1][k] for k in range(KVH)]
+    attended = jnp.concatenate(parts, axis=0)
     mean = jnp.sum(attended * attended, keepdims=True) * (1.0 / (HQ * HD))
     return attended * lax.rsqrt(mean + 1e-06) * gain
 
@@ -204,22 +206,22 @@
         copy.wait()
 
 
-def moved_kernel(send_slot, send_to, lengths, gain, att, given_row, spread, out, mine, kv):
+def moved_kernel(send_slot, send_to, lengths, gain, att, given_row, spread, out, mine):
     me = lax.axis_index(GROUP)
     mine[...] = att[...]
 
     @pl.when(send_to[me] != me)
     def _():
-        kv[...] = given_row[...]
         slots = mine.shape[1]
         given = send_slot[me]
-        length = lengths[given]
-        base, line = place_of(length, True)
         packet = spread[send_to[me], 0:TILE].astype(jnp.float32)
-        for i in range(2):
-            put_line(kv, i, base, line, [packet[PER + i : PER + i + 1, k * HD : (k + 1) * HD] for k in range(KVH)])
-        heads = [packet[0:PER, k * HD : (k + 1) * HD] for k in range(KVH)]
-        normed = attend(heads, kv.at[0:1], kv.at[1:2], 0, length, gain[...])
+
+        def by_head(first, last):
+            return [packet[first:last, k * HD : (k + 1) * HD] for k in range(KVH)]
+
+        token = (by_head(PER, PER + 1), by_head(PER + 1, PER + 2))
+        rows = (given_row.at[0:1], given_row.at[1:2])
+        normed = attend(by_head(0, PER), *rows, 0, lengths[given], gain[...], token)
         for j in range(slots):
             pl.when(given == j)(lambda j=j: mine.__setitem__((slice(None), j, slice(None)), normed))
 
@@ -241,15 +243,14 @@
         pl.when(receive_from[d] != d)(lambda d=d: piece(d).wait())
 
 
-def ffn_kernel(near, far, pick, gate_weight, up_weight, down_weight, mine, theirs, up_v, down_v, sems):
-    core = lax.axis_index("core")
-    width = mine.shape[1]
+def ffn_kernel(near, far, pick, gate_weight, up_weight, down_weight, hidden, theirs, up_v, down_v, sems):
+    width = theirs.shape[1]
     step = up_v.shape[0] // CHUNKS
-    sides = [pl.ds(pl.multiple_of(side * width, width), width) for side in (1 - core, core)]
+    side = pl.ds(pl.multiple_of((1 - lax.axis_index("core")) * width, width), width)
     chunks = [pl.ds(c * step, step) for c in range(CHUNKS)]
-    ups = [pltpu.make_async_copy(up_weight.at[at], up_v.at[at], sems.at[0, c]) for c, at in enumerate(chunks)]
-    downs = [pltpu.make_async_copy(down_weight.at[:, at], down_v.at[:, at], sems.at[1, i]) for i, at in enumerate(sides)]
-    for load in ups + downs:
+    ups = [pltpu.make_async_copy(up_weight.at[at], up_v.at[at], sems.at[c]) for c, at in enumerate(chunks)]
+    down = pltpu.make_async_copy(down_weight.at[:, side], down_v, sems.at[CHUNKS])
+    for load in ups + [down]:
         load.start()
     x = jnp.concatenate([near[...], far[...]], axis=0)
     gate = jnp.dot(x, gate_weight[...], preferred_element_type=jnp.float32)
@@ -259,12 +260,20 @@
         x = jnp.concatenate([near[:, at], far[:, at]], axis=0)
         ups[c].wait()
         up_part += jnp.dot(x, up_v[at], preferred_element_type=jnp.float32)
-    hidden = (gate / (1.0 + jnp.exp(-gate)) * up_part).astype(jnp.bfloat16)
-    hidden = jnp.dot(pick[...], hidden, preferred_element_type=jnp.float32).astype(jnp.bfloat16)
-    downs[0].wait()
-    theirs[...] = jnp.dot(hidden, down_v[:, sides[0]], preferred_element_type=jnp.float32).astype(jnp.bfloat16)
-    downs[1].wait()
-    mine[...] = jnp.dot(hidden, down_v[:, sides[1]], preferred_element_type=jnp.float32)
+    placed = (gate / (1.0 + jnp.exp(-gate)) * up_part).astype(jnp.bfloat16)
+    placed = jnp.dot(pick[...], placed, preferred_element_type=jnp.float32).astype(jnp.bfloat16)
+    hidden[...] = placed
+    down.wait()
+    theirs[...] = jnp.dot(placed, down_v[...], preferred_element_type=jnp.float32).astype(jnp.bfloat16)
+
+
+def own_half_kernel(hidden, down_weight, mine, down_v, sem):
+    width = mine.shape[1]
+    side = pl.ds(pl.multiple_of(lax.axis_index("core") * width, width), width)
+    down = pltpu.make_async_copy(down_weight.at[:, side], down_v, sem)
+    down.start()
+    down.wait()
+    mine[...] = jnp.dot(hidden[...], down_v[...], preferred_element_type=jnp.float32)
 
 
 def place_kernel(mine, theirs, outgoing, out, rows, sem):
@@ -282,7 +291,7 @@
 
 
 def finish_kernel(
-    receive_from, land_slot, land_length, nk, nv, arrived, keys_in, values_in, decoded, keys, values, whole, sems
+    receive_from, land_slot, land_length, nk, nv, arrived, keys_in, values_in, decoded, keys, values, whole, sums, sems
 ):
     me = lax.axis_index(GROUP)
     n, wide = arrived.shape[0], arrived.shape[2]
@@ -314,12 +323,16 @@
             total += arrived[2 * c + side, 2 * TILE : 3 * TILE].astype(jnp.float32)
         for g in range(TILE // slots):
             at = (side * (TILE // slots) + g) * wide
-            decoded[:, at : at + wide] = total[g * slots : (g + 1) * slots].astype(jnp.bfloat16)
+            sums[:, at : at + wide] = total[g * slots : (g + 1) * slots].astype(jnp.bfloat16)
+    finished = pltpu.make_async_copy(sums, decoded, sems.at[2])
+    finished.start()
 
     @pl.when(arriving)
     def _():
         for store in stores:
             store.wait()
+
+    finished.wait()
 
 
 def per_device(
@@ -355,7 +368,7 @@
         in_specs=[hbm] * 9,
         out_specs=hbm,
         scratch_shapes=[SMEM((n,), i32)] * 4 + tokens + [
-            VMEM((2, n, TILE, kv_width), bf16), VMEM((TILE, kv_width), f32), VMEM((TILE, kv_width), bf16), dma((11,))
+            VMEM((2,) + pieces, bf16), VMEM((TILE, kv_width), f32), VMEM((TILE, kv_width), bf16), dma((11,))
         ],
         compiler_params=pltpu.CompilerParams(vmem_limit_bytes=60 * 2**20),
         cost_estimate=cost(0, 2**20),
@@ -395,7 +408,7 @@
         out_shape=shape((chips, slots, width)),
         in_specs=[spec(SMEM)] * 3 + [spec(VMEM)] * 4,
         out_specs=spec(VMEM),
-        scratch_shapes=[VMEM((HQ, slots, HD), f32), VMEM((2, capacity, kv_width), bf16)],
+        scratch_shapes=[VMEM((HQ, slots, HD), f32)],
         compiler_params=room,
         cost_estimate=cost(2**22, 2**20),
         name="moved",
@@ -414,22 +427,27 @@
         name="select",
     )(receive_from, spread, near)
     far, outgoing = lax.optimization_barrier((far, outgoing))
-    mine, theirs = pl.pallas_call(
+    units = gate_weight.shape[1]
+    hidden, theirs = pl.pallas_call(
         ffn_kernel,
-        out_shape=(shape((n * slots, width // 2), f32), shape((n * slots, width // 2))),
+        out_shape=(shape((n * slots, units)), shape((n * slots, width // 2))),
         in_specs=[spec(VMEM)] * 4 + [hbm] * 2,
         out_specs=(spec(VMEM), spec(VMEM)),
-        scratch_shapes=[
-            VMEM(up_weight.shape, bf16),
-            VMEM(down_weight.shape, bf16),
-            dma((2, CHUNKS)),
-        ],
+        scratch_shapes=[VMEM(up_weight.shape, bf16), VMEM((units, width // 2), bf16), dma((CHUNKS + 1,))],
         compiler_params=pltpu.CompilerParams(vmem_limit_bytes=50 * 2**20),
-        cost_estimate=cost(6 * n * slots * width * gate_weight.shape[1], 3 * 2**21),
+        cost_estimate=cost(5 * n * slots * width * units, 3 * 2**21),
         name="ffn",
-    )(
-        near, far, pick, gate_weight, up_weight, down_weight
-    )
+    )(near, far, pick, gate_weight, up_weight, down_weight)
+    mine = pl.pallas_call(
+        own_half_kernel,
+        out_shape=shape((n * slots, width // 2), f32),
+        in_specs=[spec(VMEM), hbm],
+        out_specs=spec(VMEM),
+        scratch_shapes=[VMEM((units, width // 2), bf16), dma],
+        compiler_params=pltpu.CompilerParams(vmem_limit_bytes=52 * 2**20),
+        cost_estimate=cost(n * slots * width * units, 2**20),
+        name="own_half",
+    )(hidden, down_weight)
     theirs = lax.ppermute(theirs, "core", [(0, 1), (1, 0)])
     outgoing = pl.pallas_call(
         place_kernel,
@@ -447,8 +465,8 @@
         finish_kernel,
         out_shape=(shape((slots, width)), shape(pieces), shape(pieces)),
         in_specs=[spec(SMEM)] * 3 + [spec(VMEM)] * 3 + [spec(pl.ANY)] * 2,
-        out_specs=(spec(VMEM), spec(pl.ANY), spec(pl.ANY)),
-        scratch_shapes=[VMEM((2, n, TILE, kv_width), bf16), dma((2,))],
+        out_specs=(hbm, spec(pl.ANY), spec(pl.ANY)),
+        scratch_shapes=[VMEM((2, n, TILE, kv_width), bf16), VMEM((slots, width), bf16), dma((3,))],
         input_output_aliases={6: 1, 7: 2},
         compiler_params=room,
         cost_estimate=cost(0, 2**20),

time: 71.8 us -> 70.8 us (0.986)
  Pallas kernels: 11.4 us -> 13.4 us
  waiting for transfers between devices: 12.4 us -> 11 us
  starting transfers between devices: 8.7 us -> 7.67 us
    ppermute x1, waiting for transfers between devices: 1.4 us -> 0.01 us  [per_device(): theirs = lax.ppermute(theirs, 'core', [(0, 1), (1, 0)])]
    pallas_call x1 -> x2, Pallas kernels: 2.9 us -> 4.1 us  [the longest x1 2.57 us: per_device(): pl.pallas_call(ffn_kernel, out_shape=(shape((n * slots, units)), shape((n...]
    all_to_all x1, starting transfers between devices: 8.42 us -> 7.39 us  [exchange(): return lax.all_to_all(blocks, axis, 0, 0, tiled=True)]
    pallas_call x1, Pallas kernels: 1.66 us -> 2.46 us  [per_device(): pl.pallas_call(pack_kernel, out_shape=shape((n, 2 * TILE, kv_width)), in_...]
  transfers between devices with their start and end apart: 3 -> 3, of which waited for: 3 -> 2; matrix products, arithmetic and copies ran while one was open for 0% -> 0% of each run, Pallas kernels for 7% -> 9%
where the time goes in v6:
time: 70.8 us; the launch traced here: 70.1 us
  blocking collectives  36.9 us (52%)
  Pallas kernels  13.4 us (19%)
  waiting for transfers between devices  11 us (16%)
  starting transfers between devices  7.67 us (11%)
  between operations  0.93 us (1%)
    all_to_all x2, blocking collectives, exchange(): return lax.all_to_all(blocks, axis, 0, 0, tiled=True)  36.9 us
    all_to_all x1, waiting for transfers between devices, exchange(): return lax.all_to_all(blocks, axis, 0, 0, tiled=True)  10.6 us
    all_to_all x1, starting transfers between devices, exchange(): return lax.all_to_all(blocks, axis, 0, 0, tiled=True)  7.39 us
    pallas_call x1, Pallas kernels, per_device(): pl.pallas_call(local_kernel, out_shape=(shape((HQ, slots, HD), f32), shap...  3.76 us
    pallas_call x1, Pallas kernels, per_device(): pl.pallas_call(ffn_kernel, out_shape=(shape((n * slots, units)), shape((n...  2.57 us
    pallas_call x1, Pallas kernels, per_device(): pl.pallas_call(pack_kernel, out_shape=shape((n, 2 * TILE, kv_width)), in_...  2.46 us
    pallas_call x1, Pallas kernels, per_device(): pl.pallas_call(own_half_kernel, out_shape=shape((n * slots, width // 2),...  1.53 us
  transfers between devices with their start and end apart: 3, of which 2 were waited for; matrix products, arithmetic and copies ran while one was open for 0% of the time, Pallas kernels for 9%

profile of v6, /device:TPU:0, one launch (start us, length us, event | category | flops | bytes accessed | tf_op | source)
XLA Modules:
  0.0 70.1 jit_solution(902234791868281915)
XLA Ops:
  0.6 0.0 copy-start.7
  0.6 0.0 copy-start.10
  0.7 0.0 copy-start.9
  0.7 0.0 copy-start.8
  0.7 0.0 copy-start
  0.7 0.0 copy-start.1
  0.7 0.0 copy-start.6
  0.7 0.0 copy-start.5
  0.7 0.0 copy-start.3
  0.7 0.0 copy-start.11
  0.7 0.0 copy-start.4
  0.7 0.0 copy-start.12
  0.8 2.5 %pack.1 = bf16[16,32,512]{2,1,0:T(8,128)(2,1)} custom-call(s32[16]{0:T(128)} %send_slot.5, s32[16]{0:T(128)} %send_to.5, s32[16]{0:T(128)} %receive_from.7, s32[16]{0:T(128)} %land_slot.5, bf16[32,4,128]{2,1,0:T(4,128)(2,1)} %bitcast.18, bf16[4,4,128]{2,1,0:T(4,128)(2,1)} %bitcast.22, bf16[4,4,128]{2,1,0:T(4,128)(2,1)} %bitcast.25, ...), custom_call_target="tpu_custom_call" | custom-call | bytes 1048576 | tf_op jit(solution)/shard_map/pack/pallas_call | solution.py:365
  3.2 7.4 %all-to-all-start = ((bf16[16,32,512]{2,1,0:T(8,128)(2,1)}), bf16[16,32,512]{2,1,0:T(8,128)(2,1)S(1)}, u32[]{:S(2)}, u32[]{:S(2)}) async-start(bf16[16,32,512]{2,1,0:T(8,128)(2,1)} %pack.1), calls=%async_computation | async-start | bytes 1048576 | tf_op jit(solution)/shard_map/all_to_all | solution.py:21
  10.6 0.0 copy-done.7
  10.6 0.0 copy-done.10
  10.6 0.0 copy-done.9
  10.7 0.0 copy-done.8
  10.7 0.0 copy-done
  10.7 0.0 copy-done.1
  10.7 0.0 copy-done.6
  10.7 0.0 copy-done.5
  10.7 0.0 copy-done.3
  10.7 0.0 copy-done.11
  10.7 0.0 copy-done.4
  10.7 0.0 copy-done.12
  10.7 3.8 %local.1 = (f32[32,4,128]{2,1,0:T(4,128)S(1)}, bf16[4,256,512]{2,1,0:T(8,128)(2,1)}, bf16[4,256,512]{2,1,0:T(8,128)(2,1)}, bf16[2,256,512]{2,1,0:T(8,128)(2,1)S(1)}, bf16[64,64]{1,0:T(8,128)(2,1)S(1)}) custom-call(s32[16]{0:T(128)S(1)} %copy-done.8, s32[16]{0:T(128)S(1)} %copy-done.9, s32[16]{0:T(128)S(1)} %copy-done.7, s32[16]{0:T(128)S(1)} %copy-done.10, ...), custom_call_target="tpu_custom_call" | custom-call | flops 16777216 | bytes 16777216 | tf_op jit(solution)/shard_map/local/pallas_call | solution.py:380
  14.5 0.0 copy-start.2
  14.5 10.6 %all-to-all-done.spread = bf16[16,32,512]{2,1,0:T(8,128)(2,1)S(1)} async-done(((bf16[16,32,512]{2,1,0:T(8,128)(2,1)}), bf16[16,32,512]{2,1,0:T(8,128)(2,1)S(1)}, u32[]{:S(2)}, u32[]{:S(2)}) %all-to-all-start) | async-done | bytes 524320 | tf_op jit(solution)/shard_map/all_to_all | solution.py:21
  25.1 0.6 moved.1
  25.7 13.2 %all_to_all.15 = bf16[8,4,4096]{2,1,0:T(4,128)(2,1)S(1)} all-to-all(bf16[8,4,4096]{2,1,0:T(4,128)(2,1)S(1)} %moved.1), channel_id=1, replica_groups=mesh['parts'=2,'chip'=8,'core'=2] {'chip'}, dimensions={0} | all-to-all | bytes 524288 | tf_op jit(solution)/shard_map/all_to_all | solution.py:21
  38.9 0.1 reshape.45._.near
  39.0 0.1 collective-permute-start
  39.1 1.1 %select.1.outgoing = bf16[16,48,512]{2,1,0:T(8,128)(2,1)S(1)} custom-call(s32[16]{0:T(128)S(1)} %copy-done.7, bf16[16,32,512]{2,1,0:T(8,128)(2,1)S(1)} %all-to-all-done.spread, bf16[32,4096]{1,0:T(8,128)(2,1)S(1)} %reshape.45._.near), custom_call_target="tpu_custom_call" | custom-call | bytes 1048576 | tf_op jit(solution)/shard_map/select/pallas_call | solution.py:419
  40.1 0.5 collective-permute-done.far
  40.6 0.0 copy-done.2
  40.6 2.6 %ffn.1 = (bf16[64,256]{1,0:T(8,128)(2,1)S(1)}, bf16[64,2048]{1,0:T(8,128)(2,1)S(1)}) custom-call(bf16[32,4096]{1,0:T(8,128)(2,1)S(1)} %reshape.45._.near, bf16[32,4096]{1,0:T(8,128)(2,1)S(1)} %collective-permute-done.far, bf16[64,64]{1,0:T(8,128)(2,1)S(1)} %get-tuple-element.18.pick, bf16[4096,256]{1,0:T(8,128)(2,1)S(1)} %copy-done.2, ...), custom_call_target="tpu_custom_call" | custom-call | flops 335544320 | bytes 6291456 | tf_op jit(solution)/shard_map/ffn/pallas_call | solution.py:431
  43.2 0.2 collective-permute-start.1
  43.4 1.5 %own_half.1.mine = f32[64,2048]{1,0:T(8,128)S(1)} custom-call(bf16[64,256]{1,0:T(8,128)(2,1)S(1)} %get-tuple-element.19.hidden, bf16[256,4096]{1,0:T(8,128)(2,1)} %down_weight.3), custom_call_target="tpu_custom_call" | custom-call | flops 67108864 | bytes 1048576 | tf_op jit(solution)/shard_map/own_half/pallas_call | solution.py:441
  44.9 0.0 copy-start.13
  44.9 0.0 collective-permute-done.1.theirs
  44.9 0.1 place.1
  45.1 23.8 %all_to_all.16.arrived = bf16[16,48,512]{2,1,0:T(8,128)(2,1)S(1)} all-to-all(bf16[16,48,512]{2,1,0:T(8,128)(2,1)S(1)} %place.1), channel_id=1, replica_groups=mesh['parts'=2,'chip'=8,'core'=2] {'chip','core'}, dimensions={0} | all-to-all | bytes 1572864 | tf_op jit(solution)/shard_map/all_to_all | solution.py:21
  68.9 0.0 copy-done.13
  68.9 1.3 %finish.1 = (bf16[4,4096]{1,0:T(4,128)(2,1)}, bf16[4,16,16,512]{3,2,1,0:T(8,128)(2,1)}, bf16[4,16,16,512]{3,2,1,0:T(8,128)(2,1)}) custom-call(s32[16]{0:T(128)S(1)} %copy-done.7, s32[16]{0:T(128)S(1)} %copy-done.10, s32[16]{0:T(128)S(1)} %copy-done.13, bf16[4,4,128]{2,1,0:T(4,128)(2,1)S(1)} %bitcast.24, ...), custom_call_target="tpu_custom_call", output_to_operand_aliasing={{1}: (6, {}), {2}: (7, {})} | custom-call | bytes 1048576 | tf_op jit(solution)/shard_map/finish/pallas_call | solution.py:464
Async XLA Ops:
  0.6 10.0 %copy-start.7 = (s32[16]{0:T(128)S(1)}, s32[16]{0:T(128)}, u32[]{:S(2)}) copy-start(s32[16]{0:T(128)} %receive_from.7) | copy-start | bytes 196
  0.6 10.0 %copy-start.10 = (s32[16]{0:T(128)S(1)}, s32[16]{0:T(128)}, u32[]{:S(2)}) copy-start(s32[16]{0:T(128)} %land_slot.5) | copy-start | bytes 196
  0.7 10.0 %copy-start.9 = (s32[16]{0:T(128)S(1)}, s32[16]{0:T(128)}, u32[]{:S(2)}) copy-start(s32[16]{0:T(128)} %send_to.5) | copy-start | bytes 196
  0.7 10.0 %copy-start.8 = (s32[16]{0:T(128)S(1)}, s32[16]{0:T(128)}, u32[]{:S(2)}) copy-start(s32[16]{0:T(128)} %send_slot.5) | copy-start | bytes 196
  0.7 10.0 %copy-start = (bf16[4,256,512]{2,1,0:T(8,128)(2,1)S(1)}, bf16[4,256,512]{2,1,0:T(8,128)(2,1)}, u32[]{:S(2)}) copy-start(bf16[4,256,512]{2,1,0:T(8,128)(2,1)} %ck.1) | copy-start | bytes 3145732
  0.7 10.0 %copy-start.1 = (bf16[4,256,512]{2,1,0:T(8,128)(2,1)S(1)}, bf16[4,256,512]{2,1,0:T(8,128)(2,1)}, u32[]{:S(2)}) copy-start(bf16[4,256,512]{2,1,0:T(8,128)(2,1)} %cv.1) | copy-start | bytes 3145732
  0.7 10.0 %copy-start.6 = (bf16[4,512]{1,0:T(4,128)(2,1)S(1)}, bf16[4,512]{1,0:T(4,128)(2,1)}, u32[]{:S(2)}) copy-start(bf16[4,512]{1,0:T(4,128)(2,1)} %param.27) | copy-start | bytes 12292
  0.7 10.0 %copy-start.5 = (bf16[4,512]{1,0:T(4,128)(2,1)S(1)}, bf16[4,512]{1,0:T(4,128)(2,1)}, u32[]{:S(2)}) copy-start(bf16[4,512]{1,0:T(4,128)(2,1)} %param.26) | copy-start | bytes 12292
  0.7 10.0 %copy-start.3 = (bf16[4,4096]{1,0:T(4,128)(2,1)S(1)}, bf16[4,4096]{1,0:T(4,128)(2,1)}, u32[]{:S(2)}) copy-start(bf16[4,4096]{1,0:T(4,128)(2,1)} %param.25) | copy-start | bytes 98308
  0.7 10.0 %copy-start.11 = (s32[4]{0:T(128)S(1)}, s32[4]{0:T(128)}, u32[]{:S(2)}) copy-start(s32[4]{0:T(128)} %lengths.3) | copy-start | bytes 52
  0.7 10.0 %copy-start.4 = (f32[4096]{0:T(1024)S(1)}, f32[4096]{0:T(1024)}, u32[]{:S(2)}) copy-start(f32[4096]{0:T(1024)} %param.28) | copy-start | bytes 49156
  0.7 10.0 %copy-start.12 = (s32[4]{0:T(128)S(1)}, s32[4]{0:T(128)}, u32[]{:S(2)}) copy-start(s32[4]{0:T(128)} %unfinished.1) | copy-start | bytes 52
  3.2 21.9 %all-to-all-start = ((bf16[16,32,512]{2,1,0:T(8,128)(2,1)}), bf16[16,32,512]{2,1,0:T(8,128)(2,1)S(1)}, u32[]{:S(2)}, u32[]{:S(2)}) async-start(bf16[16,32,512]{2,1,0:T(8,128)(2,1)} %pack.1), calls=%async_computation | async-start | bytes 1048576 | tf_op jit(solution)/shard_map/all_to_all | solution.py:21
  14.5 26.1 %copy-start.2 = (bf16[4096,256]{1,0:T(8,128)(2,1)S(1)}, bf16[4096,256]{1,0:T(8,128)(2,1)}, u32[]{:S(2)}) copy-start(bf16[4096,256]{1,0:T(8,128)(2,1)} %gate_weight.1) | copy-start | bytes 6291460
  39.0 1.6 %collective-permute-start = (bf16[32,4096]{1,0:T(8,128)(2,1)S(1)}, bf16[32,4096]{1,0:T(8,128)(2,1)S(1)}, u32[]{:S(2)}, u32[]{:S(2)}) collective-permute-start(bf16[32,4096]{1,0:T(8,128)(2,1)S(1)} %reshape.45._.near), channel_id=1, source_target_pairs={{0,1},{1,0},{2,3},{3,2},{4,5},{5,4},{6,7},{7,6},{8,9},{9,8},{10,11... | collective-permute-start | bytes 786440 | tf_op jit(solution)/shard_map/ppermute | solution.py:418
  43.2 1.8 %collective-permute-start.1 = (bf16[64,2048]{1,0:T(8,128)(2,1)S(1)}, bf16[64,2048]{1,0:T(8,128)(2,1)S(1)}, u32[]{:S(2)}, u32[]{:S(2)}) collective-permute-start(bf16[64,2048]{1,0:T(8,128)(2,1)S(1)} %get-tuple-element.20), channel_id=1, source_target_pairs={{0,1},{1,0},{2,3},{3,2},{4,5},{5,4},{6,7},{7,6},{8,9},{9,8},{10,11... | collective-permute-start | bytes 786440 | tf_op jit(solution)/shard_map/ppermute | solution.py:451
  44.9 24.0 %copy-start.13 = (s32[16]{0:T(128)S(1)}, s32[16]{0:T(128)}, u32[]{:S(2)}) copy-start(s32[16]{0:T(128)} %land_length.1) | copy-start | bytes 196

commit v7 on v6

--- a/solution.py
+++ b/solution.py
@@ -12,7 +12,7 @@
 HD = 128
 PER = HQ // KVH
 TILE = 16
-CHUNKS = 4
+CHUNKS = 2
 GROUP = ("chip", "core")
 SMEM, VMEM = pltpu.SMEM, pltpu.VMEM
 
@@ -231,35 +231,41 @@
             out[c, :, h * HD : (h + 1) * HD] = head
 
 
-def select_kernel(receive_from, spread, _, outgoing, piece_sem):
+def select_kernel(receive_from, spread, up_weight, _, outgoing, up_v, piece_sem, sem):
     n = outgoing.shape[0]
+    up = pltpu.make_async_copy(up_weight.at[pl.ds(0, up_v.shape[0])], up_v, sem)
 
     def piece(d):
         return pltpu.make_async_copy(spread.at[receive_from[d]], outgoing.at[d, pl.ds(0, 2 * TILE)], piece_sem.at[d])
 
+    up.start()
     for d in range(n):
         pl.when(receive_from[d] != d)(lambda d=d: piece(d).start())
     for d in range(n):
         pl.when(receive_from[d] != d)(lambda d=d: piece(d).wait())
-
-
-def ffn_kernel(near, far, pick, gate_weight, up_weight, down_weight, hidden, theirs, up_v, down_v, sems):
+    up.wait()
+
+
+def ffn_kernel(near, far, pick, gate_weight, first_up, up_weight, down_weight, hidden, theirs, up_v, down_v, sems):
     width = theirs.shape[1]
+    first = first_up.shape[0]
     step = up_v.shape[0] // CHUNKS
     side = pl.ds(pl.multiple_of((1 - lax.axis_index("core")) * width, width), width)
     chunks = [pl.ds(c * step, step) for c in range(CHUNKS)]
-    ups = [pltpu.make_async_copy(up_weight.at[at], up_v.at[at], sems.at[c]) for c, at in enumerate(chunks)]
+    ups = [
+        pltpu.make_async_copy(up_weight.at[pl.ds(first + c * step, step)], up_v.at[at], sems.at[c])
+        for c, at in enumerate(chunks)
+    ]
     down = pltpu.make_async_copy(down_weight.at[:, side], down_v, sems.at[CHUNKS])
     for load in ups + [down]:
         load.start()
     x = jnp.concatenate([near[...], far[...]], axis=0)
     gate = jnp.dot(x, gate_weight[...], preferred_element_type=jnp.float32)
-    up_part = 0.0
+    up_part = jnp.dot(x[:, :first], first_up[...], preferred_element_type=jnp.float32)
     for c in range(CHUNKS):
-        at = slice(c * step, (c + 1) * step)
-        x = jnp.concatenate([near[:, at], far[:, at]], axis=0)
+        at = slice(first + c * step, first + (c + 1) * step)
         ups[c].wait()
-        up_part += jnp.dot(x, up_v[at], preferred_element_type=jnp.float32)
+        up_part += jnp.dot(x[:, at], up_v[chunks[c]], preferred_element_type=jnp.float32)
     placed = (gate / (1.0 + jnp.exp(-gate)) * up_part).astype(jnp.bfloat16)
     placed = jnp.dot(pick[...], placed, preferred_element_type=jnp.float32).astype(jnp.bfloat16)
     hidden[...] = placed
@@ -397,7 +403,7 @@
             dma((10,)),
             dma((2,)),
         ],
-        compiler_params=room,
+        compiler_params=pltpu.CompilerParams(vmem_limit_bytes=52 * 2**20),
         cost_estimate=cost(2**24, 2**24),
         name="local",
     )(
@@ -416,28 +422,28 @@
     near = exchange(rows, "chip")
     near = near.reshape(chips * slots, width)
     far = lax.ppermute(near, "core", [(0, 1), (1, 0)])
-    outgoing = pl.pallas_call(
+    units = gate_weight.shape[1]
+    outgoing, up_v = pl.pallas_call(
         select_kernel,
-        out_shape=shape((n, 3 * TILE, kv_width)),
-        in_specs=[spec(SMEM)] + [spec(pl.ANY)] * 2,
-        out_specs=spec(pl.ANY),
-        scratch_shapes=[dma((n,))],
+        out_shape=(shape((n, 3 * TILE, kv_width)), shape((width // 2, units))),
+        in_specs=[spec(SMEM), spec(pl.ANY), hbm, spec(pl.ANY)],
+        out_specs=(spec(pl.ANY), spec(VMEM)),
+        scratch_shapes=[dma((n,)), dma],
         compiler_params=room,
         cost_estimate=cost(0, 2**20),
         name="select",
-    )(receive_from, spread, near)
+    )(receive_from, spread, up_weight, near)
     far, outgoing = lax.optimization_barrier((far, outgoing))
-    units = gate_weight.shape[1]
     hidden, theirs = pl.pallas_call(
         ffn_kernel,
         out_shape=(shape((n * slots, units)), shape((n * slots, width // 2))),
-        in_specs=[spec(VMEM)] * 4 + [hbm] * 2,
+        in_specs=[spec(VMEM)] * 5 + [hbm] * 2,
         out_specs=(spec(VMEM), spec(VMEM)),
-        scratch_shapes=[VMEM(up_weight.shape, bf16), VMEM((units, width // 2), bf16), dma((CHUNKS + 1,))],
+        scratch_shapes=[VMEM((width // 2, units), bf16), VMEM((units, width // 2), bf16), dma((CHUNKS + 1,))],
         compiler_params=pltpu.CompilerParams(vmem_limit_bytes=50 * 2**20),
         cost_estimate=cost(5 * n * slots * width * units, 3 * 2**21),
         name="ffn",
-    )(near, far, pick, gate_weight, up_weight, down_weight)
+    )(near, far, pick, gate_weight, up_v, up_weight, down_weight)
     mine = pl.pallas_call(
         own_half_kernel,
         out_shape=shape((n * slots, width // 2), f32),

time: 70.8 us -> 70.7 us (level)
  waiting for transfers between devices: 11 us -> 9.41 us
  local copies, waits for them, and re-layouts: 0.13 us -> 1.34 us
    all_to_all x1, waiting for transfers between devices: 10.6 us -> 9.04 us  [exchange(): return lax.all_to_all(blocks, axis, 0, 0, tiled=True)]
    unnamed x28, local copies, waits for them, and re-layouts: 0.06 us -> 1.28 us
  transfers between devices with their start and end apart: 3 -> 3, of which waited for: 2 -> 2; matrix products, arithmetic and copies ran while one was open for 0% -> 0% of each run, Pallas kernels for 9% -> 10%
where the time goes in v7:
time: 70.7 us; the launch traced here: 69.9 us
  blocking collectives  37 us (52%)
  Pallas kernels  13.6 us (19%)
  waiting for transfers between devices  9.41 us (13%)
  starting transfers between devices  7.67 us (11%)
  local copies, waits for them, and re-layouts  1.34 us (2%)
  between operations  0.91 us (1%)
    all_to_all x2, blocking collectives, exchange(): return lax.all_to_all(blocks, axis, 0, 0, tiled=True)  37 us
    all_to_all x1, waiting for transfers between devices, exchange(): return lax.all_to_all(blocks, axis, 0, 0, tiled=True)  9.04 us
    all_to_all x1, starting transfers between devices, exchange(): return lax.all_to_all(blocks, axis, 0, 0, tiled=True)  7.39 us
    pallas_call x1, Pallas kernels, per_device(): pl.pallas_call(local_kernel, out_shape=(shape((HQ, slots, HD), f32), shap...  4.09 us
    pallas_call x1, Pallas kernels, per_device(): pl.pallas_call(pack_kernel, out_shape=shape((n, 2 * TILE, kv_width)), in_...  2.41 us
    pallas_call x1, Pallas kernels, per_device(): pl.pallas_call(ffn_kernel, out_shape=(shape((n * slots, units)), shape((n...  2.4 us
    pallas_call x1, Pallas kernels, per_device(): pl.pallas_call(own_half_kernel, out_shape=shape((n * slots, width // 2),...  1.53 us
  transfers between devices with their start and end apart: 3, of which 2 were waited for; matrix products, arithmetic and copies ran while one was open for 0% of the time, Pallas kernels for 10%

profile of v7, /device:TPU:0, one launch (start us, length us, event | category | flops | bytes accessed | tf_op | source)
XLA Modules:
  0.0 69.9 jit_solution(11403727496716439476)
XLA Ops:
  0.6 0.0 copy-start.7
  0.6 0.0 copy-start.10
  0.7 0.0 copy-start.9
  0.7 0.0 copy-start.8
  0.7 0.0 copy-start.6
  0.7 0.0 copy-start.5
  0.7 0.0 copy-start.3
  0.7 0.0 copy-start.11
  0.7 0.0 copy-start.4
  0.7 0.0 copy-start.12
  0.7 2.4 %pack.1 = bf16[16,32,512]{2,1,0:T(8,128)(2,1)} custom-call(s32[16]{0:T(128)} %send_slot.5, s32[16]{0:T(128)} %send_to.5, s32[16]{0:T(128)} %receive_from.7, s32[16]{0:T(128)} %land_slot.5, bf16[32,4,128]{2,1,0:T(4,128)(2,1)} %bitcast.17, bf16[4,4,128]{2,1,0:T(4,128)(2,1)} %bitcast.21, bf16[4,4,128]{2,1,0:T(4,128)(2,1)} %bitcast.24, ...), custom_call_target="tpu_custom_call" | custom-call | bytes 1048576 | tf_op jit(solution)/shard_map/pack/pallas_call | solution.py:371
  3.2 7.4 %all-to-all-start = ((bf16[16,32,512]{2,1,0:T(8,128)(2,1)}), bf16[16,32,512]{2,1,0:T(8,128)(2,1)S(1)}, u32[]{:S(2)}, u32[]{:S(2)}) async-start(bf16[16,32,512]{2,1,0:T(8,128)(2,1)} %pack.1), calls=%async_computation | async-start | bytes 1048576 | tf_op jit(solution)/shard_map/all_to_all | solution.py:21
  10.5 0.0 copy-done.7
  10.6 0.0 copy-done.10
  10.6 0.0 copy-done.9
  10.6 0.0 copy-done.8
  10.6 0.0 copy-done.6
  10.6 0.0 copy-done.5
  10.6 0.0 copy-done.3
  10.6 0.0 copy-done.11
  10.6 0.0 copy-done.4
  10.6 0.0 copy-done.12
  10.6 0.0 copy-start.1
  10.7 1.2 %copy-done.1 = bf16[4,256,512]{2,1,0:T(8,128)(2,1)S(1)} copy-done((bf16[4,256,512]{2,1,0:T(8,128)(2,1)S(1)}, bf16[4,256,512]{2,1,0:T(8,128)(2,1)}, u32[]{:S(2)}) %copy-start.1) | copy-done | bytes 1048600
  11.9 0.0 copy-start
  11.9 4.1 %local.1 = (f32[32,4,128]{2,1,0:T(4,128)S(1)}, bf16[4,256,512]{2,1,0:T(8,128)(2,1)}, bf16[4,256,512]{2,1,0:T(8,128)(2,1)}, bf16[2,256,512]{2,1,0:T(8,128)(2,1)S(1)}, bf16[64,64]{1,0:T(8,128)(2,1)S(1)}) custom-call(s32[16]{0:T(128)S(1)} %copy-done.8, s32[16]{0:T(128)S(1)} %copy-done.9, s32[16]{0:T(128)S(1)} %copy-done.7, s32[16]{0:T(128)S(1)} %copy-done.10, ...), custom_call_target="tpu_custom_call" | custom-call | flops 16777216 | bytes 16777216 | tf_op jit(solution)/shard_map/local/pallas_call | solution.py:386
  16.0 9.0 %all-to-all-done.spread = bf16[16,32,512]{2,1,0:T(8,128)(2,1)S(1)} async-done(((bf16[16,32,512]{2,1,0:T(8,128)(2,1)}), bf16[16,32,512]{2,1,0:T(8,128)(2,1)S(1)}, u32[]{:S(2)}, u32[]{:S(2)}) %all-to-all-start) | async-done | bytes 524320 | tf_op jit(solution)/shard_map/all_to_all | solution.py:21
  25.0 0.6 moved.1
  25.7 13.2 %all_to_all.15 = bf16[8,4,4096]{2,1,0:T(4,128)(2,1)S(1)} all-to-all(bf16[8,4,4096]{2,1,0:T(4,128)(2,1)S(1)} %moved.1), channel_id=1, replica_groups=mesh['parts'=2,'chip'=8,'core'=2] {'chip'}, dimensions={0} | all-to-all | bytes 524288 | tf_op jit(solution)/shard_map/all_to_all | solution.py:21
  38.8 0.1 reshape.45._.near
  38.9 0.0 copy-start.2
  38.9 0.1 collective-permute-start
  39.0 0.0 copy-done
  39.0 1.1 %select.1 = (bf16[16,48,512]{2,1,0:T(8,128)(2,1)S(1)}, bf16[2048,256]{1,0:T(8,128)(2,1)S(1)}) custom-call(s32[16]{0:T(128)S(1)} %copy-done.7, bf16[16,32,512]{2,1,0:T(8,128)(2,1)S(1)} %all-to-all-done.spread, bf16[4096,256]{1,0:T(8,128)(2,1)S(1)} %copy-done, bf16[32,4096]{1,0:T(8,128)(2,1)S(1)} %reshape.45._.near), custom_call_target="tpu_custom_call" | custom-call | bytes 1048576 | tf_op jit(solution)/shard_map/select/pallas_call | solution.py:426
  40.1 0.4 collective-permute-done.far
  40.5 0.0 copy-done.2
  40.5 2.4 %ffn.1 = (bf16[64,256]{1,0:T(8,128)(2,1)S(1)}, bf16[64,2048]{1,0:T(8,128)(2,1)S(1)}) custom-call(bf16[32,4096]{1,0:T(8,128)(2,1)S(1)} %reshape.45._.near, bf16[32,4096]{1,0:T(8,128)(2,1)S(1)} %collective-permute-done.far, bf16[64,64]{1,0:T(8,128)(2,1)S(1)} %get-tuple-element.21.pick, bf16[4096,256]{1,0:T(8,128)(2,1)S(1)} %copy-done.2, ...), custom_call_target="tpu_custom_call" | custom-call | flops 335544320 | bytes 6291456 | tf_op jit(solution)/shard_map/ffn/pallas_call | solution.py:437
  42.9 0.2 collective-permute-start.1
  43.1 1.5 %own_half.1.mine = f32[64,2048]{1,0:T(8,128)S(1)} custom-call(bf16[64,256]{1,0:T(8,128)(2,1)S(1)} %get-tuple-element.23.hidden, bf16[256,4096]{1,0:T(8,128)(2,1)} %down_weight.3), custom_call_target="tpu_custom_call" | custom-call | flops 67108864 | bytes 1048576 | tf_op jit(solution)/shard_map/own_half/pallas_call | solution.py:447
  44.7 0.0 copy-start.13
  44.7 0.0 collective-permute-done.1.theirs
  44.7 0.1 place.1
  44.8 23.8 %all_to_all.16.arrived = bf16[16,48,512]{2,1,0:T(8,128)(2,1)S(1)} all-to-all(bf16[16,48,512]{2,1,0:T(8,128)(2,1)S(1)} %place.1), channel_id=1, replica_groups=mesh['parts'=2,'chip'=8,'core'=2] {'chip','core'}, dimensions={0} | all-to-all | bytes 1572864 | tf_op jit(solution)/shard_map/all_to_all | solution.py:21
  68.6 0.0 copy-done.13
  68.6 1.3 %finish.1 = (bf16[4,4096]{1,0:T(4,128)(2,1)}, bf16[4,16,16,512]{3,2,1,0:T(8,128)(2,1)}, bf16[4,16,16,512]{3,2,1,0:T(8,128)(2,1)}) custom-call(s32[16]{0:T(128)S(1)} %copy-done.7, s32[16]{0:T(128)S(1)} %copy-done.10, s32[16]{0:T(128)S(1)} %copy-done.13, bf16[4,4,128]{2,1,0:T(4,128)(2,1)S(1)} %bitcast.23, ...), custom_call_target="tpu_custom_call", output_to_operand_aliasing={{1}: (6, {}), {2}: (7, {})} | custom-call | bytes 1048576 | tf_op jit(solution)/shard_map/finish/pallas_call | solution.py:470
Async XLA Ops:
  0.6 9.9 %copy-start.7 = (s32[16]{0:T(128)S(1)}, s32[16]{0:T(128)}, u32[]{:S(2)}) copy-start(s32[16]{0:T(128)} %receive_from.7) | copy-start | bytes 196
  0.6 9.9 %copy-start.10 = (s32[16]{0:T(128)S(1)}, s32[16]{0:T(128)}, u32[]{:S(2)}) copy-start(s32[16]{0:T(128)} %land_slot.5) | copy-start | bytes 196
  0.7 9.9 %copy-start.9 = (s32[16]{0:T(128)S(1)}, s32[16]{0:T(128)}, u32[]{:S(2)}) copy-start(s32[16]{0:T(128)} %send_to.5) | copy-start | bytes 196
  0.7 9.9 %copy-start.8 = (s32[16]{0:T(128)S(1)}, s32[16]{0:T(128)}, u32[]{:S(2)}) copy-start(s32[16]{0:T(128)} %send_slot.5) | copy-start | bytes 196
  0.7 9.9 %copy-start.6 = (bf16[4,512]{1,0:T(4,128)(2,1)S(1)}, bf16[4,512]{1,0:T(4,128)(2,1)}, u32[]{:S(2)}) copy-start(bf16[4,512]{1,0:T(4,128)(2,1)} %param.27) | copy-start | bytes 12292
  0.7 9.9 %copy-start.5 = (bf16[4,512]{1,0:T(4,128)(2,1)S(1)}, bf16[4,512]{1,0:T(4,128)(2,1)}, u32[]{:S(2)}) copy-start(bf16[4,512]{1,0:T(4,128)(2,1)} %param.26) | copy-start | bytes 12292
  0.7 9.9 %copy-start.3 = (bf16[4,4096]{1,0:T(4,128)(2,1)S(1)}, bf16[4,4096]{1,0:T(4,128)(2,1)}, u32[]{:S(2)}) copy-start(bf16[4,4096]{1,0:T(4,128)(2,1)} %param.25) | copy-start | bytes 98308
  0.7 9.9 %copy-start.11 = (s32[4]{0:T(128)S(1)}, s32[4]{0:T(128)}, u32[]{:S(2)}) copy-start(s32[4]{0:T(128)} %lengths.3) | copy-start | bytes 52
  0.7 9.9 %copy-start.4 = (f32[4096]{0:T(1024)S(1)}, f32[4096]{0:T(1024)}, u32[]{:S(2)}) copy-start(f32[4096]{0:T(1024)} %param.28) | copy-start | bytes 49156
  0.7 9.9 %copy-start.12 = (s32[4]{0:T(128)S(1)}, s32[4]{0:T(128)}, u32[]{:S(2)}) copy-start(s32[4]{0:T(128)} %unfinished.1) | copy-start | bytes 52
  3.2 21.9 %all-to-all-start = ((bf16[16,32,512]{2,1,0:T(8,128)(2,1)}), bf16[16,32,512]{2,1,0:T(8,128)(2,1)S(1)}, u32[]{:S(2)}, u32[]{:S(2)}) async-start(bf16[16,32,512]{2,1,0:T(8,128)(2,1)} %pack.1), calls=%async_computation | async-start | bytes 1048576 | tf_op jit(solution)/shard_map/all_to_all | solution.py:21
  10.6 1.2 %copy-start.1 = (bf16[4,256,512]{2,1,0:T(8,128)(2,1)S(1)}, bf16[4,256,512]{2,1,0:T(8,128)(2,1)}, u32[]{:S(2)}) copy-start(bf16[4,256,512]{2,1,0:T(8,128)(2,1)} %ck.1) | copy-start | bytes 3145732
  11.9 27.1 %copy-start = (bf16[4096,256]{1,0:T(8,128)(2,1)S(1)}, bf16[4096,256]{1,0:T(8,128)(2,1)}, u32[]{:S(2)}) copy-start(bf16[4096,256]{1,0:T(8,128)(2,1)} %up_weight.3) | copy-start | bytes 6291460
  38.9 1.6 %copy-start.2 = (bf16[4096,256]{1,0:T(8,128)(2,1)S(1)}, bf16[4096,256]{1,0:T(8,128)(2,1)}, u32[]{:S(2)}) copy-start(bf16[4096,256]{1,0:T(8,128)(2,1)} %gate_weight.1) | copy-start | bytes 6291460
  38.9 1.6 %collective-permute-start = (bf16[32,4096]{1,0:T(8,128)(2,1)S(1)}, bf16[32,4096]{1,0:T(8,128)(2,1)S(1)}, u32[]{:S(2)}, u32[]{:S(2)}) collective-permute-start(bf16[32,4096]{1,0:T(8,128)(2,1)S(1)} %reshape.45._.near), channel_id=1, source_target_pairs={{0,1},{1,0},{2,3},{3,2},{4,5},{5,4},{6,7},{7,6},{8,9},{9,8},{10,11... | collective-permute-start | bytes 786440 | tf_op jit(solution)/shard_map/ppermute | solution.py:424
  42.9 1.8 %collective-permute-start.1 = (bf16[64,2048]{1,0:T(8,128)(2,1)S(1)}, bf16[64,2048]{1,0:T(8,128)(2,1)S(1)}, u32[]{:S(2)}, u32[]{:S(2)}) collective-permute-start(bf16[64,2048]{1,0:T(8,128)(2,1)S(1)} %get-tuple-element.24), channel_id=1, source_target_pairs={{0,1},{1,0},{2,3},{3,2},{4,5},{5,4},{6,7},{7,6},{8,9},{9,8},{10,11... | collective-permute-start | bytes 786440 | tf_op jit(solution)/shard_map/ppermute | solution.py:457
  44.7 24.0 %copy-start.13 = (s32[16]{0:T(128)S(1)}, s32[16]{0:T(128)}, u32[]{:S(2)}) copy-start(s32[16]{0:T(128)} %land_length.1) | copy-start | bytes 196
